TPU v7x, 32 devices: a whole 2x2x4 slice. The times are simulated.
32 devices in a mesh: expert: 8 (over z, y), ctx: 4 (over x, core).
Axes of the slice: x: 2, y: 2, z: 4, core: 2. Of those that a mesh axis runs over, the one named last changes fastest.
Arguments:
- tokens: bfloat16 [1024, 4096], P('expert', 'ctx'), may hold values from -6 to 6
- grad_out: bfloat16 [1024, 4096], P('expert', 'ctx'), may hold values from -1.5 to 1.5
- expert_ids: int32 [1024, 8], P('expert'), may hold values from 0 to 15, all different within a row; in each aligned block of 128 rows (0 to 127, 128 to 255, ...) at most 72 rows name the same one
- gate_probs: float32 [1024, 8], P('expert'), may hold values from 0.05 to 1
- gate_weight: bfloat16 [16, 1536, 4096], P('expert', 'ctx'), may hold values from -0.09375 to 0.09375
- up_weight: bfloat16 [16, 1536, 4096], P('expert', 'ctx'), may hold values from -0.09375 to 0.09375
- down_weight: bfloat16 [16, 1536, 4096], P('expert', 'ctx'), may hold values from -0.15625 to 0.15625
Outputs:
- grad_tokens: bfloat16 [1024, 4096], P('expert', 'ctx')
- grad_gates: bfloat16 [1024, 8], P('expert')
Inputs may be any that keep to these rules, and one draw needn't show every extreme that they name: `expert_ids`: each row names 8 different experts. Within the 128 rows of one index of expert (aligned blocks), no expert is named more than 72 times, and in every draw some expert is named exactly 72 times in some block.
All inputs are finite; a program needn't handle non-finite values.
Results may differ from a plain program's by a relative error of at most 0.014.
Values may be sent and summed in bfloat16 or wider, within the bound.
No kernel may reach another device: no remote copies, remote signals or barrier semaphores. Data moves between devices by JAX's collectives and lax.ppermute only.
A program may use at most 128 MiB of HBM per device.

v0:
```python
import jax
import jax.numpy as jnp
from jax import lax
from jax.sharding import PartitionSpec as P


def route_tables(expert_ids, experts, capacity):
    tok_count, top_count = expert_ids.shape
    flat_ids = expert_ids.reshape(-1)
    one_hot = (flat_ids[:, None] == jnp.arange(experts, dtype=jnp.int32)[None, :]).astype(jnp.int32)
    earlier = jnp.cumsum(one_hot, axis=0) - one_hot
    slot_rank = jnp.sum(earlier * one_hot, axis=1)
    slot_index = (flat_ids * capacity + slot_rank).reshape(tok_count, top_count)
    matches = (
        slot_index[:, :, None] == jnp.arange(experts * capacity, dtype=jnp.int32)[None, None, :]
    )
    placing = jnp.any(matches, axis=1).astype(jnp.bfloat16)
    return (slot_index, placing)


def body(tokens, grad_out, expert_ids, gate_probs, gate_weight, up_weight, down_weight):
    tok_count, top_count = expert_ids.shape
    groups = lax.axis_size("expert")
    local_count = gate_weight.shape[0]
    experts = local_count * groups
    capacity = tok_count * top_count // experts + max(1, tok_count * top_count // (8 * experts))
    full_width = gate_weight.shape[2]
    slot_index, placing = route_tables(expert_ids, experts, capacity)
    sent_rows = jnp.einsum("tc,td->cd", placing, tokens, preferred_element_type=jnp.float32).astype(
        jnp.bfloat16
    )
    sent_grads = jnp.einsum(
        "tc,td->cd", placing, grad_out, preferred_element_type=jnp.float32
    ).astype(jnp.bfloat16)
    sent_rows = sent_rows.reshape(groups, local_count * capacity, -1)
    sent_grads = sent_grads.reshape(groups, local_count * capacity, -1)
    got_rows, got_grads = (
        lax.all_to_all(sent_rows, "expert", split_axis=0, concat_axis=0, tiled=True),
        lax.all_to_all(sent_grads, "expert", split_axis=0, concat_axis=0, tiled=True),
    )
    rows_in, rows_grad = (
        lax.all_gather(got_rows, "ctx", axis=2, tiled=True),
        lax.all_gather(got_grads, "ctx", axis=2, tiled=True),
    )
    rows_in = rows_in.reshape(groups, local_count, capacity, full_width)
    rows_grad = rows_grad.reshape(groups, local_count, capacity, full_width)
    pre_gate = jnp.einsum(
        "secd,efd->secf", rows_in, gate_weight, preferred_element_type=jnp.float32
    )
    pre_up = jnp.einsum("secd,efd->secf", rows_in, up_weight, preferred_element_type=jnp.float32)
    grad_hidden = jnp.einsum(
        "secd,efd->secf", rows_grad, down_weight, preferred_element_type=jnp.float32
    )
    sigmoid_gate = jax.nn.sigmoid(pre_gate)
    activated = pre_gate * sigmoid_gate
    gate_score = jnp.sum(activated * pre_up * grad_hidden, axis=3)
    grad_pre_gate = (
        grad_hidden * pre_up * sigmoid_gate * (1.0 + pre_gate * (1.0 - sigmoid_gate))
    ).astype(jnp.bfloat16)
    grad_pre_up = (grad_hidden * activated).astype(jnp.bfloat16)
    partials = jnp.einsum(
        "secf,efd->secd", grad_pre_gate, gate_weight, preferred_element_type=jnp.float32
    )
    partials = partials + jnp.einsum(
        "secf,efd->secd", grad_pre_up, up_weight, preferred_element_type=jnp.float32
    )
    block_terms = partials.astype(jnp.bfloat16)
    summed = lax.psum_scatter(block_terms, "ctx", scatter_dimension=3, tiled=True).astype(
        jnp.float32
    )
    gate_total = lax.psum(gate_score, "ctx")
    back_rows = summed.astype(jnp.bfloat16).reshape(groups, local_count * capacity, -1)
    back_scores = gate_total.astype(jnp.bfloat16).reshape(groups, local_count * capacity)
    home_rows, home_scores = (
        lax.all_to_all(back_rows, "expert", split_axis=0, concat_axis=0, tiled=True),
        lax.all_to_all(back_scores, "expert", split_axis=0, concat_axis=0, tiled=True),
    )
    contribution = home_rows.reshape(experts * capacity, -1)
    picked = jnp.take(contribution, slot_index.reshape(-1), axis=0).reshape(
        tok_count, top_count, -1
    )
    grad_tokens = jnp.sum(gate_probs[:, :, None] * picked.astype(jnp.float32), axis=1)
    grad_gates = jnp.take(home_scores.reshape(-1), slot_index.reshape(-1)).reshape(
        tok_count, top_count
    )
    return (grad_tokens.astype(jnp.bfloat16), grad_gates)


def solution(mesh):
    in_specs = (
        P("expert", "ctx"),
        P("expert", "ctx"),
        P("expert", None),
        P("expert", None),
        P("expert", "ctx", None),
        P("expert", "ctx", None),
        P("expert", "ctx", None),
    )
    out_specs = (P("expert", "ctx"), P("expert", None))
    return jax.shard_map(body, mesh=mesh, in_specs=in_specs, out_specs=out_specs, check_vma=False)
```

profile of v0, /device:TPU:8, one launch (start us, length us, event | category | flops | bytes accessed | tf_op | source)
XLA Modules:
  0.0 402.7 jit_solution(1945704785532264489)
XLA Ops:
  7.2 0.8 copy.50
  8.0 0.1 eq.39
  8.2 4.5 %reduce-window.6 = s32[16,8,128]{2,1,0:T(8,128)S(1)} reduce-window(s32[16,8,128]{2,1,0:T(8,128)S(1)} %fusion.30, s32[]{:T(128)} %constant.23.clone.1), window={size=1x1x128 pad=0_0x0_0x127_0}, to_apply=%region_0.0 | reduce-window | flops 2080768 | bytes 131076 | tf_op jit(solution)/shard_map/reduce-window
  12.8 0.1 copy.53
  13.3 1.5 fusion.13
  14.8 0.8 convolution_convert_fusion
  15.6 59.1 %all_to_all.25 = bf16[8,144,1024]{2,1,0:T(8,128)(2,1)} all-to-all(bf16[8,144,1024]{2,1,0:T(8,128)(2,1)S(1)} %bitcast.106), channel_id=1, replica_groups=mesh['expert'=8,'ctx'=4] {'expert'}, dimensions={0} | all-to-all | bytes 4718592 | tf_op jit(solution)/shard_map/all_to_all | solution.py:38
  74.9 0.9 copy-done.3
  75.7 0.8 convolution_convert_fusion.1
  76.5 57.0 %all_to_all.26 = bf16[8,144,1024]{2,1,0:T(8,128)(2,1)} all-to-all(bf16[8,144,1024]{2,1,0:T(8,128)(2,1)S(1)} %bitcast.105), channel_id=1, replica_groups=mesh['expert'=8,'ctx'=4] {'expert'}, dimensions={0} | all-to-all | bytes 4718592 | tf_op jit(solution)/shard_map/all_to_all | solution.py:39
  133.6 0.2 reduce-scatter.2.cloned.1.call-start
  133.8 4.8 %all-gather.5.cloned.1.call-done = bf16[8,144,4096]{2,1,0:T(8,128)(2,1)} async-done(((bf16[8,144,1024]{2,1,0:T(8,128)(2,1)}), bf16[8,144,4096]{2,1,0:T(8,128)(2,1)}) %all-gather.5.cloned.1.call-update) | async-done | bytes 9437200 | tf_op jit(solution)/shard_map/all_gather | solution.py:42
  138.6 9.5 %fusion.3 = f32[2,8,72,384]{3,2,1,0:T(8,128)S(1)} fusion(bf16[8,2,72,4096]{3,2,1,0:T(8,128)(2,1)} %bitcast.113, bf16[2,384,4096]{2,1,0:T(8,128)(2,1)} %param.11), kind=kOutput, calls=%fused_computation.6 | convolution fusion | flops 3623878656 | bytes 17498112 | tf_op jit(solution)/shard_map/secd,efd->secf/dot_general | solution.py:47
  148.1 56.4 %all-gather.3.cloned.1.call-done = bf16[8,144,4096]{2,1,0:T(8,128)(2,1)} async-done(((bf16[8,144,1024]{2,1,0:T(8,128)(2,1)}), bf16[8,144,4096]{2,1,0:T(8,128)(2,1)}) %all-gather.3.cloned.1.call-update) | async-done | bytes 9437200 | tf_op jit(solution)/shard_map/all_gather | solution.py:43
  204.4 9.6 %fusion.1 = f32[2,8,72,384]{3,2,1,0:T(8,128)S(1)} fusion(bf16[8,2,72,4096]{3,2,1,0:T(8,128)(2,1)} %bitcast.115, bf16[2,384,4096]{2,1,0:T(8,128)(2,1)} %param.13), kind=kOutput, calls=%fused_computation.4 | convolution fusion | flops 3623878656 | bytes 17498112 | tf_op jit(solution)/shard_map/secd,efd->secf/dot_general | solution.py:51
  214.0 10.5 %fusion.22 = (f32[8,2,72]{2,0,1:T(8,128)S(1)}, f32[2,8,72,384]{3,2,1,0:T(8,128)S(1)}) fusion(f32[2,8,72,384]{3,2,1,0:T(8,128)S(1)} %fusion.1, f32[2,8,72,384]{3,2,1,0:T(8,128)S(1)} %fusion.3, bf16[2,384,4096]{2,1,0:T(8,128)(2,1)} %param.12, bf16[8,2,72,4096]{3,2,1,0:T(8,128)(2,1)} %bitcast.114), kind=kOutput, calls=%fused_computation.35 | convolution fusion | flops 3626974208 | bytes 21041664 | tf_op jit(solution)/shard_map/secd,efd->secf/dot_general | solution.py:50
  224.6 9.3 %fusion.7 = f32[2,8,72,4096]{3,2,1,0:T(8,128)} fusion(bf16[2,384,4096]{2,1,0:T(8,128)(2,1)S(1)} %bitcast.108, f32[2,8,72,384]{3,2,1,0:T(8,128)S(1)} %fusion.3, f32[2,8,72,384]{3,2,1,0:T(8,128)S(1)} %get-tuple-element.15, f32[2,8,72,384]{3,2,1,0:T(8,128)S(1)} %fusion.1), kind=kOutput, calls=%fused_computation.10 | convolution fusion | flops 3628302336 | bytes 30474240 | tf_op jit(solution)/shard_map/secf,efd->secd/dot_general | solution.py:61
  233.9 13.6 %fusion = bf16[8,2,72,4096]{3,2,0,1:T(8,128)(2,1)} fusion(f32[2,8,72,4096]{3,2,1,0:T(8,128)} %fusion.7, bf16[2,384,4096]{2,1,0:T(8,128)(2,1)} %param.12, f32[2,8,72,384]{3,2,1,0:T(8,128)} %copy-done.2, f32[2,8,72,384]{3,2,1,0:T(8,128)S(1)} %fusion.3), kind=kOutput, calls=%fused_computation.3 | convolution fusion | flops 3635970048 | bytes 38141952 | tf_op jit(solution)/shard_map/secf,efd->secd/dot_general | solution.py:64
  247.5 6.4 %psum.7 = bf16[8,2,72]{2,0,1:T(8,128)(2,1)S(1)} all-reduce(f32[8,2,72]{2,0,1:T(8,128)S(1)} %get-tuple-element.14), channel_id=1, replica_groups=mesh['expert'=8,'ctx'=4] {'ctx'}, use_global_device_ids=true, to_apply=%region_7.8 | all-reduce | flops 1152 | bytes 6912 | tf_op jit(solution)/shard_map/psum | solution.py:71
  253.9 0.7 all_to_all.20
  254.6 6.1 %all-to-all-start.3 = ((bf16[8,1,144]{2,1,0:T(2,128)(2,1)}), bf16[8,1,144]{2,1,0:T(2,128)(2,1)S(1)}, u32[]{:S(2)}, u32[]{:S(2)}) async-start(bf16[8,1,144]{2,1,0:T(2,128)(2,1)} %all_to_all.20), calls=%async_computation.4 | async-start | bytes 16384 | tf_op jit(solution)/shard_map/all_to_all | solution.py:76
  260.7 65.4 %reduce-scatter.2.cloned.1.call-done = bf16[8,2,72,1024]{3,2,0,1:T(8,128)(2,1)} async-done(((bf16[8,2,72,4096]{3,2,0,1:T(8,128)(2,1)}), bf16[8,2,72,1024]{3,2,0,1:T(8,128)(2,1)}) %reduce-scatter.2.cloned.1.call-update) | async-done | bytes 2359312 | tf_op jit(solution)/shard_map/reduce_scatter | solution.py:68
  326.1 3.3 copy.58
  329.4 6.2 %all-to-all-start.2 = ((bf16[8,144,1024]{2,1,0:T(8,128)(2,1)}), bf16[8,144,1024]{2,1,0:T(8,128)(2,1)S(1)}, u32[]{:S(2)}, u32[]{:S(2)}) async-start(bf16[8,144,1024]{2,1,0:T(8,128)(2,1)} %bitcast.104), calls=%async_computation.3 | async-start | bytes 4718592 | tf_op jit(solution)/shard_map/all_to_all | solution.py:75
  335.6 0.1 mul.67
  335.7 0.1 copy.49
  335.9 0.1 reshape.110
  336.0 6.8 %gather_fusion.1 = bf16[1024]{0:T(1024)(128)(2,1)S(1)} fusion(bf16[1152]{0:T(1024)(128)(2,1)S(1)} %reshape.110, s32[1024]{0:T(1024)S(1)} %broadcast_clamp_fusion), kind=kCustom, calls=%fused_computation.1 | custom fusion | bytes 8192 | tf_op jit(solution)/shard_map/jit(_take)/gather | solution.py:83
  342.9 0.7 copy.61
  343.6 43.4 %all-to-all-done.2 = bf16[8,144,1024]{2,1,0:T(8,128)(2,1)S(1)} async-done(((bf16[8,144,1024]{2,1,0:T(8,128)(2,1)}), bf16[8,144,1024]{2,1,0:T(8,128)(2,1)S(1)}, u32[]{:S(2)}, u32[]{:S(2)}) %all-to-all-start.2) | async-done | bytes 2359328 | tf_op jit(solution)/shard_map/all_to_all | solution.py:75
  387.0 5.4 %gather_fusion = bf16[1024,1024]{1,0:T(8,128)(2,1)} fusion(bf16[1152,1024]{1,0:T(8,128)(2,1)S(1)} %bitcast.103, s32[1024]{0:T(1024)S(1)} %broadcast_clamp_fusion), kind=kCustom, calls=%fused_computation | custom fusion | bytes 4198400 | tf_op jit(solution)/shard_map/jit(_take)/gather | solution.py:79
  392.4 3.8 multiply_reduce_fusion
  (36 shorter events, 0.8 us)
Async XLA Ops:
  7.2 7.7 %copy-start = (bf16[128,1024]{1,0:T(8,128)(2,1)S(1)}, bf16[128,1024]{1,0:T(8,128)(2,1)}, u32[]{:S(2)}) copy-start(bf16[128,1024]{1,0:T(8,128)(2,1)} %param.7) | copy-start | bytes 786436
  7.2 131.4 %all-gather.5.cloned.1.call-start = ((), (), s32[]{:S(2)}) async-start(), calls=%async_computation.6 | async-start | bytes 11796480 | tf_op jit(solution)/shard_map/all_gather | solution.py:42
  74.8 1.0 copy-start.3
  74.8 129.6 %all-gather.3.cloned.1.call-start = ((), (), s32[]{:S(2)}) async-start(), calls=%async_computation.5 | async-start | bytes 11796480 | tf_op jit(solution)/shard_map/all_gather | solution.py:43
  133.6 192.5 %reduce-scatter.2.cloned.1.call-start = ((), (), s32[]{:S(2)}) async-start(), calls=%async_computation.7 | async-start | bytes 11796480 | tf_op jit(solution)/shard_map/reduce_scatter | solution.py:68
  204.4 20.2 %slice-start = ((s8[6291456]{0:T(1024)(128)(4,1)}), s8[4194304]{0:T(1024)(128)(4,1)S(1)}, s32[]{:S(2)}) async-start(s8[6291456]{0:T(1024)(128)(4,1)} %bitcast.107), calls=%async_computation.8 | async-start | bytes 8388608
  214.0 10.5 %copy-start.2 = (f32[2,8,72,384]{3,2,1,0:T(8,128)}, f32[2,8,72,384]{3,2,1,0:T(8,128)S(1)}, u32[]{:S(2)}) copy-start(f32[2,8,72,384]{3,2,1,0:T(8,128)S(1)} %fusion.1) | copy-start | bytes 5308420
  214.0 10.5 %slice-start.1 = ((s8[6291456]{0:T(1024)(128)(4,1)}), s8[2097152]{0:T(1024)(128)(4,1)S(1)}, s32[]{:S(2)}) async-start(s8[6291456]{0:T(1024)(128)(4,1)} %bitcast.107), calls=%async_computation.9 | async-start | bytes 4194304
  254.6 74.8 %all-to-all-start.3 = ((bf16[8,1,144]{2,1,0:T(2,128)(2,1)}), bf16[8,1,144]{2,1,0:T(2,128)(2,1)S(1)}, u32[]{:S(2)}, u32[]{:S(2)}) async-start(bf16[8,1,144]{2,1,0:T(2,128)(2,1)} %all_to_all.20), calls=%async_computation.4 | async-start | bytes 16384 | tf_op jit(solution)/shard_map/all_to_all | solution.py:76
  329.4 6.3 %copy-start.4 = (f32[128,8]{0,1:T(8,128)S(1)}, f32[128,8]{0,1:T(8,128)}, u32[]{:S(2)}) copy-start(f32[128,8]{0,1:T(8,128)} %param.10) | copy-start | bytes 12292
  329.4 57.6 %all-to-all-start.2 = ((bf16[8,144,1024]{2,1,0:T(8,128)(2,1)}), bf16[8,144,1024]{2,1,0:T(8,128)(2,1)S(1)}, u32[]{:S(2)}, u32[]{:S(2)}) async-start(bf16[8,144,1024]{2,1,0:T(8,128)(2,1)} %bitcast.104), calls=%async_computation.3 | async-start | bytes 4718592 | tf_op jit(solution)/shard_map/all_to_all | solution.py:75
  387.0 9.2 %copy-start.1 = (bf16[128,1024]{1,0:T(8,128)(2,1)S(1)}, bf16[128,1024]{1,0:T(8,128)(2,1)}, u32[]{:S(2)}) copy-start(bf16[128,1024]{1,0:T(8,128)(2,1)} %param.7) | copy-start | bytes 786436
Sparse Core Ops, SparseCore 0:
  74.9 63.6 all-gather.4
  140.1 64.2 all-gather.2
  247.6 78.4 reduce-scatter.1
where the time goes:
time: 407 us; the launch traced here: 403 us
  waiting for transfers between devices  170 us (42%)
  blocking collectives  123 us (30%)
  matrix products  54.1 us (13%)
  local copies, waits for them, and re-layouts  19.5 us (5%)
  between operations  14 us (3%)
  starting transfers between devices  12.5 us (3%)
  other arithmetic  10.1 us (2%)
    reduce_scatter x1, waiting for transfers between devices, body(): lax.psum_scatter(block_terms, 'ctx', scatter_dimension=3, tiled=True)  65.4 us
    all_to_all x1, blocking collectives, body(): lax.all_to_all(sent_rows, 'expert', split_axis=0, concat_axis=0, tiled=True)  59.1 us
    all_to_all x1, blocking collectives, body(): lax.all_to_all(sent_grads, 'expert', split_axis=0, concat_axis=0, tiled=T...  57 us
    all_gather x1, waiting for transfers between devices, body(): lax.all_gather(got_grads, 'ctx', axis=2, tiled=True)  56.4 us
    all_to_all x1, waiting for transfers between devices, body(): lax.all_to_all(back_rows, 'expert', split_axis=0, concat_axis=0, tiled=True)  43.4 us
    dot_general x1, matrix products, body(): jnp.einsum('secf,efd->secd', grad_pre_up, up_weight, preferred_element_ty...  13.6 us
    dot_general x1, matrix products, body(): jnp.einsum('secd,efd->secf', rows_in, up_weight, preferred_element_type=j...  10.5 us
    dot_general x1, matrix products, body(): jnp.einsum('secd,efd->secf', rows_grad, down_weight, preferred_element_ty...  9.6 us
  transfers between devices with their start and end apart: 5, of which 4 were waited for; matrix products, arithmetic and copies ran while one was open for 5% of the time, Pallas kernels for 0%

commit v1 on v0

v1 whole, which is shorter than its diff:
```python
import functools
import jax
import jax.numpy as jnp
from jax import lax
from jax.experimental import pallas as pl
from jax.experimental.pallas import tpu as pltpu
from jax.sharding import Mesh, PartitionSpec as P

NT = (((1,), (1,)), ((), ()))
NN = (((1,), (0,)), ((), ()))


def expert_kernel(plan, *refs):
    piece_at, out_at, n_in, n_q, ndy, ndx, local, tile, wide = plan
    where = refs[0]
    pieces = refs[1 : 1 + n_in]
    probs, wg_hbm, wu_hbm, wd_hbm = refs[1 + n_in : 5 + n_in]
    outs = refs[5 + n_in : 5 + n_in + 2 * n_q]
    score, wg, wu, wd, d_gate, d_up, w_sem = refs[5 + n_in + 2 * n_q :]
    rows, width = pieces[0].shape[1:]
    units = wg.shape[0]
    hidden = units // local
    tiles = units // tile
    slabs = [(q, dy) for q in range(n_q) for dy in range(ndy)]
    blocks = [(dx, dc) for dx in range(ndx) for dc in range(2)]

    def feature(dx, dc):
        return pl.multiple_of(where[1 + 2 * dx + dc] * width, width)

    def weight_copy(k, n):
        part = pl.ds(pl.multiple_of(n * tile, tile), tile)
        source, target = ((wg_hbm, wg), (wu_hbm, wu), (wd_hbm, wd))[k]
        return pltpu.make_async_copy(source.at[part], target.at[part], w_sem.at[k, n])

    for k in range(3):
        weight_copy(k, 0).start()

    def product(kind, ref, first):
        total = None
        for dx, dc in blocks:
            x = jnp.concatenate([pieces[piece_at[q][dy, dx, dc]][kind] for q, dy in slabs], axis=0)
            w = ref[pl.ds(first, tile), pl.ds(feature(dx, dc), width)]
            term = lax.dot_general(x, w, NT, preferred_element_type=jnp.float32)
            total = term if total is None else total + term
        return total

    column = lax.broadcasted_iota(jnp.int32, (rows, probs.shape[3]), 1)
    shares = []
    for e in range(local):
        mine = column == where[0] * local + e
        shares.append(
            jnp.concatenate(
                [
                    jnp.sum(jnp.where(mine, probs[q, dy], 0.0), axis=1, keepdims=True)
                    for q, dy in slabs
                ],
                axis=0,
            )
        )
    score[...] = jnp.zeros(score.shape, jnp.float32)
    score_lane = lax.broadcasted_iota(jnp.int32, score.shape, 1)

    @pl.loop(0, tiles)
    def _(n):
        first = pl.multiple_of(n * tile, tile)
        weight_copy(0, n).wait()

        @pl.when(n + 1 < tiles)
        def _():
            for k in range(3):
                weight_copy(k, n + 1).start()

        gate = product(0, wg, first)
        weight_copy(1, n).wait()
        up = product(0, wu, first)
        weight_copy(2, n).wait()
        hid = product(1, wd, first)
        unit = first + lax.broadcasted_iota(jnp.int32, gate.shape, 1)
        share = jnp.zeros(gate.shape, jnp.float32)
        sig = jax.nn.sigmoid(gate)
        act = gate * sig
        both = up * hid
        scores = act * both
        total = score[...]
        for e in range(local):
            inside = (unit >= e * hidden) & (unit < (e + 1) * hidden)
            share = jnp.where(inside, shares[e], share)
            own = jnp.sum(jnp.where(inside, scores, 0.0), axis=1, keepdims=True)
            total = total + jnp.where(score_lane == e, own, 0.0)
        score[...] = total
        d_gate[:, pl.ds(first, tile)] = (share * (both * sig * (1.0 + gate * (1.0 - sig)))).astype(
            jnp.bfloat16
        )
        d_up[:, pl.ds(first, tile)] = (share * (hid * act)).astype(jnp.bfloat16)

    for dx, dc in blocks:
        @pl.loop(0, width // wide)
        def _(n):
            at = pl.multiple_of(n * wide, wide)
            source = pl.ds(pl.multiple_of(feature(dx, dc) + at, wide), wide)
            total = lax.dot_general(
                d_gate[...], wg[:, source], NN, preferred_element_type=jnp.float32
            ) + lax.dot_general(d_up[...], wu[:, source], NN, preferred_element_type=jnp.float32)
            total = total.astype(jnp.bfloat16)
            for i, (q, dy) in enumerate(slabs):
                outs[2 * q + dc][out_at[q][dy, dx], :, pl.ds(at, wide)] = total[i * rows : (i + 1) * rows]


def expert_call(where, pieces, probs, wg, wu, wd, local, piece_at, out_at, ndy, ndx):
    units, full = wg.shape
    rows, width = pieces[0][0].shape[1:]
    tile = next(t for t in (256, 128, 64, 32, 16) if units % t == 0)
    wide = next(t for t in (1024, 512, 256, 128) if width % t == 0)
    vmem, hbm = pl.BlockSpec(memory_space=pltpu.VMEM), pl.BlockSpec(memory_space=pltpu.HBM)
    out = jax.ShapeDtypeStruct((ndy * ndx, rows, width), jnp.bfloat16)
    n_q, first = len(pieces), 0
    places = []
    for at, of in zip(piece_at, pieces):
        places.append({l: first + i for l, i in at.items()})
        first += len(of)
    plan = (places, out_at, first, n_q, ndy, ndx, local, tile, wide)
    weight = pltpu.VMEM((units, full), jnp.bfloat16)
    m = n_q * ndy * rows
    results = pl.pallas_call(
        functools.partial(expert_kernel, plan),
        in_specs=[pl.BlockSpec(memory_space=pltpu.SMEM)] + [vmem] * (first + 1) + [hbm] * 3,
        out_specs=[vmem] * (2 * n_q + 1),
        scratch_shapes=[weight] * 3
        + [pltpu.VMEM((m, units), jnp.bfloat16)] * 2
        + [pltpu.SemaphoreType.DMA((3, units // tile))],
        out_shape=[out] * (2 * n_q) + [jax.ShapeDtypeStruct((m, 128), jnp.float32)],
        compiler_params=pltpu.CompilerParams(vmem_limit_bytes=40 << 20),
        cost_estimate=pl.CostEstimate(
            flops=10 * m * units * full, bytes_accessed=6 * units * full, transcendentals=0
        ),
    )(where, *[p for of in pieces for p in of], probs, *[
        pltpu.with_memory_space_constraint(w, pltpu.HBM) for w in (wg, wu, wd)
    ])
    return [results[2 * q : 2 * q + 2] for q in range(n_q)], results[-1]


def exchange(x, axis, step):
    return lax.ppermute(x, axis, [(i, i ^ step) for i in range(lax.axis_size(axis))])


def bits(size):
    return [1 << b for b in range(size.bit_length() - 1)]


def last_bit(v):
    return 1 << (v.bit_length() - 1)


def added(a, b):
    return (a.astype(jnp.float32) + b.astype(jnp.float32)).astype(jnp.bfloat16)


def body(tokens, grad_out, expert_ids, gate_probs, gate_weight, up_weight, down_weight):
    far, near, cols = lax.axis_size("far"), lax.axis_size("near"), lax.axis_size("col")
    z, y, x, c = (lax.axis_index(n) for n in ("far", "near", "col", "half"))
    me = z * near + y
    local, _, full = gate_weight.shape
    weights = [w.reshape(-1, full) for w in (gate_weight, up_weight, down_weight)]
    experts = local * far * near
    rows, width = tokens.shape
    spread = jax.nn.one_hot(expert_ids, experts, dtype=jnp.float32)
    probs = jnp.sum(spread * gate_probs[:, :, None], axis=1)
    features = [(x ^ dx) * 2 + (c ^ dc) for dx in range(cols) for dc in range(2)]
    where = jnp.stack([me] + features).astype(jnp.int32)
    labels = [(dy, dx) for dy in range(near) for dx in range(cols)]
    depth = {l: bin(l[0]).count("1") + bin(l[1]).count("1") for l in labels}
    depths = max(depth.values())

    have = [{} for _ in range(far)]
    have[0][0, 0, 0] = jnp.stack([tokens, grad_out])
    scores = [None] * far

    def level_ops(q, level):
        ops = []
        for dy, dx in labels:
            if depth[dy, dx] != level:
                continue
            if dy and (q % 2 == 0 or not dx):
                ops.append((q, (dy, dx, 0), (dy ^ last_bit(dy), dx, 0), "near", last_bit(dy)))
            else:
                ops.append((q, (dy, dx, 0), (dy, dx ^ last_bit(dx), 0), "col", last_bit(dx)))
        return sorted(ops, key=lambda o: o[3])

    def half_ops(q, levels):
        return [(q, (dy, dx, 1), (dy, dx, 0), "half", 1) for dy, dx in labels if depth[dy, dx] in levels]

    def far_ops(q):
        return [(q, (0, 0, 0), None, "far", q)] if 0 < q < far else []

    def tied(values, ready):
        return lax.optimization_barrier((values, ready))[0] if ready else values

    def run(ops, ready):
        sources = [have[0][0, 0, 0] if o[2] is None else have[o[0]][o[2]] for o in ops]
        for o, a in zip(ops, tied(sources, ready)):
            have[o[0]][o[1]] = exchange(a, o[3], o[4])
        return [have[o[0]][o[1]] for o in ops if o[3] in ("near", "col")]

    def compute(qs, ready):
        pieces = [list(have[q].values()) for q in qs]
        piece_at = [{l: i for i, l in enumerate(have[q])} for q in qs]
        out_at = []
        for q in qs:
            x_major = q % 2 == 1
            out_at.append({(dy, dx): dx * near + dy if x_major else dy * cols + dx for dy, dx in labels})
        table = tied(jnp.stack([both[q] for q in qs]), ready)
        outs, score = expert_call(where, pieces, table, *weights, local, piece_at, out_at, near, cols)
        for i, q in enumerate(qs):
            scores[q] = score[i * near * rows : (i + 1) * near * rows]
        return outs

    class Sum:
        def __init__(self, q, keep, send):
            self.q, self.keep = q, keep
            axes = ("col", "near") if q % 2 == 1 else ("near", "col")
            self.steps = [(a, s) for a in axes for s in reversed(bits(near if a == "near" else cols))]
            self.got = exchange(send, "half", 1)

        def fold(self):
            half = self.keep.shape[0] // 2
            self.send = added(self.keep[half:], self.got[half:])
            self.keep = added(self.keep[:half], self.got[:half])
            return [self.send, self.keep]

        def step(self, ready=()):
            axis, step = self.steps.pop(0)
            self.got = exchange(tied(self.send, list(ready)), axis, step)

        def home(self):
            mine = added(self.keep[0], self.got[0])
            return exchange(mine, "far", self.q) if self.q else mine

    table = [probs] + [exchange(probs, "far", q) for q in range(1, far)]
    both, done = None, []

    def group(ops, extra=()):
        ready = (done[-2] if len(done) > 1 else []) + list(extra)
        done.append(run(ops, ready))

    sums, total = [], None

    def finish(s):
        nonlocal total
        mine = s.home().astype(jnp.float32)
        total = mine if total is None else total + mine

    waiting, late = [], []
    for p in range(0, far, 2):
        a, b = p, p + 1
        if p == 0:
            group(far_ops(1) + far_ops(2) + level_ops(0, 1))
            group(far_ops(3) + level_ops(1, 1) + half_ops(0, (0,)), have[1].values())
            both = jnp.stack(table)
            group(level_ops(a, 2) + half_ops(a, (1,)), [both])
            both = jnp.stack([both, exchange(both, "near", 1)], axis=1)
            group(level_ops(b, 2) + half_ops(b, (0, 1)), list(have[2].values()) if far > 2 else [])
        else:
            group(level_ops(a, 1) + half_ops(a, (0,)) + late[: len(late) // 2] + far_ops(a + 2), [both])
            group(level_ops(b, 1) + half_ops(b, (0,)) + late[len(late) // 2 :] + far_ops(b + 2))
            late = []
            outs = compute(waiting, [])
            sums = [Sum(q, *o) for q, o in zip(waiting, outs)]
            waiting = []
            group(level_ops(a, 2) + half_ops(a, (1,)), sum(map(list, outs), []))
            group(level_ops(b, 2) + half_ops(b, (1,)), have[a + 2].values() if a + 2 < far else ())
        for level in range(3, depths + 1):
            group(level_ops(a, level) + half_ops(a, (level - 1,)))
            group(level_ops(b, level) + half_ops(b, (level - 1,)))
        late = half_ops(a, (depths,)) + half_ops(b, (depths,))
        waiting = [a, b]
        if sums and p + 2 < far:
            folded = [s.fold() for s in sums]
            while sums[0].steps:
                for s in sums:
                    s.step()
                if sums[0].steps:
                    for s in sums:
                        s.fold()
            for s in sums:
                finish(s)
            sums = []
    run(late, [])
    folded = sum([s.fold() for s in sums], [])
    for s in sums:
        s.step()
    first = Sum(waiting[0], *compute(waiting[:1], folded)[0])
    folded = sum([s.fold() for s in sums], [])
    for s in sums:
        s.step()
    folded += first.fold()
    first.step()
    second = Sum(waiting[1], *compute(waiting[1:], folded)[0])
    rest = sums + [first, second]
    second.fold()
    second.step()
    while rest:
        for s in list(rest):
            if s.steps:
                s.fold()
                s.step()
            else:
                finish(s)
                rest.remove(s)
    grad_tokens = total.astype(jnp.bfloat16)

    table = jnp.stack([s.reshape(near, rows, -1)[:, :, :local] for s in scores])
    table = table.transpose(0, 1, 3, 2)
    table = table + exchange(table, "half", 1)
    for step in bits(cols):
        table = table + exchange(table, "col", step)
    parts = [[table[q, dy] if dy == 0 else None for dy in range(near)] for q in range(far)]
    for dy in range(1, near):
        got = exchange(table[:, dy], "near", dy)
        for q in range(far):
            parts[q][dy] = got[q]
    for q in range(1, far):
        got = exchange(jnp.stack(parts[q]), "far", q)
        parts[q] = [got[dy] for dy in range(near)]
    found = jnp.stack([p for of in parts for p in of])
    index = jnp.arange(far * near)
    mine = (index[:, None] ^ me) == index[None, :]
    by_expert = jnp.sum(jnp.where(mine[:, :, None, None], found[None], 0.0), axis=1)
    by_expert = by_expert.reshape(experts, rows)
    grad_gates = jnp.sum(spread * by_expert.T[:, None, :], axis=2)
    return (grad_tokens, grad_gates.astype(jnp.bfloat16))


def solution(mesh):
    expert, ctx = mesh.shape["expert"], mesh.shape["ctx"]
    fine = Mesh(mesh.devices.reshape(expert // 2, 2, ctx // 2, 2), ("far", "near", "col", "half"))
    e, c = ("far", "near"), ("col", "half")
    return jax.shard_map(
        body,
        mesh=fine,
        in_specs=(P(e, c), P(e, c), P(e), P(e), P(e, c), P(e, c), P(e, c)),
        out_specs=(P(e, c), P(e)),
        check_vma=False,
    )
```

time: 407 us -> 252 us (0.62)
  blocking collectives: 123 us -> 0 us
  Pallas kernels: 0 us -> 62.4 us
  matrix products: 54.1 us -> 0 us
  waiting for transfers between devices: 170 us -> 116 us
  starting transfers between devices: 12.5 us -> 49.3 us
  local copies, waits for them, and re-layouts: 19.5 us -> 6.19 us
  between operations: 14 us -> 0.91 us
  other arithmetic: 10.1 us -> 17.1 us
    all_to_all x2 -> x0, blocking collectives: 116 us -> none  [the longest x1 59.1 us: body(): lax.all_to_all(sent_rows, 'expert', split_axis=0, concat_axis=0, tiled=True)]
    ppermute x0 -> x56, waiting for transfers between devices: none -> 116 us  [exchange(): lax.ppermute(x, axis, [(i, i ^ step) for i in range(lax.axis_size(axis))])]
    reduce_scatter x1 -> x0, waiting for transfers between devices: 65.4 us -> none  [body(): lax.psum_scatter(block_terms, 'ctx', scatter_dimension=3, tiled=True)]
    pallas_call x0 -> x3, Pallas kernels: none -> 62.4 us  [expert_call(): pl.pallas_call(functools.partial(expert_kernel, plan), in_specs=[pl.Block...]
    all_gather x2 -> x0, waiting for transfers between devices: 61.1 us -> none  [the longest x1 56.4 us: body(): lax.all_gather(got_grads, 'ctx', axis=2, tiled=True)]
    dot_general x7 -> x0, matrix products: 54.1 us -> none  [the longest x1 13.6 us: body(): jnp.einsum('secf,efd->secd', grad_pre_up, up_weight, preferred_element_ty...]
    ppermute x0 -> x56, starting transfers between devices: none -> 49.3 us  [exchange(): lax.ppermute(x, axis, [(i, i ^ step) for i in range(lax.axis_size(axis))])]
    all_to_all x2 -> x0, waiting for transfers between devices: 43.4 us -> none  [the longest x1 43.4 us: body(): lax.all_to_all(back_rows, 'expert', split_axis=0, concat_axis=0, tiled=True)]
  transfers between devices with their start and end apart: 5 -> 56, of which waited for: 4 -> 16; matrix products, arithmetic and copies ran while one was open for 5% -> 7% of each run, Pallas kernels for 0% -> 18%
where the time goes in v1:
time: 252 us
  waiting for transfers between devices  116 us (46%)
  Pallas kernels  62.4 us (25%)
  starting transfers between devices  49.3 us (20%)
  other arithmetic  17.1 us (7%)
  local copies, waits for them, and re-layouts  6.19 us (2%)
    ppermute x56, waiting for transfers between devices, exchange(): lax.ppermute(x, axis, [(i, i ^ step) for i in range(lax.axis_size(axis))])  116 us
    pallas_call x3, Pallas kernels, expert_call(): pl.pallas_call(functools.partial(expert_kernel, plan), in_specs=[pl.Block...  62.4 us
    ppermute x56, starting transfers between devices, exchange(): lax.ppermute(x, axis, [(i, i ^ step) for i in range(lax.axis_size(axis))])  49.3 us
    convert_element_type x11, other arithmetic, added(): return (a.astype(jnp.float32) + b.astype(jnp.float32)).astype(jnp.bfloat16)  11.9 us
    unnamed x30, local copies, waits for them, and re-layouts  5.29 us
  transfers between devices with their start and end apart: 56, of which 16 were waited for; matrix products, arithmetic and copies ran while one was open for 7% of the time, Pallas kernels for 18%

profile of v1, /device:TPU:8, one launch (start us, length us, event | category | flops | bytes accessed | tf_op | source)
XLA Modules:
  0.0 251.6 jit_solution(9338546281987874302)
XLA Ops:
  1.8 1.9 collective-permute-start
  3.7 1.5 collective-permute-start.1
  6.0 2.8 %collective-permute-start.6 = (f32[128,16]{0,1:T(8,128)S(1)}, f32[128,16]{0,1:T(8,128)S(1)}, u32[]{:S(2)}, u32[]{:S(2)}) collective-permute-start(f32[128,16]{0,1:T(8,128)S(1)} %select_reduce_fusion.2), channel_id=1, source_target_pairs={{0,24},{8,16},{16,8},{24,0},{1,25},{9,17},{17,9},{25,1},{2,26},{10... | collective-permute-start | bytes 24584 | tf_op jit(solution)/shard_map/ppermute | solution.py:143
  10.1 5.5 %collective-permute-done.2.refs_9_ = bf16[2,128,1024]{2,1,0:T(8,128)(2,1)S(1)} collective-permute-done((bf16[2,128,1024]{2,1,0:T(8,128)(2,1)S(1)}, bf16[2,128,1024]{2,1,0:T(8,128)(2,1)S(1)}, u32[]{:S(2)}, u32[]{:S(2)}) %collective-permute-start.2) | collective-permute-done | bytes 524320 | tf_op jit(solution)/shard_map/ppermute | solution.py:143
  15.6 2.7 %collective-permute-start.5 = (f32[128,16]{0,1:T(8,128)S(1)}, f32[128,16]{0,1:T(8,128)S(1)}, u32[]{:S(2)}, u32[]{:S(2)}) collective-permute-start(f32[128,16]{0,1:T(8,128)S(1)} %select_reduce_fusion.2), channel_id=1, source_target_pairs={{0,16},{8,24},{16,0},{24,8},{1,17},{9,25},{17,1},{25,9},{2,18},{10... | collective-permute-start | bytes 24584 | tf_op jit(solution)/shard_map/ppermute | solution.py:143
  21.8 1.7 collective-permute-start.19
  24.0 27.3 %collective-permute-done.10.refs_1_ = bf16[2,128,1024]{2,1,0:T(8,128)(2,1)S(1)} collective-permute-done((bf16[2,128,1024]{2,1,0:T(8,128)(2,1)S(1)}, bf16[2,128,1024]{2,1,0:T(8,128)(2,1)S(1)}, u32[]{:S(2)}, u32[]{:S(2)}) %collective-permute-start.10) | collective-permute-done | bytes 524320 | tf_op jit(solution)/shard_map/ppermute | solution.py:143
  53.2 11.0 %collective-permute-done.19.refs_1_ = bf16[2,128,1024]{2,1,0:T(8,128)(2,1)S(1)} collective-permute-done((bf16[2,128,1024]{2,1,0:T(8,128)(2,1)S(1)}, bf16[2,128,1024]{2,1,0:T(8,128)(2,1)S(1)}, u32[]{:S(2)}, u32[]{:S(2)}) %collective-permute-start.19) | collective-permute-done | bytes 524320 | tf_op jit(solution)/shard_map/ppermute | solution.py:143
  64.4 1.6 collective-permute-start.11
  66.2 7.0 %collective-permute-done.11 = f32[4,128,16]{2,1,0:T(8,128)S(1)} collective-permute-done((f32[4,128,16]{2,1,0:T(8,128)S(1)}, f32[4,128,16]{2,1,0:T(8,128)S(1)}, u32[]{:S(2)}, u32[]{:S(2)}) %collective-permute-start.11) | collective-permute-done | bytes 32800 | tf_op jit(solution)/shard_map/ppermute | solution.py:143
  75.2 1.6 collective-permute-start.28
  76.8 1.5 collective-permute-start.29
  79.4 29.7 %shard_map.86 = (bf16[4,128,1024]{2,1,0:T(8,128)(2,1)S(1)}, bf16[4,128,1024]{2,1,0:T(8,128)(2,1)S(1)}, bf16[4,128,1024]{2,1,0:T(8,128)(2,1)S(1)}, bf16[4,128,1024]{2,1,0:T(8,128)(2,1)S(1)}, f32[512,128]{1,0:T(8,128)S(1)}) custom-call(s32[5]{0:T(128)S(1)} %stack.87.refs_0_, bf16[2,128,1024]{2,1,0:T(8,128)(2,1)S(1)} %pad_maximum_fusion.1.refs_1_, ...), custom_call_target="tpu_custom_call" | custom-call | flops 16106127360 | bytes 18874368 | tf_op jit(solution)/shard_map/pallas_call | solution.py:124
  111.2 12.4 %collective-permute-done.31.refs_5_ = bf16[2,128,1024]{2,1,0:T(8,128)(2,1)S(1)} collective-permute-done((bf16[2,128,1024]{2,1,0:T(8,128)(2,1)S(1)}, bf16[2,128,1024]{2,1,0:T(8,128)(2,1)S(1)}, u32[]{:S(2)}, u32[]{:S(2)}) %collective-permute-start.31) | collective-permute-done | bytes 524320 | tf_op jit(solution)/shard_map/ppermute | solution.py:143
  129.0 16.1 %shard_map.87 = (bf16[4,128,1024]{2,1,0:T(8,128)(2,1)S(1)}, bf16[4,128,1024]{2,1,0:T(8,128)(2,1)S(1)}, f32[256,128]{1,0:T(8,128)S(1)}) custom-call(s32[5]{0:T(128)S(1)} %stack.87.refs_0_, bf16[2,128,1024]{2,1,0:T(8,128)(2,1)S(1)} %collective-permute-done.10.refs_1_, bf16[2,128,1024]{2,1,0:T(8,128)(2,1)S(1)} %collective-permute-done.28.refs_2_, ...), custom_call_target="tpu_custom_call" | custom-call | flops 8053063680 | bytes 18874368 | tf_op jit(solution)/shard_map/pallas_call | solution.py:124
  147.4 2.3 collective-permute-done.25
  153.3 6.9 %collective-permute-done.22 = bf16[2,128,1024]{2,1,0:T(8,128)(2,1)} collective-permute-done((bf16[2,128,1024]{2,1,0:T(8,128)(2,1)}, bf16[2,128,1024]{2,1,0:T(8,128)(2,1)}, u32[]{:S(2)}, u32[]{:S(2)}) %collective-permute-start.22) | collective-permute-done | bytes 524320 | tf_op jit(solution)/shard_map/ppermute | solution.py:143
  160.3 2.1 add_convert_fusion.19
  162.9 2.6 %collective-permute-done.26 = bf16[1,128,1024]{2,1,0:T(8,128)(2,1)} collective-permute-done((bf16[1,128,1024]{2,1,0:T(8,128)(2,1)}, bf16[1,128,1024]{2,1,0:T(8,128)(2,1)}, u32[]{:S(2)}, u32[]{:S(2)}) %collective-permute-start.26) | collective-permute-done | bytes 262176 | tf_op jit(solution)/shard_map/ppermute | solution.py:143
  165.4 1.9 fusion.4
  167.4 2.6 %add_convert_fusion.3 = (bf16[2,128,1024]{2,1,0:T(8,128)(2,1)}, bf16[2,128,1024]{2,1,0:T(8,128)(2,1)}) fusion(bf16[4,128,1024]{2,1,0:T(8,128)(2,1)} %collective-permute-done.35, bf16[4,128,1024]{2,1,0:T(8,128)(2,1)S(1)} %get-tuple-element.64), kind=kLoop, calls=%fused_computation.3 | loop fusion | flops 2097152 | bytes 3145728 | tf_op jit(solution)/shard_map/convert_element_type | solution.py:155
  172.9 16.6 %shard_map.88 = (bf16[4,128,1024]{2,1,0:T(8,128)(2,1)S(1)}, bf16[4,128,1024]{2,1,0:T(8,128)(2,1)S(1)}, f32[256,128]{1,0:T(8,128)S(1)}) custom-call(s32[5]{0:T(128)S(1)} %stack.87.refs_0_, bf16[2,128,1024]{2,1,0:T(8,128)(2,1)S(1)} %collective-permute-done.19.refs_1_, bf16[2,128,1024]{2,1,0:T(8,128)(2,1)S(1)} %copy-done.3, ...), custom_call_target="tpu_custom_call" | custom-call | flops 8053063680 | bytes 18874368 | tf_op jit(solution)/shard_map/pallas_call | solution.py:124
  191.0 1.6 collective-permute-start.51
  195.9 11.1 %collective-permute-done.52 = f32[4,2,128]{2,0,1:T(4,128)S(1)} collective-permute-done((f32[4,2,128]{2,0,1:T(4,128)S(1)}, f32[4,2,128]{2,0,1:T(4,128)S(1)}, u32[]{:S(2)}, u32[]{:S(2)}) %collective-permute-start.52) | collective-permute-done | bytes 4128 | tf_op jit(solution)/shard_map/ppermute | solution.py:143
  207.1 1.8 collective-permute-start.53
  209.3 1.6 collective-permute-start.47
  211.5 3.4 %collective-permute-start.54 = (f32[2,2,128]{2,1,0:T(2,128)S(1)}, f32[2,2,128]{2,1,0:T(2,128)S(1)}, u32[]{:S(2)}, u32[]{:S(2)}) collective-permute-start(f32[2,2,128]{2,1,0:T(2,128)S(1)} %pad_maximum_fusion.4), channel_id=1, source_target_pairs={{0,16},{8,24},{16,0},{24,8},{1,17},{9,25},{17,1},{25,9},{2,18},{10... | collective-permute-start | bytes 6152 | tf_op jit(solution)/shard_map/ppermute | solution.py:143
  215.9 5.6 %collective-permute-done.47 = bf16[2,128,1024]{2,1,0:T(8,128)(2,1)S(1)} collective-permute-done((bf16[2,128,1024]{2,1,0:T(8,128)(2,1)S(1)}, bf16[2,128,1024]{2,1,0:T(8,128)(2,1)S(1)}, u32[]{:S(2)}, u32[]{:S(2)}) %collective-permute-start.47) | collective-permute-done | bytes 524320 | tf_op jit(solution)/shard_map/ppermute | solution.py:143
  223.7 4.2 %collective-permute-done.37 = bf16[1,128,1024]{2,1,0:T(8,128)(2,1)S(1)} collective-permute-done((bf16[1,128,1024]{2,1,0:T(8,128)(2,1)S(1)}, bf16[1,128,1024]{2,1,0:T(8,128)(2,1)S(1)}, u32[]{:S(2)}, u32[]{:S(2)}) %collective-permute-start.37) | collective-permute-done | bytes 262176 | tf_op jit(solution)/shard_map/ppermute | solution.py:143
  229.7 1.6 collective-permute-start.49
  232.7 11.1 %collective-permute-done.38 = bf16[128,1024]{1,0:T(8,128)(2,1)S(1)} collective-permute-done((bf16[128,1024]{1,0:T(8,128)(2,1)S(1)}, bf16[128,1024]{1,0:T(8,128)(2,1)S(1)}, u32[]{:S(2)}, u32[]{:S(2)}) %collective-permute-start.38) | collective-permute-done | bytes 262176 | tf_op jit(solution)/shard_map/ppermute | solution.py:143
  243.8 6.8 %collective-permute-done.49 = bf16[128,1024]{1,0:T(8,128)(2,1)S(1)} collective-permute-done((bf16[128,1024]{1,0:T(8,128)(2,1)S(1)}, bf16[128,1024]{1,0:T(8,128)(2,1)S(1)}, u32[]{:S(2)}, u32[]{:S(2)}) %collective-permute-start.49) | collective-permute-done | bytes 262176 | tf_op jit(solution)/shard_map/ppermute | solution.py:143
  (148 shorter events, 42.6 us)
Async XLA Ops:
  1.8 20.0 %collective-permute-start = (bf16[2,128,1024]{2,1,0:T(8,128)(2,1)S(1)}, bf16[2,128,1024]{2,1,0:T(8,128)(2,1)S(1)}, u32[]{:S(2)}, u32[]{:S(2)}) collective-permute-start(bf16[2,128,1024]{2,1,0:T(8,128)(2,1)S(1)} %pad_maximum_fusion.1.refs_1_), channel_id=1, source_target_pairs={{0,2},{2,0},{1,3},{3,1},{4,6},{6,4},{5,7},{7,5},{8,10},{10,8},{9,1... | collective-permute-start | bytes 1572872 | tf_op jit(solution)/shard_map/ppermute | solution.py:143
  3.7 19.8 %collective-permute-start.1 = (bf16[2,128,1024]{2,1,0:T(8,128)(2,1)S(1)}, bf16[2,128,1024]{2,1,0:T(8,128)(2,1)S(1)}, u32[]{:S(2)}, u32[]{:S(2)}) collective-permute-start(bf16[2,128,1024]{2,1,0:T(8,128)(2,1)S(1)} %pad_maximum_fusion.1.refs_1_), channel_id=1, source_target_pairs={{0,4},{4,0},{1,5},{5,1},{2,6},{6,2},{3,7},{7,3},{8,12},{12,8},{9,1... | collective-permute-start | bytes 1572872 | tf_op jit(solution)/shard_map/ppermute | solution.py:143
  18.3 33.0 %collective-permute-start.10 = (bf16[2,128,1024]{2,1,0:T(8,128)(2,1)S(1)}, bf16[2,128,1024]{2,1,0:T(8,128)(2,1)S(1)}, u32[]{:S(2)}, u32[]{:S(2)}) collective-permute-start(bf16[2,128,1024]{2,1,0:T(8,128)(2,1)S(1)} %pad_maximum_fusion.1.refs_1_), channel_id=1, source_target_pairs={{0,16},{8,24},{16,0},{24,8},{1,17},{9,25},{17,1},{25,9},{2,18},{10... | collective-permute-start | bytes 1572872 | tf_op jit(solution)/shard_map/ppermute | solution.py:143
  18.5 32.7 %collective-permute-start.13 = (bf16[2,128,1024]{2,1,0:T(8,128)(2,1)S(1)}, bf16[2,128,1024]{2,1,0:T(8,128)(2,1)S(1)}, u32[]{:S(2)}, u32[]{:S(2)}) collective-permute-start(bf16[2,128,1024]{2,1,0:T(8,128)(2,1)S(1)} %collective-permute-done.2.refs_9_), channel_id=1, source_target_pairs={{0,2},{2,0},{1,3},{3,1},{4,6},{6,4},{5,7},{7,5},{8,10},{10,8},{9,1... | collective-permute-start | bytes 1572872 | tf_op jit(solution)/shard_map/ppermute | solution.py:143
  20.3 31.0 %collective-permute-start.14 = (bf16[2,128,1024]{2,1,0:T(8,128)(2,1)S(1)}, bf16[2,128,1024]{2,1,0:T(8,128)(2,1)}, u32[]{:S(2)}, u32[]{:S(2)}) collective-permute-start(bf16[2,128,1024]{2,1,0:T(8,128)(2,1)S(1)} %collective-permute-done.2.refs_9_), channel_id=1, source_target_pairs={{0,4},{4,0},{1,5},{5,1},{2,6},{6,2},{3,7},{7,3},{8,12},{12,8},{9,1... | collective-permute-start | bytes 1572872 | tf_op jit(solution)/shard_map/ppermute | solution.py:143
  21.8 42.4 %collective-permute-start.19 = (bf16[2,128,1024]{2,1,0:T(8,128)(2,1)S(1)}, bf16[2,128,1024]{2,1,0:T(8,128)(2,1)S(1)}, u32[]{:S(2)}, u32[]{:S(2)}) collective-permute-start(bf16[2,128,1024]{2,1,0:T(8,128)(2,1)S(1)} %pad_maximum_fusion.1.refs_1_), channel_id=1, source_target_pairs={{0,24},{8,16},{16,8},{24,0},{1,25},{9,17},{17,9},{25,1},{2,26},{10... | collective-permute-start | bytes 1572872 | tf_op jit(solution)/shard_map/ppermute | solution.py:143
  23.5 40.9 %collective-permute-start.7 = (bf16[2,128,1024]{2,1,0:T(8,128)(2,1)S(1)}, bf16[2,128,1024]{2,1,0:T(8,128)(2,1)}, u32[]{:S(2)}, u32[]{:S(2)}) collective-permute-start(bf16[2,128,1024]{2,1,0:T(8,128)(2,1)S(1)} %collective-permute-done.refs_2_), channel_id=1, source_target_pairs={{0,4},{4,0},{1,5},{5,1},{2,6},{6,2},{3,7},{7,3},{8,12},{12,8},{9,1... | collective-permute-start | bytes 1572872 | tf_op jit(solution)/shard_map/ppermute | solution.py:143
  51.3 14.7 %collective-permute-start.15 = (bf16[2,128,1024]{2,1,0:T(8,128)(2,1)}, bf16[2,128,1024]{2,1,0:T(8,128)(2,1)}, u32[]{:S(2)}, u32[]{:S(2)}) collective-permute-start(bf16[2,128,1024]{2,1,0:T(8,128)(2,1)} %collective-permute-done.14.refs_11_), channel_id=1, source_target_pairs={{0,2},{2,0},{1,3},{3,1},{4,6},{6,4},{5,7},{7,5},{8,10},{10,8},{9,1... | collective-permute-start | bytes 1572872 | tf_op jit(solution)/shard_map/ppermute | solution.py:143
  52.7 20.5 %collective-permute-start.8 = (bf16[2,128,1024]{2,1,0:T(8,128)(2,1)S(1)}, bf16[2,128,1024]{2,1,0:T(8,128)(2,1)}, u32[]{:S(2)}, u32[]{:S(2)}) collective-permute-start(bf16[2,128,1024]{2,1,0:T(8,128)(2,1)S(1)} %collective-permute-done.refs_2_), channel_id=1, source_target_pairs={{0,1},{1,0},{2,3},{3,2},{4,5},{5,4},{6,7},{7,6},{8,9},{9,8},{10,11... | collective-permute-start | bytes 1572872 | tf_op jit(solution)/shard_map/ppermute | solution.py:143
  52.7 21.0 %collective-permute-start.9 = (bf16[2,128,1024]{2,1,0:T(8,128)(2,1)S(1)}, bf16[2,128,1024]{2,1,0:T(8,128)(2,1)}, u32[]{:S(2)}, u32[]{:S(2)}) collective-permute-start(bf16[2,128,1024]{2,1,0:T(8,128)(2,1)S(1)} %collective-permute-done.1.refs_3_), channel_id=1, source_target_pairs={{0,1},{1,0},{2,3},{3,2},{4,5},{5,4},{6,7},{7,6},{8,9},{9,8},{10,11... | collective-permute-start | bytes 1572872 | tf_op jit(solution)/shard_map/ppermute | solution.py:143
  75.2 34.5 %collective-permute-start.28 = (bf16[2,128,1024]{2,1,0:T(8,128)(2,1)S(1)}, bf16[2,128,1024]{2,1,0:T(8,128)(2,1)S(1)}, u32[]{:S(2)}, u32[]{:S(2)}) collective-permute-start(bf16[2,128,1024]{2,1,0:T(8,128)(2,1)S(1)} %collective-permute-done.10.refs_1_), channel_id=1, source_target_pairs={{0,2},{2,0},{1,3},{3,1},{4,6},{6,4},{5,7},{7,5},{8,10},{10,8},{9,1... | collective-permute-start | bytes 1572872 | tf_op jit(solution)/shard_map/ppermute | solution.py:143
  76.8 32.9 %collective-permute-start.29 = (bf16[2,128,1024]{2,1,0:T(8,128)(2,1)S(1)}, bf16[2,128,1024]{2,1,0:T(8,128)(2,1)S(1)}, u32[]{:S(2)}, u32[]{:S(2)}) collective-permute-start(bf16[2,128,1024]{2,1,0:T(8,128)(2,1)S(1)} %collective-permute-done.10.refs_1_), channel_id=1, source_target_pairs={{0,4},{4,0},{1,5},{5,1},{2,6},{6,2},{3,7},{7,3},{8,12},{12,8},{9,1... | collective-permute-start | bytes 1572872 | tf_op jit(solution)/shard_map/ppermute | solution.py:143
  109.1 14.5 %collective-permute-start.24 = (bf16[4,128,1024]{2,1,0:T(8,128)(2,1)S(1)}, bf16[4,128,1024]{2,1,0:T(8,128)(2,1)S(1)}, u32[]{:S(2)}, u32[]{:S(2)}) collective-permute-start(bf16[4,128,1024]{2,1,0:T(8,128)(2,1)S(1)} %get-tuple-element.56), channel_id=1, source_target_pairs={{0,1},{1,0},{2,3},{3,2},{4,5},{5,4},{6,7},{7,6},{8,9},{9,8},{10,11... | collective-permute-start | bytes 3145736 | tf_op jit(solution)/shard_map/ppermute | solution.py:143
  109.2 15.4 %collective-permute-start.21 = (bf16[4,128,1024]{2,1,0:T(8,128)(2,1)S(1)}, bf16[4,128,1024]{2,1,0:T(8,128)(2,1)S(1)}, u32[]{:S(2)}, u32[]{:S(2)}) collective-permute-start(bf16[4,128,1024]{2,1,0:T(8,128)(2,1)S(1)} %get-tuple-element.54), channel_id=1, source_target_pairs={{0,1},{1,0},{2,3},{3,2},{4,5},{5,4},{6,7},{7,6},{8,9},{9,8},{10,11... | collective-permute-start | bytes 3145736 | tf_op jit(solution)/shard_map/ppermute | solution.py:143
  109.7 13.9 %collective-permute-start.31 = (bf16[2,128,1024]{2,1,0:T(8,128)(2,1)S(1)}, bf16[2,128,1024]{2,1,0:T(8,128)(2,1)S(1)}, u32[]{:S(2)}, u32[]{:S(2)}) collective-permute-start(bf16[2,128,1024]{2,1,0:T(8,128)(2,1)S(1)} %collective-permute-done.28.refs_2_), channel_id=1, source_target_pairs={{0,4},{4,0},{1,5},{5,1},{2,6},{6,2},{3,7},{7,3},{8,12},{12,8},{9,1... | collective-permute-start | bytes 1572872 | tf_op jit(solution)/shard_map/ppermute | solution.py:143
  110.6 16.3 %collective-permute-start.30 = (bf16[2,128,1024]{2,1,0:T(8,128)(2,1)S(1)}, bf16[2,128,1024]{2,1,0:T(8,128)(2,1)S(1)}, u32[]{:S(2)}, u32[]{:S(2)}) collective-permute-start(bf16[2,128,1024]{2,1,0:T(8,128)(2,1)S(1)} %collective-permute-done.10.refs_1_), channel_id=1, source_target_pairs={{0,1},{1,0},{2,3},{3,2},{4,5},{5,4},{6,7},{7,6},{8,9},{9,8},{10,11... | collective-permute-start | bytes 1572872 | tf_op jit(solution)/shard_map/ppermute | solution.py:143
  110.7 17.8 %collective-permute-start.32 = (bf16[2,128,1024]{2,1,0:T(8,128)(2,1)S(1)}, bf16[2,128,1024]{2,1,0:T(8,128)(2,1)S(1)}, u32[]{:S(2)}, u32[]{:S(2)}) collective-permute-start(bf16[2,128,1024]{2,1,0:T(8,128)(2,1)S(1)} %collective-permute-done.28.refs_2_), channel_id=1, source_target_pairs={{0,1},{1,0},{2,3},{3,2},{4,5},{5,4},{6,7},{7,6},{8,9},{9,8},{10,11... | collective-permute-start | bytes 1572872 | tf_op jit(solution)/shard_map/ppermute | solution.py:143
  124.6 21.8 %collective-permute-start.39 = (bf16[2,128,1024]{2,1,0:T(8,128)(2,1)S(1)}, bf16[2,128,1024]{2,1,0:T(8,128)(2,1)S(1)}, u32[]{:S(2)}, u32[]{:S(2)}) collective-permute-start(bf16[2,128,1024]{2,1,0:T(8,128)(2,1)S(1)} %collective-permute-done.19.refs_1_), channel_id=1, source_target_pairs={{0,2},{2,0},{1,3},{3,1},{4,6},{6,4},{5,7},{7,5},{8,10},{10,8},{9,1... | collective-permute-start | bytes 1572872 | tf_op jit(solution)/shard_map/ppermute | solution.py:143
  126.9 19.6 %collective-permute-start.40 = (bf16[2,128,1024]{2,1,0:T(8,128)(2,1)S(1)}, bf16[2,128,1024]{2,1,0:T(8,128)(2,1)}, u32[]{:S(2)}, u32[]{:S(2)}) collective-permute-start(bf16[2,128,1024]{2,1,0:T(8,128)(2,1)S(1)} %collective-permute-done.19.refs_1_), channel_id=1, source_target_pairs={{0,4},{4,0},{1,5},{5,1},{2,6},{6,2},{3,7},{7,3},{8,12},{12,8},{9,1... | collective-permute-start | bytes 1572872 | tf_op jit(solution)/shard_map/ppermute | solution.py:143
  128.4 21.3 %collective-permute-start.25 = (bf16[2,128,1024]{2,1,0:T(8,128)(2,1)S(1)}, bf16[2,128,1024]{2,1,0:T(8,128)(2,1)S(1)}, u32[]{:S(2)}, u32[]{:S(2)}) collective-permute-start(bf16[2,128,1024]{2,1,0:T(8,128)(2,1)S(1)} %get-tuple-element.85), channel_id=1, source_target_pairs={{0,2},{2,0},{1,3},{3,1},{4,6},{6,4},{5,7},{7,5},{8,10},{10,8},{9,1... | collective-permute-start | bytes 1572872 | tf_op jit(solution)/shard_map/ppermute | solution.py:143
  145.1 22.3 %collective-permute-start.35 = (bf16[4,128,1024]{2,1,0:T(8,128)(2,1)S(1)}, bf16[4,128,1024]{2,1,0:T(8,128)(2,1)}, u32[]{:S(2)}, u32[]{:S(2)}) collective-permute-start(bf16[4,128,1024]{2,1,0:T(8,128)(2,1)S(1)} %get-tuple-element.65), channel_id=1, source_target_pairs={{0,1},{1,0},{2,3},{3,2},{4,5},{5,4},{6,7},{7,6},{8,9},{9,8},{10,11... | collective-permute-start | bytes 3145736 | tf_op jit(solution)/shard_map/ppermute | solution.py:143
  145.2 15.1 %collective-permute-start.22 = (bf16[2,128,1024]{2,1,0:T(8,128)(2,1)}, bf16[2,128,1024]{2,1,0:T(8,128)(2,1)}, u32[]{:S(2)}, u32[]{:S(2)}) collective-permute-start(bf16[2,128,1024]{2,1,0:T(8,128)(2,1)} %get-tuple-element.87), channel_id=1, source_target_pairs={{0,4},{4,0},{1,5},{5,1},{2,6},{6,2},{3,7},{7,3},{8,12},{12,8},{9,1... | collective-permute-start | bytes 1572872 | tf_op jit(solution)/shard_map/ppermute | solution.py:143
  146.3 23.6 %collective-permute-start.41 = (bf16[2,128,1024]{2,1,0:T(8,128)(2,1)S(1)}, bf16[2,128,1024]{2,1,0:T(8,128)(2,1)S(1)}, u32[]{:S(2)}, u32[]{:S(2)}) collective-permute-start(bf16[2,128,1024]{2,1,0:T(8,128)(2,1)S(1)} %collective-permute-done.19.refs_1_), channel_id=1, source_target_pairs={{0,1},{1,0},{2,3},{3,2},{4,5},{5,4},{6,7},{7,6},{8,9},{9,8},{10,11... | collective-permute-start | bytes 1572872 | tf_op jit(solution)/shard_map/ppermute | solution.py:143
  146.5 15.9 %collective-permute-start.42 = (bf16[2,128,1024]{2,1,0:T(8,128)(2,1)}, bf16[2,128,1024]{2,1,0:T(8,128)(2,1)}, u32[]{:S(2)}, u32[]{:S(2)}) collective-permute-start(bf16[2,128,1024]{2,1,0:T(8,128)(2,1)} %collective-permute-done.40.refs_3_), channel_id=1, source_target_pairs={{0,2},{2,0},{1,3},{3,1},{4,6},{6,4},{5,7},{7,5},{8,10},{10,8},{9,1... | collective-permute-start | bytes 1572872 | tf_op jit(solution)/shard_map/ppermute | solution.py:143
  150.6 14.9 %collective-permute-start.26 = (bf16[1,128,1024]{2,1,0:T(8,128)(2,1)}, bf16[1,128,1024]{2,1,0:T(8,128)(2,1)}, u32[]{:S(2)}, u32[]{:S(2)}) collective-permute-start(bf16[1,128,1024]{2,1,0:T(8,128)(2,1)} %add_convert_fusion.15), channel_id=1, source_target_pairs={{0,4},{4,0},{1,5},{5,1},{2,6},{6,2},{3,7},{7,3},{8,12},{12,8},{9,1... | collective-permute-start | bytes 786440 | tf_op jit(solution)/shard_map/ppermute | solution.py:143
  192.6 40.1 %collective-permute-start.23 = (bf16[1,128,1024]{2,1,0:T(8,128)(2,1)S(1)}, bf16[1,128,1024]{2,1,0:T(8,128)(2,1)S(1)}, u32[]{:S(2)}, u32[]{:S(2)}) collective-permute-start(bf16[1,128,1024]{2,1,0:T(8,128)(2,1)S(1)} %copy-done.10), channel_id=1, source_target_pairs={{0,2},{2,0},{1,3},{3,1},{4,6},{6,4},{5,7},{7,5},{8,10},{10,8},{9,1... | collective-permute-start | bytes 786440 | tf_op jit(solution)/shard_map/ppermute | solution.py:143
  193.2 39.5 %collective-permute-start.27 = (bf16[128,1024]{1,0:T(8,128)(2,1)}, bf16[128,1024]{1,0:T(8,128)(2,1)S(1)}, u32[]{:S(2)}, u32[]{:S(2)}) collective-permute-start(bf16[128,1024]{1,0:T(8,128)(2,1)} %fusion.4), channel_id=1, source_target_pairs={{0,8},{8,0},{16,24},{24,16},{1,9},{9,1},{17,25},{25,17},{2,10},{10... | collective-permute-start | bytes 786440 | tf_op jit(solution)/shard_map/ppermute | solution.py:143
  193.2 18.3 %collective-permute-start.36 = (bf16[2,128,1024]{2,1,0:T(8,128)(2,1)}, bf16[2,128,1024]{2,1,0:T(8,128)(2,1)S(1)}, u32[]{:S(2)}, u32[]{:S(2)}) collective-permute-start(bf16[2,128,1024]{2,1,0:T(8,128)(2,1)} %get-tuple-element.83), channel_id=1, source_target_pairs={{0,4},{4,0},{1,5},{5,1},{2,6},{6,2},{3,7},{7,3},{8,12},{12,8},{9,1... | collective-permute-start | bytes 1572872 | tf_op jit(solution)/shard_map/ppermute | solution.py:143
  194.3 14.6 %collective-permute-start.46 = (bf16[4,128,1024]{2,1,0:T(8,128)(2,1)S(1)}, bf16[4,128,1024]{2,1,0:T(8,128)(2,1)S(1)}, u32[]{:S(2)}, u32[]{:S(2)}) collective-permute-start(bf16[4,128,1024]{2,1,0:T(8,128)(2,1)S(1)} %get-tuple-element.74), channel_id=1, source_target_pairs={{0,1},{1,0},{2,3},{3,2},{4,5},{5,4},{6,7},{7,6},{8,9},{9,8},{10,11... | collective-permute-start | bytes 3145736 | tf_op jit(solution)/shard_map/ppermute | solution.py:143
  210.9 20.4 %collective-permute-start.55 = (f32[2,2,128]{2,1,0:T(2,128)S(1)}, f32[2,2,128]{2,1,0:T(2,128)S(1)}, u32[]{:S(2)}, u32[]{:S(2)}) collective-permute-start(f32[2,2,128]{2,1,0:T(2,128)S(1)} %pad_maximum_fusion.5), channel_id=1, source_target_pairs={{0,24},{8,16},{16,8},{24,0},{1,25},{9,17},{17,9},{25,1},{2,26},{10... | collective-permute-start | bytes 6152 | tf_op jit(solution)/shard_map/ppermute | solution.py:143
  229.0 14.9 %collective-permute-start.38 = (bf16[128,1024]{1,0:T(8,128)(2,1)S(1)}, bf16[128,1024]{1,0:T(8,128)(2,1)S(1)}, u32[]{:S(2)}, u32[]{:S(2)}) collective-permute-start(bf16[128,1024]{1,0:T(8,128)(2,1)S(1)} %fusion.5), channel_id=1, source_target_pairs={{0,16},{8,24},{16,0},{24,8},{1,17},{9,25},{17,1},{25,9},{2,18},{10... | collective-permute-start | bytes 786440 | tf_op jit(solution)/shard_map/ppermute | solution.py:143
  229.7 20.9 %collective-permute-start.49 = (bf16[128,1024]{1,0:T(8,128)(2,1)S(1)}, bf16[128,1024]{1,0:T(8,128)(2,1)S(1)}, u32[]{:S(2)}, u32[]{:S(2)}) collective-permute-start(bf16[128,1024]{1,0:T(8,128)(2,1)S(1)} %fusion.6), channel_id=1, source_target_pairs={{0,24},{8,16},{16,8},{24,0},{1,25},{9,17},{17,9},{25,1},{2,26},{10... | collective-permute-start | bytes 786440 | tf_op jit(solution)/shard_map/ppermute | solution.py:143
  (35 other events, 281.0 us)

commit v2 on v0

v2 whole, which is shorter than its diff:
```python
import functools
import jax
import jax.numpy as jnp
from jax import lax
from jax.experimental import pallas as pl
from jax.experimental.pallas import tpu as pltpu
from jax.sharding import Mesh, PartitionSpec as P

NT = (((1,), (1,)), ((), ()))
NN = (((1,), (0,)), ((), ()))
TN = (((0,), (0,)), ((), ()))


def padded(count):
    return 16 * -(-count // 16)


def expert_kernel(plan, *refs):
    at, out_at, n_in, ndy, ndx, local, experts, rows, tile, wide = plan
    where = refs[0]
    pieces = refs[1 : 1 + n_in]
    wg, wu, wd, keep, send, d_gate, d_up, score = refs[1 + n_in :]
    width = pieces[0].shape[1]
    units = wg.shape[0]
    hidden = units // local
    blocks = [(dx, dc) for dx in range(ndx) for dc in range(2)]

    def feature(dx, dc):
        return pl.multiple_of(where[1 + 2 * dx + dc] * width, width)

    def part(kind, dy, dx, dc):
        ref, first = at[kind, dy, dx, dc]
        return pieces[ref][first : first + rows]

    def product(kind, ref, first):
        total = None
        for dx, dc in blocks:
            x = jnp.concatenate([part(kind, dy, dx, dc) for dy in range(ndy)], axis=0)
            w = ref[pl.ds(first, tile), pl.ds(feature(dx, dc), width)]
            term = lax.dot_general(x, w, NT, preferred_element_type=jnp.float32)
            total = term if total is None else total + term
        return total

    slots = padded(experts)
    expert = lax.broadcasted_iota(jnp.int32, (slots, 128), 0)
    column = lax.broadcasted_iota(jnp.int32, (slots, 128), 1)
    mine = jnp.where((expert == where[0] * local + column) & (column < local), 1.0, 0.0).astype(jnp.bfloat16)
    shares = []
    for dy in range(ndy):
        ref, first = at[2, dy, 0, 0]
        table = pieces[ref][first : first + slots]
        shares.append(
            sum(
                lax.dot_general(
                    table[:, i * rows : (i + 1) * rows], mine, TN, preferred_element_type=jnp.float32
                )
                for i in range(3)
            )
        )
    shares = jnp.concatenate(shares, axis=0)
    score[...] = jnp.zeros(score.shape, jnp.float32)

    @pl.loop(0, units // tile)
    def _(n):
        first = pl.multiple_of(n * tile, tile)
        gate, up, hid = product(0, wg, first), product(0, wu, first), product(1, wd, first)
        unit = first + lax.broadcasted_iota(jnp.int32, gate.shape, 1)
        share = jnp.zeros(gate.shape, jnp.float32)
        sig = jax.nn.sigmoid(gate)
        act = gate * sig
        both = up * hid
        scores = act * both
        for e in range(local):
            inside = (unit >= e * hidden) & (unit < (e + 1) * hidden)
            share = jnp.where(inside, shares[:, e : e + 1], share)
        row = lax.broadcasted_iota(jnp.int32, (score.shape[0], tile), 0) * hidden
        of = first + lax.broadcasted_iota(jnp.int32, (score.shape[0], tile), 1)
        pick = jnp.where((of >= row) & (of < row + hidden), 1.0, 0.0).astype(jnp.bfloat16)
        high = scores.astype(jnp.bfloat16)
        low = (scores - high.astype(jnp.float32)).astype(jnp.bfloat16)
        score[...] += lax.dot_general(pick, high, NT, preferred_element_type=jnp.float32) + lax.dot_general(
            pick, low, NT, preferred_element_type=jnp.float32
        )
        d_gate[:, pl.ds(first, tile)] = (share * (both * sig * (1.0 + gate * (1.0 - sig)))).astype(
            jnp.bfloat16
        )
        d_up[:, pl.ds(first, tile)] = (share * (hid * act)).astype(jnp.bfloat16)

    extra = keep.shape[1] - rows
    per_row = width // rows
    place = lax.broadcasted_iota(jnp.int32, (extra, width), 0) * per_row
    place = place + lax.broadcasted_iota(jnp.int32, (extra, width), 1) // rows
    for dy in range(ndy):
        table = jnp.zeros((extra, width), jnp.float32)
        for e in range(local):
            line = jnp.concatenate([score[e : e + 1, dy * rows : (dy + 1) * rows]] * per_row, axis=1)
            table = jnp.where(place == where[0] * local + e, line, table)
        for dx, dc in blocks:
            (keep, send)[dc][out_at[dy, dx], rows:, :] = table.astype(jnp.bfloat16)

    for dx, dc in blocks:

        @pl.loop(0, width // wide)
        def _(n):
            start = pl.multiple_of(n * wide, wide)
            source = pl.ds(pl.multiple_of(feature(dx, dc) + start, wide), wide)
            total = lax.dot_general(
                d_gate[...], wg[:, source], NN, preferred_element_type=jnp.float32
            ) + lax.dot_general(d_up[...], wu[:, source], NN, preferred_element_type=jnp.float32)
            total = total.astype(jnp.bfloat16)
            for dy in range(ndy):
                (keep, send)[dc][out_at[dy, dx], :rows, pl.ds(start, wide)] = total[dy * rows : (dy + 1) * rows]


def expert_call(where, pieces, weights, local, experts, rows, at, out_at, ndy, ndx):
    units, full = weights[0].shape
    width = pieces[0].shape[1]
    tile = next(t for t in (256, 128, 64, 32, 16) if units % t == 0)
    wide = next(t for t in (1024, 512, 256, 128) if width % t == 0)
    vmem = pl.BlockSpec(memory_space=pltpu.VMEM)
    extra = padded(-(-experts // (width // rows)))
    out = jax.ShapeDtypeStruct((ndy * ndx, rows + extra, width), jnp.bfloat16)
    m = ndy * rows
    return pl.pallas_call(
        functools.partial(
            expert_kernel, (at, out_at, len(pieces), ndy, ndx, local, experts, rows, tile, wide)
        ),
        in_specs=[pl.BlockSpec(memory_space=pltpu.SMEM)] + [vmem] * (len(pieces) + 3),
        out_specs=[vmem] * 2,
        scratch_shapes=[pltpu.VMEM((m, units), jnp.bfloat16)] * 2
        + [pltpu.VMEM((padded(local), m), jnp.float32)],
        out_shape=[out] * 2,
        compiler_params=pltpu.CompilerParams(vmem_limit_bytes=16 << 20),
        cost_estimate=pl.CostEstimate(
            flops=10 * m * units * full, bytes_accessed=6 * units * full, transcendentals=0
        ),
    )(where, *pieces, *weights)


def exchange(x, axis, step):
    return lax.ppermute(x, axis, [(i, i ^ step) for i in range(lax.axis_size(axis))])


def passed(x, axis, pairs):
    return lax.ppermute(x, axis, pairs)


def bits(size):
    return [1 << b for b in range(size.bit_length() - 1)]


def last_bit(v):
    return 1 << (v.bit_length() - 1)


def added(a, b):
    return (a.astype(jnp.float32) + b.astype(jnp.float32)).astype(jnp.bfloat16)


class Cell:
    def __init__(self, value):
        self.v = value


def together(cells):
    cells = list({id(c): c for c in cells}.values())
    if len(cells) > 1:
        for c, v in zip(cells, lax.optimization_barrier([c.v for c in cells])):
            c.v = v


def touch_kernel(where, *refs):
    for i in range(where.shape[0]):
        refs[-1][i] = where[i]


def touch_call(where, arrays):
    smem, vmem = pl.BlockSpec(memory_space=pltpu.SMEM), pl.BlockSpec(memory_space=pltpu.VMEM)
    return pl.pallas_call(
        touch_kernel,
        in_specs=[smem] + [vmem] * len(arrays),
        out_specs=smem,
        out_shape=jax.ShapeDtypeStruct(where.shape, where.dtype),
        compiler_params=pltpu.CompilerParams(vmem_limit_bytes=2 << 20),
    )(where, *arrays)


def body(tokens, grad_out, expert_ids, gate_probs, gate_weight, up_weight, down_weight):
    far, near, cols = lax.axis_size("far"), lax.axis_size("near"), lax.axis_size("col")
    z, y, x, c = (lax.axis_index(n) for n in ("far", "near", "col", "half"))
    me = z * near + y
    local, _, full = gate_weight.shape
    weights = [w.reshape(-1, full) for w in (gate_weight, up_weight, down_weight)]
    experts = local * far * near
    rows, width = tokens.shape
    features = [(x ^ dx) * 2 + (c ^ dc) for dx in range(cols) for dc in range(2)]
    where = Cell(jnp.stack([me] + features).astype(jnp.int32))
    labels = [(dy, dx) for dy in range(near) for dx in range(cols)]
    depth = {l: bin(l[0]).count("1") + bin(l[1]).count("1") for l in labels}
    depths = max(depth.values())

    spread = jax.nn.one_hot(expert_ids, experts, dtype=jnp.float32)
    probs = jnp.sum(spread * gate_probs[:, :, None], axis=1).T
    parts = []
    for _ in range(3):
        parts.append(lax.reduce_precision(probs, 8, 7))
        probs = probs - parts[-1]
    table = jnp.concatenate(parts, axis=1).astype(jnp.bfloat16)
    table = jnp.pad(table, ((0, padded(experts) - experts), (0, width - 3 * rows)))

    have = [{} for _ in range(far)]
    have[0][0, 0, 0] = [Cell(jnp.concatenate([tokens, grad_out, table], axis=0))]

    def far_ops(q):
        return [(q, (0, 0, 0), [(c, None) for c in have[0][0, 0, 0]], "far", q)] if 0 < q < far else []

    line = far == 4
    inner = (z == 1) | (z == 2)
    outward, across = [(1, 0), (2, 3)], [(1, 2), (2, 1)]
    held = {}

    def line_sources(r):
        if r == 0:
            return [have[0][0, 0, 0][0]]
        if r == 1:
            return [held["across"], have[1][0, 0, 0][0]]
        return [held["inner"]] if r == 2 else []

    def line_step(r):
        if r == 0:
            own = have[0][0, 0, 0][0].v
            have[1][0, 0, 0] = [Cell(exchange(own, "far", 1))]
            held["across"] = Cell(passed(own, "far", across))
            return [have[1][0, 0, 0][0], held["across"]]
        if r == 1:
            held["outer"] = Cell(passed(held["across"].v, "far", outward))
            held["inner"] = Cell(passed(have[1][0, 0, 0][0].v, "far", across))
            return [held["outer"], held["inner"]]
        if r == 2:
            held["last"] = Cell(passed(held["inner"].v, "far", outward))
            return [held["last"]]
        return []

    def line_arrive(r):
        if r == 2:
            have[2][0, 0, 0] = [Cell(jnp.where(inner, held["inner"].v, held["outer"].v))]
        if r == 3:
            have[3][0, 0, 0] = [Cell(jnp.where(inner, held["across"].v, held["last"].v))]

    def level_ops(q, level):
        ops = []
        for dy, dx in labels:
            if depth[dy, dx] != level:
                continue
            if dy and dx:
                by_near, by_col = have[q][dy ^ last_bit(dy), dx, 0], have[q][dy, dx ^ last_bit(dx), 0]
                t = (by_near[0], (0, rows) if len(by_near) == 1 else None)
                g = (by_col[-1], (rows, 2 * rows) if len(by_col) == 1 else None)
                ops.append((q, (dy, dx, 0), [t], "near", last_bit(dy)))
                ops.append((q, (dy, dx, 0), [g], "col", last_bit(dx)))
            elif dy:
                whole = have[q][dy ^ last_bit(dy), dx, 0]
                ops.append((q, (dy, dx, 0), [(c, None) for c in whole], "near", last_bit(dy)))
            else:
                whole = have[q][dy, dx ^ last_bit(dx), 0]
                ops.append((q, (dy, dx, 0), [(c, None) for c in whole], "col", last_bit(dx)))
        return ops

    def half_ops(q, level):
        return [
            (q, (dy, dx, 1), [(c, None) for c in have[q][dy, dx, 0]], "half", 1)
            for dy, dx in labels
            if depth[dy, dx] == level
        ]

    def compute(q):
        pieces, at = [], {}
        for l, cells in have[q].items():
            first = len(pieces)
            pieces += [c.v for c in cells]
            at[(0,) + l] = (first, 0)
            at[(1,) + l] = (first, rows) if len(cells) == 1 else (first + 1, 0)
            at[(2,) + l] = (first, 2 * rows)
        out_at = {(dy, dx): dy * cols + dx for dy, dx in labels}
        return expert_call(where.v, pieces, weights, local, experts, rows, at, out_at, near, cols)

    class Sum:
        def __init__(self, q, keep, send):
            self.q, self.fresh = q, True
            self.cells = [Cell(keep), Cell(send)]
            self.todo = [
                [(a, s) for a in o for s in reversed(bits(near if a == "near" else cols))]
                for o in (("near", "col"), ("col", "near"))
            ]

        def begin(self):
            keep, send = (c.v for c in self.cells)
            shape = (near, cols) + keep.shape[1:]
            part = shape[2] // 2
            keep, got = keep.reshape(shape), exchange(send, "half", 1).reshape(shape)
            self.fold([keep[:, :, :part], keep[:, :, part:]], [got[:, :, :part], got[:, :, part:]])
            self.fresh = False

        def left(self):
            return len(self.todo[0])

        def fold(self, keep, got):
            self.keep, self.send = [], []
            for k, g, todo in zip(keep, got, self.todo):
                dim = 0 if todo[0][0] == "near" else 1
                (k0, k1), (g0, g1) = jnp.split(k, 2, axis=dim), jnp.split(g, 2, axis=dim)
                self.send.append(Cell(added(k1, g1)))
                self.keep.append(Cell(added(k0, g0)))

        def step(self):
            self.got = [Cell(exchange(s.v, *todo.pop(0))) for s, todo in zip(self.send, self.todo)]
            return self.got

        def refold(self):
            self.fold([c.v for c in self.keep], [c.v for c in self.got])

        def home(self):
            mine = [added(k.v, g.v)[0, 0] for k, g in zip(self.keep, self.got)]
            mine = jnp.concatenate(mine, axis=0)
            return exchange(mine, "far", self.q) if self.q else mine

    ready, sums, total = [where], [], None
    r = 0
    while r < far + depths or sums:
        if line and r:
            together(ready + line_sources(r))
            ready = ready[:1]
            line_arrive(r)
        ops = []
        for q in range(far):
            if 0 <= r - q < depths:
                ops += level_ops(q, r - q + 1)
        ops += [] if line else far_ops(r + 1)
        for q in range(far):
            if 0 <= r - q <= depths:
                ops += half_ops(q, r - q)
        if r and not line:
            together(ready + [c for o in ops for c, _ in o[2]])
        ready = ready[:1] if not r else []
        if line:
            ready += line_step(r)
        for s in list(sums):
            if not s.fresh and not s.left():
                mine = s.home().astype(jnp.float32)
                total = mine if total is None else total + mine
                sums.remove(s)
        for s in sums:
            if not s.fresh:
                s.refold()
                ready += s.step()
        for q, label, sources, axis, bit in ops:
            for c, cut in sources:
                got = Cell(exchange(c.v if cut is None else c.v[cut[0] : cut[1]], axis, bit))
                have[q].setdefault(label, []).append(got)
                if axis != "half":
                    ready.append(got)
        for s in sums:
            if s.fresh:
                s.begin()
                if 0 <= r - depths < far:
                    together(s.send + [where])
                ready += s.step()
        if 0 <= r - depths < far:
            s = Sum(r - depths, *compute(r - depths))
            sums.append(s)
            ready += s.cells
        r += 1

    grad_tokens = total[:rows].astype(jnp.bfloat16)
    by_expert = total[rows:].reshape(-1, rows)[:experts]
    grad_gates = jnp.sum(spread * by_expert.T[:, None, :], axis=2)
    return (grad_tokens, grad_gates.astype(jnp.bfloat16))


def solution(mesh):
    expert, ctx = mesh.shape["expert"], mesh.shape["ctx"]
    fine = Mesh(mesh.devices.reshape(expert // 2, 2, ctx // 2, 2), ("far", "near", "col", "half"))
    e, c = ("far", "near"), ("col", "half")
    return jax.shard_map(
        body,
        mesh=fine,
        in_specs=(P(e, c), P(e, c), P(e), P(e), P(e, c), P(e, c), P(e, c)),
        out_specs=(P(e, c), P(e)),
        check_vma=False,
    )
```

time: 407 us -> 191 us (0.47)
  blocking collectives: 123 us -> 0 us
  waiting for transfers between devices: 170 us -> 77.2 us
  matrix products: 54.1 us -> 0 us
  Pallas kernels: 0 us -> 44.1 us
  starting transfers between devices: 12.5 us -> 52.5 us
  between operations: 14 us -> 1.24 us
  local copies, waits for them, and re-layouts: 19.5 us -> 10.2 us
  other arithmetic: 10.1 us -> 5.43 us
    all_to_all x2 -> x0, blocking collectives: 116 us -> none  [the longest x1 59.1 us: body(): lax.all_to_all(sent_rows, 'expert', split_axis=0, concat_axis=0, tiled=True)]
    ppermute x0 -> x64, waiting for transfers between devices: none -> 77.2 us  [the longest x60 74.1 us: exchange(): lax.ppermute(x, axis, [(i, i ^ step) for i in range(lax.axis_size(axis))])]
    reduce_scatter x1 -> x0, waiting for transfers between devices: 65.4 us -> none  [body(): lax.psum_scatter(block_terms, 'ctx', scatter_dimension=3, tiled=True)]
    all_gather x2 -> x0, waiting for transfers between devices: 61.1 us -> none  [the longest x1 56.4 us: body(): lax.all_gather(got_grads, 'ctx', axis=2, tiled=True)]
    dot_general x7 -> x0, matrix products: 54.1 us -> none  [the longest x1 13.6 us: body(): jnp.einsum('secf,efd->secd', grad_pre_up, up_weight, preferred_element_ty...]
    ppermute x0 -> x64, starting transfers between devices: none -> 52.5 us  [the longest x60 41.9 us: exchange(): lax.ppermute(x, axis, [(i, i ^ step) for i in range(lax.axis_size(axis))])]
    pallas_call x0 -> x4, Pallas kernels: none -> 44.1 us  [expert_call(): pl.pallas_call(functools.partial(expert_kernel, (at, out_at, len(pieces),...]
    all_to_all x2 -> x0, waiting for transfers between devices: 43.4 us -> none  [the longest x1 43.4 us: body(): lax.all_to_all(back_rows, 'expert', split_axis=0, concat_axis=0, tiled=True)]
  transfers between devices with their start and end apart: 5 -> 64, of which waited for: 4 -> 24; matrix products, arithmetic and copies ran while one was open for 5% -> 2% of each run, Pallas kernels for 0% -> 23%
where the time goes in v2:
time: 191 us
  waiting for transfers between devices  77.2 us (40%)
  starting transfers between devices  52.5 us (27%)
  Pallas kernels  44.1 us (23%)
  local copies, waits for them, and re-layouts  10.2 us (5%)
  other arithmetic  5.43 us (3%)
    ppermute x60, waiting for transfers between devices, exchange(): lax.ppermute(x, axis, [(i, i ^ step) for i in range(lax.axis_size(axis))])  74.1 us
    pallas_call x4, Pallas kernels, expert_call(): pl.pallas_call(functools.partial(expert_kernel, (at, out_at, len(pieces),...  44.1 us
    ppermute x60, starting transfers between devices, exchange(): lax.ppermute(x, axis, [(i, i ^ step) for i in range(lax.axis_size(axis))])  41.9 us
    ppermute x4, starting transfers between devices, passed(): return lax.ppermute(x, axis, pairs)  10.6 us
    unnamed x28, local copies, waits for them, and re-layouts  9.17 us
  transfers between devices with their start and end apart: 64, of which 24 were waited for; matrix products, arithmetic and copies ran while one was open for 2% of the time, Pallas kernels for 23%

profile of v2, /device:TPU:8, one launch (start us, length us, event | category | flops | bytes accessed | tf_op | source)
XLA Modules:
  0.0 190.6 jit_solution(17499041433224846025)
XLA Ops:
  2.5 5.0 %collective-permute-start.1 = (bf16[272,1024]{1,0:T(8,128)(2,1)S(1)}, bf16[272,1024]{1,0:T(8,128)(2,1)S(1)}, u32[]{:S(2)}, u32[]{:S(2)}) collective-permute-start(bf16[272,1024]{1,0:T(8,128)(2,1)S(1)} %pad_maximum_fusion.refs_1_), channel_id=1, source_target_pairs={{8,16},{16,8},{9,17},{17,9},{10,18},{18,10},{11,19},{19,11},{12,20... | collective-permute-start | bytes 1671176 | tf_op jit(solution)/shard_map/ppermute | solution.py:145
  7.6 1.6 collective-permute-start.2
  9.1 1.5 collective-permute-start.3
  10.7 6.1 %collective-permute-done.refs_1_ = bf16[272,1024]{1,0:T(8,128)(2,1)S(1)} collective-permute-done((bf16[272,1024]{1,0:T(8,128)(2,1)S(1)}, bf16[272,1024]{1,0:T(8,128)(2,1)S(1)}, u32[]{:S(2)}, u32[]{:S(2)}) %collective-permute-start) | collective-permute-done | bytes 557088 | tf_op jit(solution)/shard_map/ppermute | solution.py:141
  16.9 3.0 %collective-permute-done.1 = bf16[272,1024]{1,0:T(8,128)(2,1)S(1)} collective-permute-done((bf16[272,1024]{1,0:T(8,128)(2,1)S(1)}, bf16[272,1024]{1,0:T(8,128)(2,1)S(1)}, u32[]{:S(2)}, u32[]{:S(2)}) %collective-permute-start.1) | collective-permute-done | bytes 557088 | tf_op jit(solution)/shard_map/ppermute | solution.py:145
  19.9 1.5 collective-permute-done.2.refs_2_
  22.7 2.2 %collective-permute-start.5 = (bf16[272,1024]{1,0:T(8,128)(2,1)S(1)}, bf16[272,1024]{1,0:T(8,128)(2,1)S(1)}, u32[]{:S(2)}, u32[]{:S(2)}) collective-permute-start(bf16[272,1024]{1,0:T(8,128)(2,1)S(1)} %collective-permute-done.refs_1_), channel_id=1, source_target_pairs={{8,16},{16,8},{9,17},{17,9},{10,18},{18,10},{11,19},{19,11},{12,20... | collective-permute-start | bytes 1671176 | tf_op jit(solution)/shard_map/ppermute | solution.py:145
  25.9 1.6 collective-permute-start.6
  28.0 2.1 %collective-permute-start.4 = (bf16[272,1024]{1,0:T(8,128)(2,1)}, bf16[272,1024]{1,0:T(8,128)(2,1)}, u32[]{:S(2)}, u32[]{:S(2)}) collective-permute-start(bf16[272,1024]{1,0:T(8,128)(2,1)} %copy-done.7), channel_id=1, source_target_pairs={{8,0},{16,24},{9,1},{17,25},{10,2},{18,26},{11,3},{19,27},{12,4},{... | collective-permute-start | bytes 1671176 | tf_op jit(solution)/shard_map/ppermute | solution.py:145
  30.2 5.1 %collective-permute-done.6.refs_5_ = bf16[128,1024]{1,0:T(8,128)(2,1)S(1)} collective-permute-done((bf16[128,1024]{1,0:T(8,128)(2,1)S(1)}, bf16[128,1024]{1,0:T(8,128)(2,1)S(1)}, u32[]{:S(2)}, u32[]{:S(2)}) %collective-permute-start.6) | collective-permute-done | bytes 262176 | tf_op jit(solution)/shard_map/ppermute | solution.py:141
  36.3 6.9 %collective-permute-done.7.refs_6_ = bf16[128,1024]{1,0:T(8,128)(2,1)S(1)} collective-permute-done((bf16[128,1024]{1,0:T(8,128)(2,1)S(1)}, bf16[128,1024]{1,0:T(8,128)(2,1)S(1)}, u32[]{:S(2)}, u32[]{:S(2)}) %collective-permute-start.7) | collective-permute-done | bytes 262176 | tf_op jit(solution)/shard_map/ppermute | solution.py:141
  47.0 1.5 collective-permute-start.14
  51.8 2.8 %copy-done = bf16[2,384,4096]{2,1,0:T(8,128)(2,1)S(1)} copy-done((bf16[2,384,4096]{2,1,0:T(8,128)(2,1)S(1)}, bf16[2,384,4096]{2,1,0:T(8,128)(2,1)}, u32[]{:S(2)}) %copy-start) | copy-done | bytes 6291480
  54.6 2.8 %copy-done.1 = bf16[2,384,4096]{2,1,0:T(8,128)(2,1)S(1)} copy-done((bf16[2,384,4096]{2,1,0:T(8,128)(2,1)S(1)}, bf16[2,384,4096]{2,1,0:T(8,128)(2,1)}, u32[]{:S(2)}) %copy-start.1) | copy-done | bytes 6291480
  57.4 2.8 %copy-done.2 = bf16[2,384,4096]{2,1,0:T(8,128)(2,1)S(1)} copy-done((bf16[2,384,4096]{2,1,0:T(8,128)(2,1)S(1)}, bf16[2,384,4096]{2,1,0:T(8,128)(2,1)}, u32[]{:S(2)}) %copy-start.2) | copy-done | bytes 6291480
  60.2 11.7 %shard_map.86 = (bf16[4,144,1024]{2,1,0:T(8,128)(2,1)S(1)}, bf16[4,144,1024]{2,1,0:T(8,128)(2,1)S(1)}) custom-call(s32[5]{0:T(128)S(1)} %stack.23.refs_0_, bf16[272,1024]{1,0:T(8,128)(2,1)S(1)} %pad_maximum_fusion.refs_1_, bf16[272,1024]{1,0:T(8,128)(2,1)S(1)} %collective-permute-done.2.refs_2_, bf16[272,1024]{1,0:T(8,128)(2,1)S(1)} %collective-permute-done.3.refs_3_, ...), custom_call_target="tpu_custom_call" | custom-call | flops 8053063680 | bytes 18874368 | tf_op jit(solution)/shard_map/pallas_call | solution.py:124
  73.2 2.4 %collective-permute-done.27.refs_4_ = bf16[272,1024]{1,0:T(8,128)(2,1)S(1)} collective-permute-done((bf16[272,1024]{1,0:T(8,128)(2,1)S(1)}, bf16[272,1024]{1,0:T(8,128)(2,1)S(1)}, u32[]{:S(2)}, u32[]{:S(2)}) %collective-permute-start.27) | collective-permute-done | bytes 557088 | tf_op jit(solution)/shard_map/ppermute | solution.py:141
  81.2 3.7 %collective-permute-done.21.refs_5_ = bf16[128,1024]{1,0:T(8,128)(2,1)S(1)} collective-permute-done((bf16[128,1024]{1,0:T(8,128)(2,1)S(1)}, bf16[128,1024]{1,0:T(8,128)(2,1)S(1)}, u32[]{:S(2)}, u32[]{:S(2)}) %collective-permute-start.21) | collective-permute-done | bytes 262176 | tf_op jit(solution)/shard_map/ppermute | solution.py:141
  85.6 10.8 %shard_map.87 = (bf16[4,144,1024]{2,1,0:T(8,128)(2,1)S(1)}, bf16[4,144,1024]{2,1,0:T(8,128)(2,1)S(1)}) custom-call(s32[5]{0:T(128)S(1)} %stack.23.refs_0_, bf16[272,1024]{1,0:T(8,128)(2,1)S(1)} %collective-permute-done.refs_1_, bf16[272,1024]{1,0:T(8,128)(2,1)S(1)} %collective-permute-done.8.refs_2_, bf16[272,1024]{1,0:T(8,128)(2,1)S(1)} %collective-permute-done.9.refs_3_, ...), custom_call_target="tpu_custom_call" | custom-call | flops 8053063680 | bytes 18874368 | tf_op jit(solution)/shard_map/pallas_call | solution.py:124
  96.4 1.9 collective-permute-done.22.refs_6_
  98.3 4.3 %collective-permute-done.25 = bf16[1,2,72,1024]{3,2,1,0:T(8,128)(2,1)S(1)} collective-permute-done((bf16[1,2,72,1024]{3,2,1,0:T(8,128)(2,1)S(1)}, bf16[1,2,72,1024]{3,2,1,0:T(8,128)(2,1)S(1)}, u32[]{:S(2)}, u32[]{:S(2)}) %collective-permute-start.25) | collective-permute-done | bytes 294944 | tf_op jit(solution)/shard_map/ppermute | solution.py:141
  104.9 1.7 collective-permute-done.36
  109.6 1.4 collective-permute-start.34
  111.0 3.1 %collective-permute-done.33 = bf16[1,1,72,1024]{3,2,1,0:T(8,128)(2,1)S(1)} collective-permute-done((bf16[1,1,72,1024]{3,2,1,0:T(8,128)(2,1)S(1)}, bf16[1,1,72,1024]{3,2,1,0:T(8,128)(2,1)S(1)}, u32[]{:S(2)}, u32[]{:S(2)}) %collective-permute-start.33) | collective-permute-done | bytes 147488 | tf_op jit(solution)/shard_map/ppermute | solution.py:141
  117.3 10.9 %shard_map.88 = (bf16[4,144,1024]{2,1,0:T(8,128)(2,1)S(1)}, bf16[4,144,1024]{2,1,0:T(8,128)(2,1)S(1)}) custom-call(s32[5]{0:T(128)S(1)} %stack.23.refs_0_, bf16[272,1024]{1,0:T(8,128)(2,1)S(1)} %broadcast_select_fusion.1.refs_1_, bf16[272,1024]{1,0:T(8,128)(2,1)S(1)} %collective-permute-done.13.refs_2_, ...), custom_call_target="tpu_custom_call" | custom-call | flops 8053063680 | bytes 18874368 | tf_op jit(solution)/shard_map/pallas_call | solution.py:124
  129.5 1.7 collective-permute-done.46
  136.0 10.8 %shard_map.89 = (bf16[4,144,1024]{2,1,0:T(8,128)(2,1)S(1)}, bf16[4,144,1024]{2,1,0:T(8,128)(2,1)S(1)}) custom-call(s32[5]{0:T(128)S(1)} %stack.23.refs_0_, bf16[272,1024]{1,0:T(8,128)(2,1)S(1)} %broadcast_select_fusion.refs_1_, bf16[272,1024]{1,0:T(8,128)(2,1)S(1)} %collective-permute-done.23.refs_2_, bf16[272,1024]{1,0:T(8,128)(2,1)S(1)} %collective-permute-done.24.refs_3_, ...), custom_call_target="tpu_custom_call" | custom-call | flops 8053063680 | bytes 18874368 | tf_op jit(solution)/shard_map/pallas_call | solution.py:124
  153.3 1.4 collective-permute-done.55
  154.7 5.6 %collective-permute-done.59 = bf16[2,1,72,1024]{3,2,1,0:T(8,128)(2,1)S(1)} collective-permute-done((bf16[2,1,72,1024]{3,2,1,0:T(8,128)(2,1)S(1)}, bf16[2,1,72,1024]{3,2,1,0:T(8,128)(2,1)S(1)}, u32[]{:S(2)}, u32[]{:S(2)}) %collective-permute-start.59) | collective-permute-done | bytes 294944 | tf_op jit(solution)/shard_map/ppermute | solution.py:141
  162.9 2.7 %collective-permute-done.62 = bf16[1,1,72,1024]{3,2,1,0:T(8,128)(2,1)S(1)} collective-permute-done((bf16[1,1,72,1024]{3,2,1,0:T(8,128)(2,1)S(1)}, bf16[1,1,72,1024]{3,2,1,0:T(8,128)(2,1)S(1)}, u32[]{:S(2)}, u32[]{:S(2)}) %collective-permute-start.62) | collective-permute-done | bytes 147488 | tf_op jit(solution)/shard_map/ppermute | solution.py:141
  168.3 14.6 %collective-permute-done.60 = bf16[144,1024]{1,0:T(8,128)(2,1)S(1)} collective-permute-done((bf16[144,1024]{1,0:T(8,128)(2,1)S(1)}, bf16[144,1024]{1,0:T(8,128)(2,1)S(1)}, u32[]{:S(2)}, u32[]{:S(2)}) %collective-permute-start.60) | collective-permute-done | bytes 294944 | tf_op jit(solution)/shard_map/ppermute | solution.py:141
  182.9 6.1 %collective-permute-done.63 = bf16[144,1024]{1,0:T(8,128)(2,1)S(1)} collective-permute-done((bf16[144,1024]{1,0:T(8,128)(2,1)S(1)}, bf16[144,1024]{1,0:T(8,128)(2,1)S(1)}, u32[]{:S(2)}, u32[]{:S(2)}) %collective-permute-start.63) | collective-permute-done | bytes 294944 | tf_op jit(solution)/shard_map/ppermute | solution.py:141
  (172 shorter events, 48.2 us)
Async XLA Ops:
  2.5 14.4 %collective-permute-start = (bf16[272,1024]{1,0:T(8,128)(2,1)S(1)}, bf16[272,1024]{1,0:T(8,128)(2,1)S(1)}, u32[]{:S(2)}, u32[]{:S(2)}) collective-permute-start(bf16[272,1024]{1,0:T(8,128)(2,1)S(1)} %pad_maximum_fusion.refs_1_), channel_id=1, source_target_pairs={{0,8},{8,0},{16,24},{24,16},{1,9},{9,1},{17,25},{25,17},{2,10},{10... | collective-permute-start | bytes 1671176 | tf_op jit(solution)/shard_map/ppermute | solution.py:141
  2.5 17.4 %collective-permute-start.1 = (bf16[272,1024]{1,0:T(8,128)(2,1)S(1)}, bf16[272,1024]{1,0:T(8,128)(2,1)S(1)}, u32[]{:S(2)}, u32[]{:S(2)}) collective-permute-start(bf16[272,1024]{1,0:T(8,128)(2,1)S(1)} %pad_maximum_fusion.refs_1_), channel_id=1, source_target_pairs={{8,16},{16,8},{9,17},{17,9},{10,18},{18,10},{11,19},{19,11},{12,20... | collective-permute-start | bytes 1671176 | tf_op jit(solution)/shard_map/ppermute | solution.py:145
  7.6 13.9 %collective-permute-start.2 = (bf16[272,1024]{1,0:T(8,128)(2,1)S(1)}, bf16[272,1024]{1,0:T(8,128)(2,1)S(1)}, u32[]{:S(2)}, u32[]{:S(2)}) collective-permute-start(bf16[272,1024]{1,0:T(8,128)(2,1)S(1)} %pad_maximum_fusion.refs_1_), channel_id=1, source_target_pairs={{0,2},{2,0},{1,3},{3,1},{4,6},{6,4},{5,7},{7,5},{8,10},{10,8},{9,1... | collective-permute-start | bytes 1671176 | tf_op jit(solution)/shard_map/ppermute | solution.py:141
  9.1 13.5 %collective-permute-start.3 = (bf16[272,1024]{1,0:T(8,128)(2,1)S(1)}, bf16[272,1024]{1,0:T(8,128)(2,1)S(1)}, u32[]{:S(2)}, u32[]{:S(2)}) collective-permute-start(bf16[272,1024]{1,0:T(8,128)(2,1)S(1)} %pad_maximum_fusion.refs_1_), channel_id=1, source_target_pairs={{0,4},{4,0},{1,5},{5,1},{2,6},{6,2},{3,7},{7,3},{8,12},{12,8},{9,1... | collective-permute-start | bytes 1671176 | tf_op jit(solution)/shard_map/ppermute | solution.py:141
  22.7 20.5 %collective-permute-start.5 = (bf16[272,1024]{1,0:T(8,128)(2,1)S(1)}, bf16[272,1024]{1,0:T(8,128)(2,1)S(1)}, u32[]{:S(2)}, u32[]{:S(2)}) collective-permute-start(bf16[272,1024]{1,0:T(8,128)(2,1)S(1)} %collective-permute-done.refs_1_), channel_id=1, source_target_pairs={{8,16},{16,8},{9,17},{17,9},{10,18},{18,10},{11,19},{19,11},{12,20... | collective-permute-start | bytes 1671176 | tf_op jit(solution)/shard_map/ppermute | solution.py:145
  24.9 18.8 %collective-permute-start.8 = (bf16[272,1024]{1,0:T(8,128)(2,1)S(1)}, bf16[272,1024]{1,0:T(8,128)(2,1)S(1)}, u32[]{:S(2)}, u32[]{:S(2)}) collective-permute-start(bf16[272,1024]{1,0:T(8,128)(2,1)S(1)} %collective-permute-done.refs_1_), channel_id=1, source_target_pairs={{0,2},{2,0},{1,3},{3,1},{4,6},{6,4},{5,7},{7,5},{8,10},{10,8},{9,1... | collective-permute-start | bytes 1671176 | tf_op jit(solution)/shard_map/ppermute | solution.py:141
  27.5 16.9 %collective-permute-start.9 = (bf16[272,1024]{1,0:T(8,128)(2,1)S(1)}, bf16[272,1024]{1,0:T(8,128)(2,1)S(1)}, u32[]{:S(2)}, u32[]{:S(2)}) collective-permute-start(bf16[272,1024]{1,0:T(8,128)(2,1)S(1)} %collective-permute-done.refs_1_), channel_id=1, source_target_pairs={{0,4},{4,0},{1,5},{5,1},{2,6},{6,2},{3,7},{7,3},{8,12},{12,8},{9,1... | collective-permute-start | bytes 1671176 | tf_op jit(solution)/shard_map/ppermute | solution.py:141
  28.0 16.4 %collective-permute-start.4 = (bf16[272,1024]{1,0:T(8,128)(2,1)}, bf16[272,1024]{1,0:T(8,128)(2,1)}, u32[]{:S(2)}, u32[]{:S(2)}) collective-permute-start(bf16[272,1024]{1,0:T(8,128)(2,1)} %copy-done.7), channel_id=1, source_target_pairs={{8,0},{16,24},{9,1},{17,25},{10,2},{18,26},{11,3},{19,27},{12,4},{... | collective-permute-start | bytes 1671176 | tf_op jit(solution)/shard_map/ppermute | solution.py:145
  45.6 26.3 %collective-permute-start.13 = (bf16[272,1024]{1,0:T(8,128)(2,1)S(1)}, bf16[272,1024]{1,0:T(8,128)(2,1)S(1)}, u32[]{:S(2)}, u32[]{:S(2)}) collective-permute-start(bf16[272,1024]{1,0:T(8,128)(2,1)S(1)} %broadcast_select_fusion.1.refs_1_), channel_id=1, source_target_pairs={{0,2},{2,0},{1,3},{3,1},{4,6},{6,4},{5,7},{7,5},{8,10},{10,8},{9,1... | collective-permute-start | bytes 1671176 | tf_op jit(solution)/shard_map/ppermute | solution.py:141
  47.0 24.9 %collective-permute-start.14 = (bf16[272,1024]{1,0:T(8,128)(2,1)S(1)}, bf16[272,1024]{1,0:T(8,128)(2,1)S(1)}, u32[]{:S(2)}, u32[]{:S(2)}) collective-permute-start(bf16[272,1024]{1,0:T(8,128)(2,1)S(1)} %broadcast_select_fusion.1.refs_1_), channel_id=1, source_target_pairs={{0,4},{4,0},{1,5},{5,1},{2,6},{6,2},{3,7},{7,3},{8,12},{12,8},{9,1... | collective-permute-start | bytes 1671176 | tf_op jit(solution)/shard_map/ppermute | solution.py:141
  48.5 23.4 %collective-permute-start.10 = (bf16[272,1024]{1,0:T(8,128)(2,1)S(1)}, bf16[272,1024]{1,0:T(8,128)(2,1)S(1)}, u32[]{:S(2)}, u32[]{:S(2)}) collective-permute-start(bf16[272,1024]{1,0:T(8,128)(2,1)S(1)} %copy-done.10), channel_id=1, source_target_pairs={{8,0},{16,24},{9,1},{17,25},{10,2},{18,26},{11,3},{19,27},{12,4},{... | collective-permute-start | bytes 1671176 | tf_op jit(solution)/shard_map/ppermute | solution.py:145
  49.8 22.0 %collective-permute-start.11 = (bf16[128,1024]{1,0:T(8,128)(2,1)S(1)}, bf16[128,1024]{1,0:T(8,128)(2,1)S(1)}, u32[]{:S(2)}, u32[]{:S(2)}) collective-permute-start(bf16[128,1024]{1,0:T(8,128)(2,1)S(1)} %slice.86), channel_id=1, source_target_pairs={{0,4},{4,0},{1,5},{5,1},{2,6},{6,2},{3,7},{7,3},{8,12},{12,8},{9,1... | collective-permute-start | bytes 786440 | tf_op jit(solution)/shard_map/ppermute | solution.py:141
  50.5 21.4 %collective-permute-start.12 = (bf16[128,1024]{1,0:T(8,128)(2,1)S(1)}, bf16[128,1024]{1,0:T(8,128)(2,1)S(1)}, u32[]{:S(2)}, u32[]{:S(2)}) collective-permute-start(bf16[128,1024]{1,0:T(8,128)(2,1)S(1)} %slice.87), channel_id=1, source_target_pairs={{0,2},{2,0},{1,3},{3,1},{4,6},{6,4},{5,7},{7,5},{8,10},{10,8},{9,1... | collective-permute-start | bytes 786440 | tf_op jit(solution)/shard_map/ppermute | solution.py:141
  77.1 21.2 %collective-permute-start.23 = (bf16[272,1024]{1,0:T(8,128)(2,1)S(1)}, bf16[272,1024]{1,0:T(8,128)(2,1)S(1)}, u32[]{:S(2)}, u32[]{:S(2)}) collective-permute-start(bf16[272,1024]{1,0:T(8,128)(2,1)S(1)} %broadcast_select_fusion.refs_1_), channel_id=1, source_target_pairs={{0,2},{2,0},{1,3},{3,1},{4,6},{6,4},{5,7},{7,5},{8,10},{10,8},{9,1... | collective-permute-start | bytes 1671176 | tf_op jit(solution)/shard_map/ppermute | solution.py:141
  78.5 19.8 %collective-permute-start.24 = (bf16[272,1024]{1,0:T(8,128)(2,1)S(1)}, bf16[272,1024]{1,0:T(8,128)(2,1)S(1)}, u32[]{:S(2)}, u32[]{:S(2)}) collective-permute-start(bf16[272,1024]{1,0:T(8,128)(2,1)S(1)} %broadcast_select_fusion.refs_1_), channel_id=1, source_target_pairs={{0,4},{4,0},{1,5},{5,1},{2,6},{6,2},{3,7},{7,3},{8,12},{12,8},{9,1... | collective-permute-start | bytes 1671176 | tf_op jit(solution)/shard_map/ppermute | solution.py:141
  79.1 19.2 %collective-permute-start.22 = (bf16[128,1024]{1,0:T(8,128)(2,1)S(1)}, bf16[128,1024]{1,0:T(8,128)(2,1)S(1)}, u32[]{:S(2)}, u32[]{:S(2)}) collective-permute-start(bf16[128,1024]{1,0:T(8,128)(2,1)S(1)} %slice.89), channel_id=1, source_target_pairs={{0,2},{2,0},{1,3},{3,1},{4,6},{6,4},{5,7},{7,5},{8,10},{10,8},{9,1... | collective-permute-start | bytes 786440 | tf_op jit(solution)/shard_map/ppermute | solution.py:141
  80.4 22.2 %collective-permute-start.25 = (bf16[1,2,72,1024]{3,2,1,0:T(8,128)(2,1)S(1)}, bf16[1,2,72,1024]{3,2,1,0:T(8,128)(2,1)S(1)}, u32[]{:S(2)}, u32[]{:S(2)}) collective-permute-start(bf16[1,2,72,1024]{3,2,1,0:T(8,128)(2,1)S(1)} %get-tuple-element.83), channel_id=1, source_target_pairs={{0,4},{4,0},{1,5},{5,1},{2,6},{6,2},{3,7},{7,3},{8,12},{12,8},{9,1... | collective-permute-start | bytes 884744 | tf_op jit(solution)/shard_map/ppermute | solution.py:141
  84.9 18.8 %collective-permute-start.26 = (bf16[2,1,72,1024]{3,2,1,0:T(8,128)(2,1)S(1)}, bf16[2,1,72,1024]{3,2,1,0:T(8,128)(2,1)S(1)}, u32[]{:S(2)}, u32[]{:S(2)}) collective-permute-start(bf16[2,1,72,1024]{3,2,1,0:T(8,128)(2,1)S(1)} %get-tuple-element.84), channel_id=1, source_target_pairs={{0,2},{2,0},{1,3},{3,1},{4,6},{6,4},{5,7},{7,5},{8,10},{10,8},{9,1... | collective-permute-start | bytes 884744 | tf_op jit(solution)/shard_map/ppermute | solution.py:141
  104.7 10.6 %collective-permute-start.42 = (bf16[128,1024]{1,0:T(8,128)(2,1)S(1)}, bf16[128,1024]{1,0:T(8,128)(2,1)S(1)}, u32[]{:S(2)}, u32[]{:S(2)}) collective-permute-start(bf16[128,1024]{1,0:T(8,128)(2,1)S(1)} %collective-permute-done.21.refs_5_), channel_id=1, source_target_pairs={{0,1},{1,0},{2,3},{3,2},{4,5},{5,4},{6,7},{7,6},{8,9},{9,8},{10,11... | collective-permute-start | bytes 786440 | tf_op jit(solution)/shard_map/ppermute | solution.py:141
  108.8 19.4 %collective-permute-start.32 = (bf16[1,1,72,1024]{3,2,1,0:T(8,128)(2,1)S(1)}, bf16[1,1,72,1024]{3,2,1,0:T(8,128)(2,1)S(1)}, u32[]{:S(2)}, u32[]{:S(2)}) collective-permute-start(bf16[1,1,72,1024]{3,2,1,0:T(8,128)(2,1)S(1)} %add_convert_fusion.38), channel_id=1, source_target_pairs={{0,2},{2,0},{1,3},{3,1},{4,6},{6,4},{5,7},{7,5},{8,10},{10,8},{9,1... | collective-permute-start | bytes 442376 | tf_op jit(solution)/shard_map/ppermute | solution.py:141
  109.6 18.6 %collective-permute-start.34 = (bf16[128,1024]{1,0:T(8,128)(2,1)S(1)}, bf16[128,1024]{1,0:T(8,128)(2,1)S(1)}, u32[]{:S(2)}, u32[]{:S(2)}) collective-permute-start(bf16[128,1024]{1,0:T(8,128)(2,1)S(1)} %slice.90), channel_id=1, source_target_pairs={{0,4},{4,0},{1,5},{5,1},{2,6},{6,2},{3,7},{7,3},{8,12},{12,8},{9,1... | collective-permute-start | bytes 786440 | tf_op jit(solution)/shard_map/ppermute | solution.py:141
  114.1 14.2 %collective-permute-start.35 = (bf16[128,1024]{1,0:T(8,128)(2,1)S(1)}, bf16[128,1024]{1,0:T(8,128)(2,1)S(1)}, u32[]{:S(2)}, u32[]{:S(2)}) collective-permute-start(bf16[128,1024]{1,0:T(8,128)(2,1)S(1)} %slice.91), channel_id=1, source_target_pairs={{0,2},{2,0},{1,3},{3,1},{4,6},{6,4},{5,7},{7,5},{8,10},{10,8},{9,1... | collective-permute-start | bytes 786440 | tf_op jit(solution)/shard_map/ppermute | solution.py:141
  115.4 12.9 %collective-permute-start.37 = (bf16[1,2,72,1024]{3,2,1,0:T(8,128)(2,1)S(1)}, bf16[1,2,72,1024]{3,2,1,0:T(8,128)(2,1)S(1)}, u32[]{:S(2)}, u32[]{:S(2)}) collective-permute-start(bf16[1,2,72,1024]{3,2,1,0:T(8,128)(2,1)S(1)} %get-tuple-element.96), channel_id=1, source_target_pairs={{0,4},{4,0},{1,5},{5,1},{2,6},{6,2},{3,7},{7,3},{8,12},{12,8},{9,1... | collective-permute-start | bytes 884744 | tf_op jit(solution)/shard_map/ppermute | solution.py:141
  116.0 12.3 %collective-permute-start.38 = (bf16[2,1,72,1024]{3,2,1,0:T(8,128)(2,1)S(1)}, bf16[2,1,72,1024]{3,2,1,0:T(8,128)(2,1)S(1)}, u32[]{:S(2)}, u32[]{:S(2)}) collective-permute-start(bf16[2,1,72,1024]{3,2,1,0:T(8,128)(2,1)S(1)} %get-tuple-element.97), channel_id=1, source_target_pairs={{0,2},{2,0},{1,3},{3,1},{4,6},{6,4},{5,7},{7,5},{8,10},{10,8},{9,1... | collective-permute-start | bytes 884744 | tf_op jit(solution)/shard_map/ppermute | solution.py:141
  131.9 14.8 %collective-permute-start.45 = (bf16[1,1,72,1024]{3,2,1,0:T(8,128)(2,1)S(1)}, bf16[1,1,72,1024]{3,2,1,0:T(8,128)(2,1)S(1)}, u32[]{:S(2)}, u32[]{:S(2)}) collective-permute-start(bf16[1,1,72,1024]{3,2,1,0:T(8,128)(2,1)S(1)} %add_convert_fusion.31), channel_id=1, source_target_pairs={{0,4},{4,0},{1,5},{5,1},{2,6},{6,2},{3,7},{7,3},{8,12},{12,8},{9,1... | collective-permute-start | bytes 442376 | tf_op jit(solution)/shard_map/ppermute | solution.py:141
  132.8 14.0 %collective-permute-start.44 = (bf16[1,1,72,1024]{3,2,1,0:T(8,128)(2,1)S(1)}, bf16[1,1,72,1024]{3,2,1,0:T(8,128)(2,1)S(1)}, u32[]{:S(2)}, u32[]{:S(2)}) collective-permute-start(bf16[1,1,72,1024]{3,2,1,0:T(8,128)(2,1)S(1)} %add_convert_fusion.32), channel_id=1, source_target_pairs={{0,2},{2,0},{1,3},{3,1},{4,6},{6,4},{5,7},{7,5},{8,10},{10,8},{9,1... | collective-permute-start | bytes 442376 | tf_op jit(solution)/shard_map/ppermute | solution.py:141
  134.1 12.7 %collective-permute-start.47 = (bf16[1,2,72,1024]{3,2,1,0:T(8,128)(2,1)S(1)}, bf16[1,2,72,1024]{3,2,1,0:T(8,128)(2,1)S(1)}, u32[]{:S(2)}, u32[]{:S(2)}) collective-permute-start(bf16[1,2,72,1024]{3,2,1,0:T(8,128)(2,1)S(1)} %get-tuple-element.109), channel_id=1, source_target_pairs={{0,4},{4,0},{1,5},{5,1},{2,6},{6,2},{3,7},{7,3},{8,12},{12,8},{9,1... | collective-permute-start | bytes 884744 | tf_op jit(solution)/shard_map/ppermute | solution.py:141
  134.9 11.9 %collective-permute-start.48 = (bf16[2,1,72,1024]{3,2,1,0:T(8,128)(2,1)S(1)}, bf16[2,1,72,1024]{3,2,1,0:T(8,128)(2,1)S(1)}, u32[]{:S(2)}, u32[]{:S(2)}) collective-permute-start(bf16[2,1,72,1024]{3,2,1,0:T(8,128)(2,1)S(1)} %get-tuple-element.110), channel_id=1, source_target_pairs={{0,2},{2,0},{1,3},{3,1},{4,6},{6,4},{5,7},{7,5},{8,10},{10,8},{9,1... | collective-permute-start | bytes 884744 | tf_op jit(solution)/shard_map/ppermute | solution.py:141
  150.2 10.1 %collective-permute-start.59 = (bf16[2,1,72,1024]{3,2,1,0:T(8,128)(2,1)S(1)}, bf16[2,1,72,1024]{3,2,1,0:T(8,128)(2,1)S(1)}, u32[]{:S(2)}, u32[]{:S(2)}) collective-permute-start(bf16[2,1,72,1024]{3,2,1,0:T(8,128)(2,1)S(1)} %get-tuple-element.129), channel_id=1, source_target_pairs={{0,2},{2,0},{1,3},{3,1},{4,6},{6,4},{5,7},{7,5},{8,10},{10,8},{9,1... | collective-permute-start | bytes 884744 | tf_op jit(solution)/shard_map/ppermute | solution.py:141
  152.6 15.7 %collective-permute-start.54 = (bf16[144,1024]{1,0:T(8,128)(2,1)S(1)}, bf16[144,1024]{1,0:T(8,128)(2,1)S(1)}, u32[]{:S(2)}, u32[]{:S(2)}) collective-permute-start(bf16[144,1024]{1,0:T(8,128)(2,1)S(1)} %pad_maximum_fusion.1), channel_id=1, source_target_pairs={{0,8},{8,0},{16,24},{24,16},{1,9},{9,1},{17,25},{25,17},{2,10},{10... | collective-permute-start | bytes 884744 | tf_op jit(solution)/shard_map/ppermute | solution.py:141
  162.8 20.2 %collective-permute-start.60 = (bf16[144,1024]{1,0:T(8,128)(2,1)S(1)}, bf16[144,1024]{1,0:T(8,128)(2,1)S(1)}, u32[]{:S(2)}, u32[]{:S(2)}) collective-permute-start(bf16[144,1024]{1,0:T(8,128)(2,1)S(1)} %pad_maximum_fusion.2), channel_id=1, source_target_pairs={{0,16},{8,24},{16,0},{24,8},{1,17},{9,25},{17,1},{25,9},{2,18},{10... | collective-permute-start | bytes 884744 | tf_op jit(solution)/shard_map/ppermute | solution.py:141
  167.0 22.1 %collective-permute-start.63 = (bf16[144,1024]{1,0:T(8,128)(2,1)S(1)}, bf16[144,1024]{1,0:T(8,128)(2,1)S(1)}, u32[]{:S(2)}, u32[]{:S(2)}) collective-permute-start(bf16[144,1024]{1,0:T(8,128)(2,1)S(1)} %pad_maximum_fusion.3), channel_id=1, source_target_pairs={{0,24},{8,16},{16,8},{24,0},{1,25},{9,17},{17,9},{25,1},{2,26},{10... | collective-permute-start | bytes 884744 | tf_op jit(solution)/shard_map/ppermute | solution.py:141
  (46 other events, 296.3 us)

commit v3 on v2

--- a/solution.py
+++ b/solution.py
@@ -169,6 +169,38 @@
             c.v = v
 
 
+def exchange(x, axis, step):
+    return lax.ppermute(x, axis, [(i, i ^ step) for i in range(lax.axis_size(axis))])
+
+
+def passed(x, axis, pairs):
+    return lax.ppermute(x, axis, pairs)
+
+
+def bits(size):
+    return [1 << b for b in range(size.bit_length() - 1)]
+
+
+def last_bit(v):
+    return 1 << (v.bit_length() - 1)
+
+
+def added(a, b):
+    return (a.astype(jnp.float32) + b.astype(jnp.float32)).astype(jnp.bfloat16)
+
+
+class Cell:
+    def __init__(self, value):
+        self.v = value
+
+
+def together(cells):
+    cells = list({id(c): c for c in cells}.values())
+    if len(cells) > 1:
+        for c, v in zip(cells, lax.optimization_barrier([c.v for c in cells])):
+            c.v = v
+
+
 def touch_kernel(where, *refs):
     for i in range(where.shape[0]):
         refs[-1][i] = where[i]
@@ -252,7 +284,10 @@
         for dy, dx in labels:
             if depth[dy, dx] != level:
                 continue
-            if dy and dx:
+            if dy and dx and q % 2:
+                whole = have[q][dy, dx ^ last_bit(dx), 0]
+                ops.append((q, (dy, dx, 0), [(c, None) for c in whole], "col", last_bit(dx)))
+            elif dy and dx:
                 by_near, by_col = have[q][dy ^ last_bit(dy), dx, 0], have[q][dy, dx ^ last_bit(dx), 0]
                 t = (by_near[0], (0, rows) if len(by_near) == 1 else None)
                 g = (by_col[-1], (rows, 2 * rows) if len(by_col) == 1 else None)
@@ -282,24 +317,28 @@
             at[(1,) + l] = (first, rows) if len(cells) == 1 else (first + 1, 0)
             at[(2,) + l] = (first, 2 * rows)
         out_at = {(dy, dx): dy * cols + dx for dy, dx in labels}
-        return expert_call(where.v, pieces, weights, local, experts, rows, at, out_at, near, cols)
+        return expert_call(where, pieces, weights, local, experts, rows, at, out_at, near, cols)
 
     class Sum:
         def __init__(self, q, keep, send):
-            self.q, self.fresh = q, True
+            self.q, self.half, self.todo, self.mine = q, None, None, None
             self.cells = [Cell(keep), Cell(send)]
+            self.urgent = q > 0
+            self.orders = [("near", "col"), ("col", "near")][: 2 if self.urgent else 1]
+
+        def begin(self):
+            self.half = Cell(exchange(self.cells[1].v, "half", 1))
+
+        def first(self):
+            keep = self.cells[0].v
+            shape = (near, cols) + keep.shape[1:]
+            part = shape[2] // len(self.orders)
+            keep, got = keep.reshape(shape), self.half.v.reshape(shape)
+            cut = lambda x: [x[:, :, i * part : (i + 1) * part] for i in range(len(self.orders))]
             self.todo = [
-                [(a, s) for a in o for s in reversed(bits(near if a == "near" else cols))]
-                for o in (("near", "col"), ("col", "near"))
+                [(a, s) for a in o for s in reversed(bits(near if a == "near" else cols))] for o in self.orders
             ]
-
-        def begin(self):
-            keep, send = (c.v for c in self.cells)
-            shape = (near, cols) + keep.shape[1:]
-            part = shape[2] // 2
-            keep, got = keep.reshape(shape), exchange(send, "half", 1).reshape(shape)
-            self.fold([keep[:, :, :part], keep[:, :, part:]], [got[:, :, :part], got[:, :, part:]])
-            self.fresh = False
+            self.fold(cut(keep), cut(got))
 
         def left(self):
             return len(self.todo[0])
@@ -319,17 +358,20 @@
         def refold(self):
             self.fold([c.v for c in self.keep], [c.v for c in self.got])
 
+        def finish(self):
+            mine = [added(k.v, g.v)[0, 0] for k, g in zip(self.keep, self.got)]
+            self.mine = Cell(mine[0] if len(mine) == 1 else jnp.concatenate(mine, axis=0))
+
         def home(self):
-            mine = [added(k.v, g.v)[0, 0] for k, g in zip(self.keep, self.got)]
-            mine = jnp.concatenate(mine, axis=0)
-            return exchange(mine, "far", self.q) if self.q else mine
-
-    ready, sums, total = [where], [], None
+            homes.append(Cell(exchange(self.mine.v, "far", self.q) if self.q else self.mine.v))
+            sums.remove(self)
+
+    where = where.v
+    ready, sums, homes, held_back = [], [], [], []
     r = 0
     while r < far + depths or sums:
         if line and r:
             together(ready + line_sources(r))
-            ready = ready[:1]
             line_arrive(r)
         ops = []
         for q in range(far):
@@ -341,35 +383,48 @@
                 ops += half_ops(q, r - q)
         if r and not line:
             together(ready + [c for o in ops for c, _ in o[2]])
-        ready = ready[:1] if not r else []
-        if line:
-            ready += line_step(r)
+        ready = line_step(r) if line else []
+        working = r - depths if 0 <= r - depths < far else None
+        begun = []
         for s in list(sums):
-            if not s.fresh and not s.left():
-                mine = s.home().astype(jnp.float32)
-                total = mine if total is None else total + mine
-                sums.remove(s)
-        for s in sums:
-            if not s.fresh:
+            if s.half is None:
+                s.begin()
+                if s.urgent:
+                    s.first()
+                    begun.append(s)
+                else:
+                    ready.append(s.half)
+            elif s.todo is None:
+                s.first()
+                ready += s.step()
+            elif s.left():
                 s.refold()
                 ready += s.step()
+            elif s.mine is None:
+                s.finish()
+                s.home()
         for q, label, sources, axis, bit in ops:
             for c, cut in sources:
                 got = Cell(exchange(c.v if cut is None else c.v[cut[0] : cut[1]], axis, bit))
                 have[q].setdefault(label, []).append(got)
                 if axis != "half":
                     ready.append(got)
-        for s in sums:
-            if s.fresh:
-                s.begin()
-                if 0 <= r - depths < far:
-                    together(s.send + [where])
-                ready += s.step()
-        if 0 <= r - depths < far:
-            s = Sum(r - depths, *compute(r - depths))
+        if begun and working is not None:
+            together([c for s in begun for c in s.send] + have[working][0, 0, 0])
+        for s in begun:
+            ready += s.step()
+        ready, held_back = ready + held_back, []
+        if begun and working is None:
+            for s in [s for s in sums if s.q == far - 2 and not s.left()]:
+                s.finish()
+                s.home()
+                held_back.append(homes[-1])
+        if working is not None:
+            s = Sum(working, *compute(working))
             sums.append(s)
             ready += s.cells
         r += 1
+    total = sum(h.v.astype(jnp.float32) for h in homes)
 
     grad_tokens = total[:rows].astype(jnp.bfloat16)
     by_expert = total[rows:].reshape(-1, rows)[:experts]

time: 191 us -> 185 us (0.969); the launches traced: 191 us -> 182 us
  waiting for transfers between devices: 77.2 us -> 71.6 us
  starting transfers between devices: 52.5 us -> 48.1 us
  other arithmetic: 5.43 us -> 7.58 us
    ppermute x60 -> x54, waiting for transfers between devices: 74.1 us -> 68.4 us  [exchange(): lax.ppermute(x, axis, [(i, i ^ step) for i in range(lax.axis_size(axis))])]
    ppermute x60 -> x54, starting transfers between devices: 41.9 us -> 37.5 us  [exchange(): lax.ppermute(x, axis, [(i, i ^ step) for i in range(lax.axis_size(axis))])]
    unnamed x28 -> x24, local copies, waits for them, and re-layouts: 9.17 us -> 8.69 us
  transfers between devices with their start and end apart: 64 -> 58, of which waited for: 24 -> 24; matrix products, arithmetic and copies ran while one was open for 2% -> 3% of each run, Pallas kernels for 23% -> 24%
where the time goes in v3:
time: 185 us; the launch traced here: 182 us
  waiting for transfers between devices  71.6 us (39%)
  starting transfers between devices  48.1 us (26%)
  Pallas kernels  44.2 us (24%)
  local copies, waits for them, and re-layouts  9.6 us (5%)
  other arithmetic  7.58 us (4%)
    ppermute x54, waiting for transfers between devices, exchange(): lax.ppermute(x, axis, [(i, i ^ step) for i in range(lax.axis_size(axis))])  68.4 us
    pallas_call x4, Pallas kernels, expert_call(): pl.pallas_call(functools.partial(expert_kernel, (at, out_at, len(pieces),...  44.2 us
    ppermute x54, starting transfers between devices, exchange(): lax.ppermute(x, axis, [(i, i ^ step) for i in range(lax.axis_size(axis))])  37.5 us
    ppermute x4, starting transfers between devices, passed(): return lax.ppermute(x, axis, pairs)  10.6 us
    unnamed x24, local copies, waits for them, and re-layouts  8.69 us
  transfers between devices with their start and end apart: 58, of which 24 were waited for; matrix products, arithmetic and copies ran while one was open for 3% of the time, Pallas kernels for 24%

profile of v3, /device:TPU:8, one launch (start us, length us, event | category | flops | bytes accessed | tf_op | source)
XLA Modules:
  0.0 182.2 jit_solution(15522706153993087219)
XLA Ops:
  2.5 5.0 %collective-permute-start.1 = (bf16[272,1024]{1,0:T(8,128)(2,1)S(1)}, bf16[272,1024]{1,0:T(8,128)(2,1)}, u32[]{:S(2)}, u32[]{:S(2)}) collective-permute-start(bf16[272,1024]{1,0:T(8,128)(2,1)S(1)} %pad_maximum_fusion.refs_1_), channel_id=1, source_target_pairs={{8,16},{16,8},{9,17},{17,9},{10,18},{18,10},{11,19},{19,11},{12,20... | collective-permute-start | bytes 1671176 | tf_op jit(solution)/shard_map/ppermute | solution.py:177
  7.6 1.6 collective-permute-start.2
  9.1 1.5 collective-permute-start.3
  10.6 6.2 %collective-permute-done.refs_1_ = bf16[272,1024]{1,0:T(8,128)(2,1)S(1)} collective-permute-done((bf16[272,1024]{1,0:T(8,128)(2,1)S(1)}, bf16[272,1024]{1,0:T(8,128)(2,1)S(1)}, u32[]{:S(2)}, u32[]{:S(2)}) %collective-permute-start) | collective-permute-done | bytes 557088 | tf_op jit(solution)/shard_map/ppermute | solution.py:173
  16.9 3.1 %collective-permute-done.1 = bf16[272,1024]{1,0:T(8,128)(2,1)} collective-permute-done((bf16[272,1024]{1,0:T(8,128)(2,1)S(1)}, bf16[272,1024]{1,0:T(8,128)(2,1)}, u32[]{:S(2)}, u32[]{:S(2)}) %collective-permute-start.1) | collective-permute-done | bytes 557088 | tf_op jit(solution)/shard_map/ppermute | solution.py:177
  20.0 1.4 collective-permute-done.2.refs_2_
  22.7 2.2 %collective-permute-start.5 = (bf16[272,1024]{1,0:T(8,128)(2,1)S(1)}, bf16[272,1024]{1,0:T(8,128)(2,1)S(1)}, u32[]{:S(2)}, u32[]{:S(2)}) collective-permute-start(bf16[272,1024]{1,0:T(8,128)(2,1)S(1)} %collective-permute-done.refs_1_), channel_id=1, source_target_pairs={{8,16},{16,8},{9,17},{17,9},{10,18},{18,10},{11,19},{19,11},{12,20... | collective-permute-start | bytes 1671176 | tf_op jit(solution)/shard_map/ppermute | solution.py:177
  25.5 1.6 collective-permute-start.6
  27.6 2.1 %collective-permute-start.4 = (bf16[272,1024]{1,0:T(8,128)(2,1)}, bf16[272,1024]{1,0:T(8,128)(2,1)}, u32[]{:S(2)}, u32[]{:S(2)}) collective-permute-start(bf16[272,1024]{1,0:T(8,128)(2,1)} %collective-permute-done.1), channel_id=1, source_target_pairs={{8,0},{16,24},{9,1},{17,25},{10,2},{18,26},{11,3},{19,27},{12,4},{... | collective-permute-start | bytes 1671176 | tf_op jit(solution)/shard_map/ppermute | solution.py:177
  29.7 5.1 %collective-permute-done.6.refs_5_ = bf16[128,1024]{1,0:T(8,128)(2,1)S(1)} collective-permute-done((bf16[128,1024]{1,0:T(8,128)(2,1)S(1)}, bf16[128,1024]{1,0:T(8,128)(2,1)S(1)}, u32[]{:S(2)}, u32[]{:S(2)}) %collective-permute-start.6) | collective-permute-done | bytes 262176 | tf_op jit(solution)/shard_map/ppermute | solution.py:173
  34.8 1.5 collective-permute-start.7
  36.3 7.0 %collective-permute-done.7.refs_6_ = bf16[128,1024]{1,0:T(8,128)(2,1)S(1)} collective-permute-done((bf16[128,1024]{1,0:T(8,128)(2,1)S(1)}, bf16[128,1024]{1,0:T(8,128)(2,1)S(1)}, u32[]{:S(2)}, u32[]{:S(2)}) %collective-permute-start.7) | collective-permute-done | bytes 262176 | tf_op jit(solution)/shard_map/ppermute | solution.py:173
  47.7 1.5 collective-permute-start.13
  51.4 2.8 %copy-done = bf16[2,384,4096]{2,1,0:T(8,128)(2,1)S(1)} copy-done((bf16[2,384,4096]{2,1,0:T(8,128)(2,1)S(1)}, bf16[2,384,4096]{2,1,0:T(8,128)(2,1)}, u32[]{:S(2)}) %copy-start) | copy-done | bytes 6291480
  54.2 2.8 %copy-done.1 = bf16[2,384,4096]{2,1,0:T(8,128)(2,1)S(1)} copy-done((bf16[2,384,4096]{2,1,0:T(8,128)(2,1)S(1)}, bf16[2,384,4096]{2,1,0:T(8,128)(2,1)}, u32[]{:S(2)}) %copy-start.1) | copy-done | bytes 6291480
  57.0 2.8 %copy-done.2 = bf16[2,384,4096]{2,1,0:T(8,128)(2,1)S(1)} copy-done((bf16[2,384,4096]{2,1,0:T(8,128)(2,1)S(1)}, bf16[2,384,4096]{2,1,0:T(8,128)(2,1)}, u32[]{:S(2)}) %copy-start.2) | copy-done | bytes 6291480
  59.8 11.7 %shard_map.86 = (bf16[4,144,1024]{2,1,0:T(8,128)(2,1)S(1)}, bf16[4,144,1024]{2,1,0:T(8,128)(2,1)S(1)}) custom-call(s32[5]{0:T(128)S(1)} %stack.23.refs_0_, bf16[272,1024]{1,0:T(8,128)(2,1)S(1)} %pad_maximum_fusion.refs_1_, bf16[272,1024]{1,0:T(8,128)(2,1)S(1)} %collective-permute-done.2.refs_2_, bf16[272,1024]{1,0:T(8,128)(2,1)S(1)} %collective-permute-done.3.refs_3_, ...), custom_call_target="tpu_custom_call" | custom-call | flops 8053063680 | bytes 18874368 | tf_op jit(solution)/shard_map/pallas_call | solution.py:124
  75.7 1.5 collective-permute-start.23
  79.0 10.8 %shard_map.87 = (bf16[4,144,1024]{2,1,0:T(8,128)(2,1)S(1)}, bf16[4,144,1024]{2,1,0:T(8,128)(2,1)S(1)}) custom-call(s32[5]{0:T(128)S(1)} %stack.23.refs_0_, bf16[272,1024]{1,0:T(8,128)(2,1)S(1)} %collective-permute-done.refs_1_, bf16[272,1024]{1,0:T(8,128)(2,1)S(1)} %collective-permute-done.8.refs_2_, bf16[272,1024]{1,0:T(8,128)(2,1)S(1)} %collective-permute-done.9.refs_3_, ...), custom_call_target="tpu_custom_call" | custom-call | flops 8053063680 | bytes 18874368 | tf_op jit(solution)/shard_map/pallas_call | solution.py:124
  89.9 5.7 %collective-permute-done.20.refs_5_ = bf16[128,1024]{1,0:T(8,128)(2,1)S(1)} collective-permute-done((bf16[128,1024]{1,0:T(8,128)(2,1)S(1)}, bf16[128,1024]{1,0:T(8,128)(2,1)S(1)}, u32[]{:S(2)}, u32[]{:S(2)}) %collective-permute-start.20) | collective-permute-done | bytes 262176 | tf_op jit(solution)/shard_map/ppermute | solution.py:173
  99.3 1.5 collective-permute-start.28
  103.7 10.9 %shard_map.88 = (bf16[4,144,1024]{2,1,0:T(8,128)(2,1)S(1)}, bf16[4,144,1024]{2,1,0:T(8,128)(2,1)S(1)}) custom-call(s32[5]{0:T(128)S(1)} %stack.23.refs_0_, bf16[272,1024]{1,0:T(8,128)(2,1)S(1)} %broadcast_select_fusion.1.refs_1_, bf16[272,1024]{1,0:T(8,128)(2,1)S(1)} %collective-permute-done.12.refs_2_, ...), custom_call_target="tpu_custom_call" | custom-call | flops 8053063680 | bytes 18874368 | tf_op jit(solution)/shard_map/pallas_call | solution.py:124
  114.7 1.7 collective-permute-done.29.refs_5_
  116.4 4.7 %collective-permute-done.31 = bf16[1,2,72,1024]{3,2,1,0:T(8,128)(2,1)S(1)} collective-permute-done((bf16[1,2,72,1024]{3,2,1,0:T(8,128)(2,1)S(1)}, bf16[1,2,72,1024]{3,2,1,0:T(8,128)(2,1)S(1)}, u32[]{:S(2)}, u32[]{:S(2)}) %collective-permute-start.31) | collective-permute-done | bytes 294944 | tf_op jit(solution)/shard_map/ppermute | solution.py:173
  122.8 1.6 collective-permute-done.41
  130.3 10.8 %shard_map.89 = (bf16[4,144,1024]{2,1,0:T(8,128)(2,1)S(1)}, bf16[4,144,1024]{2,1,0:T(8,128)(2,1)S(1)}) custom-call(s32[5]{0:T(128)S(1)} %stack.23.refs_0_, bf16[272,1024]{1,0:T(8,128)(2,1)S(1)} %broadcast_select_fusion.refs_1_, bf16[272,1024]{1,0:T(8,128)(2,1)S(1)} %collective-permute-done.22.refs_2_, bf16[272,1024]{1,0:T(8,128)(2,1)S(1)} %collective-permute-done.23.refs_3_, ...), custom_call_target="tpu_custom_call" | custom-call | flops 8053063680 | bytes 18874368 | tf_op jit(solution)/shard_map/pallas_call | solution.py:124
  141.1 3.1 %collective-permute-done.43 = bf16[2,1,72,1024]{3,2,1,0:T(8,128)(2,1)S(1)} collective-permute-done((bf16[2,1,72,1024]{3,2,1,0:T(8,128)(2,1)S(1)}, bf16[2,1,72,1024]{3,2,1,0:T(8,128)(2,1)S(1)}, u32[]{:S(2)}, u32[]{:S(2)}) %collective-permute-start.43) | collective-permute-done | bytes 294944 | tf_op jit(solution)/shard_map/ppermute | solution.py:173
  146.8 3.9 %collective-permute-done.50 = bf16[1,1,72,1024]{3,2,1,0:T(8,128)(2,1)S(1)} collective-permute-done((bf16[1,1,72,1024]{3,2,1,0:T(8,128)(2,1)S(1)}, bf16[1,1,72,1024]{3,2,1,0:T(8,128)(2,1)S(1)}, u32[]{:S(2)}, u32[]{:S(2)}) %collective-permute-start.50) | collective-permute-done | bytes 147488 | tf_op jit(solution)/shard_map/ppermute | solution.py:173
  153.7 5.9 %collective-permute-done.53 = bf16[2,1,72,1024]{3,2,1,0:T(8,128)(2,1)S(1)} collective-permute-done((bf16[2,1,72,1024]{3,2,1,0:T(8,128)(2,1)S(1)}, bf16[2,1,72,1024]{3,2,1,0:T(8,128)(2,1)S(1)}, u32[]{:S(2)}, u32[]{:S(2)}) %collective-permute-start.53) | collective-permute-done | bytes 294944 | tf_op jit(solution)/shard_map/ppermute | solution.py:173
  163.1 2.8 %collective-permute-done.56 = bf16[144,1024]{1,0:T(8,128)(2,1)S(1)} collective-permute-done((bf16[144,1024]{1,0:T(8,128)(2,1)S(1)}, bf16[144,1024]{1,0:T(8,128)(2,1)S(1)}, u32[]{:S(2)}, u32[]{:S(2)}) %collective-permute-start.56) | collective-permute-done | bytes 294944 | tf_op jit(solution)/shard_map/ppermute | solution.py:173
  168.9 10.2 %collective-permute-done.48 = bf16[144,1024]{1,0:T(8,128)(2,1)S(1)} collective-permute-done((bf16[144,1024]{1,0:T(8,128)(2,1)S(1)}, bf16[144,1024]{1,0:T(8,128)(2,1)S(1)}, u32[]{:S(2)}, u32[]{:S(2)}) %collective-permute-start.48) | collective-permute-done | bytes 294944 | tf_op jit(solution)/shard_map/ppermute | solution.py:173
  179.0 1.5 collective-permute-done.57
  (150 shorter events, 44.5 us)
Async XLA Ops:
  2.4 14.4 %collective-permute-start = (bf16[272,1024]{1,0:T(8,128)(2,1)S(1)}, bf16[272,1024]{1,0:T(8,128)(2,1)S(1)}, u32[]{:S(2)}, u32[]{:S(2)}) collective-permute-start(bf16[272,1024]{1,0:T(8,128)(2,1)S(1)} %pad_maximum_fusion.refs_1_), channel_id=1, source_target_pairs={{0,8},{8,0},{16,24},{24,16},{1,9},{9,1},{17,25},{25,17},{2,10},{10... | collective-permute-start | bytes 1671176 | tf_op jit(solution)/shard_map/ppermute | solution.py:173
  2.5 17.5 %collective-permute-start.1 = (bf16[272,1024]{1,0:T(8,128)(2,1)S(1)}, bf16[272,1024]{1,0:T(8,128)(2,1)}, u32[]{:S(2)}, u32[]{:S(2)}) collective-permute-start(bf16[272,1024]{1,0:T(8,128)(2,1)S(1)} %pad_maximum_fusion.refs_1_), channel_id=1, source_target_pairs={{8,16},{16,8},{9,17},{17,9},{10,18},{18,10},{11,19},{19,11},{12,20... | collective-permute-start | bytes 1671176 | tf_op jit(solution)/shard_map/ppermute | solution.py:177
  7.6 13.9 %collective-permute-start.2 = (bf16[272,1024]{1,0:T(8,128)(2,1)S(1)}, bf16[272,1024]{1,0:T(8,128)(2,1)S(1)}, u32[]{:S(2)}, u32[]{:S(2)}) collective-permute-start(bf16[272,1024]{1,0:T(8,128)(2,1)S(1)} %pad_maximum_fusion.refs_1_), channel_id=1, source_target_pairs={{0,2},{2,0},{1,3},{3,1},{4,6},{6,4},{5,7},{7,5},{8,10},{10,8},{9,1... | collective-permute-start | bytes 1671176 | tf_op jit(solution)/shard_map/ppermute | solution.py:173
  9.1 13.5 %collective-permute-start.3 = (bf16[272,1024]{1,0:T(8,128)(2,1)S(1)}, bf16[272,1024]{1,0:T(8,128)(2,1)S(1)}, u32[]{:S(2)}, u32[]{:S(2)}) collective-permute-start(bf16[272,1024]{1,0:T(8,128)(2,1)S(1)} %pad_maximum_fusion.refs_1_), channel_id=1, source_target_pairs={{0,4},{4,0},{1,5},{5,1},{2,6},{6,2},{3,7},{7,3},{8,12},{12,8},{9,1... | collective-permute-start | bytes 1671176 | tf_op jit(solution)/shard_map/ppermute | solution.py:173
  22.7 20.6 %collective-permute-start.5 = (bf16[272,1024]{1,0:T(8,128)(2,1)S(1)}, bf16[272,1024]{1,0:T(8,128)(2,1)S(1)}, u32[]{:S(2)}, u32[]{:S(2)}) collective-permute-start(bf16[272,1024]{1,0:T(8,128)(2,1)S(1)} %collective-permute-done.refs_1_), channel_id=1, source_target_pairs={{8,16},{16,8},{9,17},{17,9},{10,18},{18,10},{11,19},{19,11},{12,20... | collective-permute-start | bytes 1671176 | tf_op jit(solution)/shard_map/ppermute | solution.py:177
  24.9 18.9 %collective-permute-start.8 = (bf16[272,1024]{1,0:T(8,128)(2,1)S(1)}, bf16[272,1024]{1,0:T(8,128)(2,1)S(1)}, u32[]{:S(2)}, u32[]{:S(2)}) collective-permute-start(bf16[272,1024]{1,0:T(8,128)(2,1)S(1)} %collective-permute-done.refs_1_), channel_id=1, source_target_pairs={{0,2},{2,0},{1,3},{3,1},{4,6},{6,4},{5,7},{7,5},{8,10},{10,8},{9,1... | collective-permute-start | bytes 1671176 | tf_op jit(solution)/shard_map/ppermute | solution.py:173
  25.5 9.3 %collective-permute-start.6 = (bf16[128,1024]{1,0:T(8,128)(2,1)S(1)}, bf16[128,1024]{1,0:T(8,128)(2,1)S(1)}, u32[]{:S(2)}, u32[]{:S(2)}) collective-permute-start(bf16[128,1024]{1,0:T(8,128)(2,1)S(1)} %slice.64), channel_id=1, source_target_pairs={{0,4},{4,0},{1,5},{5,1},{2,6},{6,2},{3,7},{7,3},{8,12},{12,8},{9,1... | collective-permute-start | bytes 786440 | tf_op jit(solution)/shard_map/ppermute | solution.py:173
  27.1 17.2 %collective-permute-start.9 = (bf16[272,1024]{1,0:T(8,128)(2,1)S(1)}, bf16[272,1024]{1,0:T(8,128)(2,1)S(1)}, u32[]{:S(2)}, u32[]{:S(2)}) collective-permute-start(bf16[272,1024]{1,0:T(8,128)(2,1)S(1)} %collective-permute-done.refs_1_), channel_id=1, source_target_pairs={{0,4},{4,0},{1,5},{5,1},{2,6},{6,2},{3,7},{7,3},{8,12},{12,8},{9,1... | collective-permute-start | bytes 1671176 | tf_op jit(solution)/shard_map/ppermute | solution.py:173
  27.6 16.7 %collective-permute-start.4 = (bf16[272,1024]{1,0:T(8,128)(2,1)}, bf16[272,1024]{1,0:T(8,128)(2,1)}, u32[]{:S(2)}, u32[]{:S(2)}) collective-permute-start(bf16[272,1024]{1,0:T(8,128)(2,1)} %collective-permute-done.1), channel_id=1, source_target_pairs={{8,0},{16,24},{9,1},{17,25},{10,2},{18,26},{11,3},{19,27},{12,4},{... | collective-permute-start | bytes 1671176 | tf_op jit(solution)/shard_map/ppermute | solution.py:177
  46.0 28.9 %collective-permute-start.24 = (bf16[272,1024]{1,0:T(8,128)(2,1)S(1)}, bf16[272,1024]{1,0:T(8,128)(2,1)S(1)}, u32[]{:S(2)}, u32[]{:S(2)}) collective-permute-start(bf16[272,1024]{1,0:T(8,128)(2,1)S(1)} %collective-permute-done.refs_1_), channel_id=1, source_target_pairs={{0,1},{1,0},{2,3},{3,2},{4,5},{5,4},{6,7},{7,6},{8,9},{9,8},{10,11... | collective-permute-start | bytes 1671176 | tf_op jit(solution)/shard_map/ppermute | solution.py:173
  46.4 25.0 %collective-permute-start.12 = (bf16[272,1024]{1,0:T(8,128)(2,1)S(1)}, bf16[272,1024]{1,0:T(8,128)(2,1)S(1)}, u32[]{:S(2)}, u32[]{:S(2)}) collective-permute-start(bf16[272,1024]{1,0:T(8,128)(2,1)S(1)} %broadcast_select_fusion.1.refs_1_), channel_id=1, source_target_pairs={{0,2},{2,0},{1,3},{3,1},{4,6},{6,4},{5,7},{7,5},{8,10},{10,8},{9,1... | collective-permute-start | bytes 1671176 | tf_op jit(solution)/shard_map/ppermute | solution.py:173
  47.7 23.8 %collective-permute-start.13 = (bf16[272,1024]{1,0:T(8,128)(2,1)S(1)}, bf16[272,1024]{1,0:T(8,128)(2,1)S(1)}, u32[]{:S(2)}, u32[]{:S(2)}) collective-permute-start(bf16[272,1024]{1,0:T(8,128)(2,1)S(1)} %broadcast_select_fusion.1.refs_1_), channel_id=1, source_target_pairs={{0,4},{4,0},{1,5},{5,1},{2,6},{6,2},{3,7},{7,3},{8,12},{12,8},{9,1... | collective-permute-start | bytes 1671176 | tf_op jit(solution)/shard_map/ppermute | solution.py:173
  49.2 23.8 %collective-permute-start.10 = (bf16[272,1024]{1,0:T(8,128)(2,1)S(1)}, bf16[272,1024]{1,0:T(8,128)(2,1)S(1)}, u32[]{:S(2)}, u32[]{:S(2)}) collective-permute-start(bf16[272,1024]{1,0:T(8,128)(2,1)S(1)} %copy-done.8), channel_id=1, source_target_pairs={{8,0},{16,24},{9,1},{17,25},{10,2},{18,26},{11,3},{19,27},{12,4},{... | collective-permute-start | bytes 1671176 | tf_op jit(solution)/shard_map/ppermute | solution.py:177
  50.6 22.4 %collective-permute-start.11 = (bf16[272,1024]{1,0:T(8,128)(2,1)S(1)}, bf16[272,1024]{1,0:T(8,128)(2,1)S(1)}, u32[]{:S(2)}, u32[]{:S(2)}) collective-permute-start(bf16[272,1024]{1,0:T(8,128)(2,1)S(1)} %collective-permute-done.9.refs_3_), channel_id=1, source_target_pairs={{0,2},{2,0},{1,3},{3,1},{4,6},{6,4},{5,7},{7,5},{8,10},{10,8},{9,1... | collective-permute-start | bytes 1671176 | tf_op jit(solution)/shard_map/ppermute | solution.py:173
  73.0 22.6 %collective-permute-start.19 = (bf16[4,144,1024]{2,1,0:T(8,128)(2,1)S(1)}, bf16[4,144,1024]{2,1,0:T(8,128)(2,1)S(1)}, u32[]{:S(2)}, u32[]{:S(2)}) collective-permute-start(bf16[4,144,1024]{2,1,0:T(8,128)(2,1)S(1)} %get-tuple-element.69), channel_id=1, source_target_pairs={{0,1},{1,0},{2,3},{3,2},{4,5},{5,4},{6,7},{7,6},{8,9},{9,8},{10,11... | collective-permute-start | bytes 3538952 | tf_op jit(solution)/shard_map/ppermute | solution.py:173
  74.9 20.7 %collective-permute-start.22 = (bf16[272,1024]{1,0:T(8,128)(2,1)S(1)}, bf16[272,1024]{1,0:T(8,128)(2,1)S(1)}, u32[]{:S(2)}, u32[]{:S(2)}) collective-permute-start(bf16[272,1024]{1,0:T(8,128)(2,1)S(1)} %broadcast_select_fusion.refs_1_), channel_id=1, source_target_pairs={{0,2},{2,0},{1,3},{3,1},{4,6},{6,4},{5,7},{7,5},{8,10},{10,8},{9,1... | collective-permute-start | bytes 1671176 | tf_op jit(solution)/shard_map/ppermute | solution.py:173
  75.7 19.9 %collective-permute-start.23 = (bf16[272,1024]{1,0:T(8,128)(2,1)S(1)}, bf16[272,1024]{1,0:T(8,128)(2,1)S(1)}, u32[]{:S(2)}, u32[]{:S(2)}) collective-permute-start(bf16[272,1024]{1,0:T(8,128)(2,1)S(1)} %broadcast_select_fusion.refs_1_), channel_id=1, source_target_pairs={{0,4},{4,0},{1,5},{5,1},{2,6},{6,2},{3,7},{7,3},{8,12},{12,8},{9,1... | collective-permute-start | bytes 1671176 | tf_op jit(solution)/shard_map/ppermute | solution.py:173
  77.2 18.3 %collective-permute-start.20 = (bf16[128,1024]{1,0:T(8,128)(2,1)S(1)}, bf16[128,1024]{1,0:T(8,128)(2,1)S(1)}, u32[]{:S(2)}, u32[]{:S(2)}) collective-permute-start(bf16[128,1024]{1,0:T(8,128)(2,1)S(1)} %slice.66), channel_id=1, source_target_pairs={{0,4},{4,0},{1,5},{5,1},{2,6},{6,2},{3,7},{7,3},{8,12},{12,8},{9,1... | collective-permute-start | bytes 786440 | tf_op jit(solution)/shard_map/ppermute | solution.py:173
  77.7 17.8 %collective-permute-start.21 = (bf16[128,1024]{1,0:T(8,128)(2,1)S(1)}, bf16[128,1024]{1,0:T(8,128)(2,1)S(1)}, u32[]{:S(2)}, u32[]{:S(2)}) collective-permute-start(bf16[128,1024]{1,0:T(8,128)(2,1)S(1)} %slice.67), channel_id=1, source_target_pairs={{0,2},{2,0},{1,3},{3,1},{4,6},{6,4},{5,7},{7,5},{8,10},{10,8},{9,1... | collective-permute-start | bytes 786440 | tf_op jit(solution)/shard_map/ppermute | solution.py:173
  99.3 17.0 %collective-permute-start.28 = (bf16[1,2,144,1024]{3,2,1,0:T(8,128)(2,1)S(1)}, bf16[1,2,144,1024]{3,2,1,0:T(8,128)(2,1)S(1)}, u32[]{:S(2)}, u32[]{:S(2)}) collective-permute-start(bf16[1,2,144,1024]{3,2,1,0:T(8,128)(2,1)S(1)} %get-tuple-element.124), channel_id=1, source_target_pairs={{0,4},{4,0},{1,5},{5,1},{2,6},{6,2},{3,7},{7,3},{8,12},{12,8},{9,1... | collective-permute-start | bytes 1769480 | tf_op jit(solution)/shard_map/ppermute | solution.py:173
  100.8 15.5 %collective-permute-start.29 = (bf16[272,1024]{1,0:T(8,128)(2,1)S(1)}, bf16[272,1024]{1,0:T(8,128)(2,1)S(1)}, u32[]{:S(2)}, u32[]{:S(2)}) collective-permute-start(bf16[272,1024]{1,0:T(8,128)(2,1)S(1)} %collective-permute-done.23.refs_3_), channel_id=1, source_target_pairs={{0,2},{2,0},{1,3},{3,1},{4,6},{6,4},{5,7},{7,5},{8,10},{10,8},{9,1... | collective-permute-start | bytes 1671176 | tf_op jit(solution)/shard_map/ppermute | solution.py:173
  102.1 19.0 %collective-permute-start.31 = (bf16[1,2,72,1024]{3,2,1,0:T(8,128)(2,1)S(1)}, bf16[1,2,72,1024]{3,2,1,0:T(8,128)(2,1)S(1)}, u32[]{:S(2)}, u32[]{:S(2)}) collective-permute-start(bf16[1,2,72,1024]{3,2,1,0:T(8,128)(2,1)S(1)} %get-tuple-element.81), channel_id=1, source_target_pairs={{0,4},{4,0},{1,5},{5,1},{2,6},{6,2},{3,7},{7,3},{8,12},{12,8},{9,1... | collective-permute-start | bytes 884744 | tf_op jit(solution)/shard_map/ppermute | solution.py:173
  102.9 18.7 %collective-permute-start.32 = (bf16[2,1,72,1024]{3,2,1,0:T(8,128)(2,1)S(1)}, bf16[2,1,72,1024]{3,2,1,0:T(8,128)(2,1)S(1)}, u32[]{:S(2)}, u32[]{:S(2)}) collective-permute-start(bf16[2,1,72,1024]{3,2,1,0:T(8,128)(2,1)S(1)} %get-tuple-element.82), channel_id=1, source_target_pairs={{0,2},{2,0},{1,3},{3,1},{4,6},{6,4},{5,7},{7,5},{8,10},{10,8},{9,1... | collective-permute-start | bytes 884744 | tf_op jit(solution)/shard_map/ppermute | solution.py:173
  124.5 16.6 %collective-permute-start.40 = (bf16[1,1,72,1024]{3,2,1,0:T(8,128)(2,1)S(1)}, bf16[1,1,72,1024]{3,2,1,0:T(8,128)(2,1)S(1)}, u32[]{:S(2)}, u32[]{:S(2)}) collective-permute-start(bf16[1,1,72,1024]{3,2,1,0:T(8,128)(2,1)S(1)} %add_convert_fusion.33), channel_id=1, source_target_pairs={{0,4},{4,0},{1,5},{5,1},{2,6},{6,2},{3,7},{7,3},{8,12},{12,8},{9,1... | collective-permute-start | bytes 442376 | tf_op jit(solution)/shard_map/ppermute | solution.py:173
  125.9 15.2 %collective-permute-start.39 = (bf16[1,1,72,1024]{3,2,1,0:T(8,128)(2,1)S(1)}, bf16[1,1,72,1024]{3,2,1,0:T(8,128)(2,1)S(1)}, u32[]{:S(2)}, u32[]{:S(2)}) collective-permute-start(bf16[1,1,72,1024]{3,2,1,0:T(8,128)(2,1)S(1)} %add_convert_fusion.34), channel_id=1, source_target_pairs={{0,2},{2,0},{1,3},{3,1},{4,6},{6,4},{5,7},{7,5},{8,10},{10,8},{9,1... | collective-permute-start | bytes 442376 | tf_op jit(solution)/shard_map/ppermute | solution.py:173
  127.3 13.8 %collective-permute-start.38 = (bf16[1,1,144,1024]{3,2,1,0:T(8,128)(2,1)S(1)}, bf16[1,1,144,1024]{3,2,1,0:T(8,128)(2,1)S(1)}, u32[]{:S(2)}, u32[]{:S(2)}) collective-permute-start(bf16[1,1,144,1024]{3,2,1,0:T(8,128)(2,1)S(1)} %add_convert_fusion.13), channel_id=1, source_target_pairs={{0,2},{2,0},{1,3},{3,1},{4,6},{6,4},{5,7},{7,5},{8,10},{10,8},{9,1... | collective-permute-start | bytes 884744 | tf_op jit(solution)/shard_map/ppermute | solution.py:173
  128.1 13.0 %collective-permute-start.42 = (bf16[1,2,72,1024]{3,2,1,0:T(8,128)(2,1)S(1)}, bf16[1,2,72,1024]{3,2,1,0:T(8,128)(2,1)S(1)}, u32[]{:S(2)}, u32[]{:S(2)}) collective-permute-start(bf16[1,2,72,1024]{3,2,1,0:T(8,128)(2,1)S(1)} %get-tuple-element.93), channel_id=1, source_target_pairs={{0,4},{4,0},{1,5},{5,1},{2,6},{6,2},{3,7},{7,3},{8,12},{12,8},{9,1... | collective-permute-start | bytes 884744 | tf_op jit(solution)/shard_map/ppermute | solution.py:173
  129.1 15.1 %collective-permute-start.43 = (bf16[2,1,72,1024]{3,2,1,0:T(8,128)(2,1)S(1)}, bf16[2,1,72,1024]{3,2,1,0:T(8,128)(2,1)S(1)}, u32[]{:S(2)}, u32[]{:S(2)}) collective-permute-start(bf16[2,1,72,1024]{3,2,1,0:T(8,128)(2,1)S(1)} %get-tuple-element.94), channel_id=1, source_target_pairs={{0,2},{2,0},{1,3},{3,1},{4,6},{6,4},{5,7},{7,5},{8,10},{10,8},{9,1... | collective-permute-start | bytes 884744 | tf_op jit(solution)/shard_map/ppermute | solution.py:173
  150.9 8.7 %collective-permute-start.53 = (bf16[2,1,72,1024]{3,2,1,0:T(8,128)(2,1)S(1)}, bf16[2,1,72,1024]{3,2,1,0:T(8,128)(2,1)S(1)}, u32[]{:S(2)}, u32[]{:S(2)}) collective-permute-start(bf16[2,1,72,1024]{3,2,1,0:T(8,128)(2,1)S(1)} %get-tuple-element.113), channel_id=1, source_target_pairs={{0,2},{2,0},{1,3},{3,1},{4,6},{6,4},{5,7},{7,5},{8,10},{10,8},{9,1... | collective-permute-start | bytes 884744 | tf_op jit(solution)/shard_map/ppermute | solution.py:173
  153.6 12.3 %collective-permute-start.56 = (bf16[144,1024]{1,0:T(8,128)(2,1)S(1)}, bf16[144,1024]{1,0:T(8,128)(2,1)S(1)}, u32[]{:S(2)}, u32[]{:S(2)}) collective-permute-start(bf16[144,1024]{1,0:T(8,128)(2,1)S(1)} %pad_maximum_fusion.2), channel_id=1, source_target_pairs={{0,16},{8,24},{16,0},{24,8},{1,17},{9,25},{17,1},{25,9},{2,18},{10... | collective-permute-start | bytes 884744 | tf_op jit(solution)/shard_map/ppermute | solution.py:173
  163.0 16.0 %collective-permute-start.48 = (bf16[144,1024]{1,0:T(8,128)(2,1)S(1)}, bf16[144,1024]{1,0:T(8,128)(2,1)S(1)}, u32[]{:S(2)}, u32[]{:S(2)}) collective-permute-start(bf16[144,1024]{1,0:T(8,128)(2,1)S(1)} %pad_maximum_fusion.1), channel_id=1, source_target_pairs={{0,8},{8,0},{16,24},{24,16},{1,9},{9,1},{17,25},{25,17},{2,10},{10... | collective-permute-start | bytes 884744 | tf_op jit(solution)/shard_map/ppermute | solution.py:173
  167.4 13.1 %collective-permute-start.57 = (bf16[144,1024]{1,0:T(8,128)(2,1)S(1)}, bf16[144,1024]{1,0:T(8,128)(2,1)S(1)}, u32[]{:S(2)}, u32[]{:S(2)}) collective-permute-start(bf16[144,1024]{1,0:T(8,128)(2,1)S(1)} %pad_maximum_fusion.3), channel_id=1, source_target_pairs={{0,24},{8,16},{16,8},{24,0},{1,25},{9,17},{17,9},{25,1},{2,26},{10... | collective-permute-start | bytes 884744 | tf_op jit(solution)/shard_map/ppermute | solution.py:173
  (38 other events, 247.8 us)

commit v4 on v3

--- a/solution.py
+++ b/solution.py
@@ -284,7 +284,7 @@
         for dy, dx in labels:
             if depth[dy, dx] != level:
                 continue
-            if dy and dx and q % 2:
+            if dy and dx and q % 4 not in (0,2,3,):
                 whole = have[q][dy, dx ^ last_bit(dx), 0]
                 ops.append((q, (dy, dx, 0), [(c, None) for c in whole], "col", last_bit(dx)))
             elif dy and dx:
@@ -324,7 +324,7 @@
             self.q, self.half, self.todo, self.mine = q, None, None, None
             self.cells = [Cell(keep), Cell(send)]
             self.urgent = q > 0
-            self.orders = [("near", "col"), ("col", "near")][: 2 if self.urgent else 1]
+            self.orders = [("near", "col"), ("col", "near")]
 
         def begin(self):
             self.half = Cell(exchange(self.cells[1].v, "half", 1))
@@ -395,8 +395,13 @@
                 else:
                     ready.append(s.half)
             elif s.todo is None:
-                s.first()
-                ready += s.step()
+                if r >= depths + 3:
+                    s.first()
+                    ready += s.step()
+                else:
+                    ready.append(s.half)
+            elif s.left() == 1 and not s.urgent and any(o.urgent and (o.todo is None or o.left()) for o in sums):
+                ready += s.got
             elif s.left():
                 s.refold()
                 ready += s.step()

time: 185 us -> 179 us (0.968); the launches traced: 182 us -> 179 us
  waiting for transfers between devices: 71.6 us -> 65.8 us
  starting transfers between devices: 48.1 us -> 50.9 us
    ppermute x54 -> x58, waiting for transfers between devices: 68.4 us -> 62.6 us  [exchange(): lax.ppermute(x, axis, [(i, i ^ step) for i in range(lax.axis_size(axis))])]
    ppermute x54 -> x58, starting transfers between devices: 37.5 us -> 40.2 us  [exchange(): lax.ppermute(x, axis, [(i, i ^ step) for i in range(lax.axis_size(axis))])]
  transfers between devices with their start and end apart: 58 -> 62, of which waited for: 24 -> 26; matrix products, arithmetic and copies ran while one was open for 3% -> 3% of each run, Pallas kernels for 24% -> 24%
where the time goes in v4:
time: 179 us
  waiting for transfers between devices  65.8 us (37%)
  starting transfers between devices  50.9 us (28%)
  Pallas kernels  43.6 us (24%)
  local copies, waits for them, and re-layouts  9.62 us (5%)
  other arithmetic  7.51 us (4%)
    ppermute x58, waiting for transfers between devices, exchange(): lax.ppermute(x, axis, [(i, i ^ step) for i in range(lax.axis_size(axis))])  62.6 us
    pallas_call x4, Pallas kernels, expert_call(): pl.pallas_call(functools.partial(expert_kernel, (at, out_at, len(pieces),...  43.6 us
    ppermute x58, starting transfers between devices, exchange(): lax.ppermute(x, axis, [(i, i ^ step) for i in range(lax.axis_size(axis))])  40.2 us
    ppermute x4, starting transfers between devices, passed(): return lax.ppermute(x, axis, pairs)  10.6 us
    unnamed x24, local copies, waits for them, and re-layouts  8.67 us
  transfers between devices with their start and end apart: 62, of which 26 were waited for; matrix products, arithmetic and copies ran while one was open for 3% of the time, Pallas kernels for 24%

profile of v4, /device:TPU:8, one launch (start us, length us, event | category | flops | bytes accessed | tf_op | source)
XLA Modules:
  0.0 178.6 jit_solution(3564059022262163051)
XLA Ops:
  2.5 5.0 %collective-permute-start.1 = (bf16[272,1024]{1,0:T(8,128)(2,1)S(1)}, bf16[272,1024]{1,0:T(8,128)(2,1)}, u32[]{:S(2)}, u32[]{:S(2)}) collective-permute-start(bf16[272,1024]{1,0:T(8,128)(2,1)S(1)} %pad_maximum_fusion.refs_1_), channel_id=1, source_target_pairs={{8,16},{16,8},{9,17},{17,9},{10,18},{18,10},{11,19},{19,11},{12,20... | collective-permute-start | bytes 1671176 | tf_op jit(solution)/shard_map/ppermute | solution.py:177
  7.6 1.6 collective-permute-start.2
  9.1 1.5 collective-permute-start.3
  10.6 6.2 %collective-permute-done.refs_1_ = bf16[272,1024]{1,0:T(8,128)(2,1)S(1)} collective-permute-done((bf16[272,1024]{1,0:T(8,128)(2,1)S(1)}, bf16[272,1024]{1,0:T(8,128)(2,1)S(1)}, u32[]{:S(2)}, u32[]{:S(2)}) %collective-permute-start) | collective-permute-done | bytes 557088 | tf_op jit(solution)/shard_map/ppermute | solution.py:173
  16.9 3.1 %collective-permute-done.1 = bf16[272,1024]{1,0:T(8,128)(2,1)} collective-permute-done((bf16[272,1024]{1,0:T(8,128)(2,1)S(1)}, bf16[272,1024]{1,0:T(8,128)(2,1)}, u32[]{:S(2)}, u32[]{:S(2)}) %collective-permute-start.1) | collective-permute-done | bytes 557088 | tf_op jit(solution)/shard_map/ppermute | solution.py:177
  20.0 1.4 collective-permute-done.2.refs_2_
  22.7 2.2 %collective-permute-start.5 = (bf16[272,1024]{1,0:T(8,128)(2,1)S(1)}, bf16[272,1024]{1,0:T(8,128)(2,1)S(1)}, u32[]{:S(2)}, u32[]{:S(2)}) collective-permute-start(bf16[272,1024]{1,0:T(8,128)(2,1)S(1)} %collective-permute-done.refs_1_), channel_id=1, source_target_pairs={{8,16},{16,8},{9,17},{17,9},{10,18},{18,10},{11,19},{19,11},{12,20... | collective-permute-start | bytes 1671176 | tf_op jit(solution)/shard_map/ppermute | solution.py:177
  25.5 1.6 collective-permute-start.6
  27.6 2.1 %collective-permute-start.4 = (bf16[272,1024]{1,0:T(8,128)(2,1)}, bf16[272,1024]{1,0:T(8,128)(2,1)}, u32[]{:S(2)}, u32[]{:S(2)}) collective-permute-start(bf16[272,1024]{1,0:T(8,128)(2,1)} %collective-permute-done.1), channel_id=1, source_target_pairs={{8,0},{16,24},{9,1},{17,25},{10,2},{18,26},{11,3},{19,27},{12,4},{... | collective-permute-start | bytes 1671176 | tf_op jit(solution)/shard_map/ppermute | solution.py:177
  29.7 5.1 %collective-permute-done.6.refs_5_ = bf16[128,1024]{1,0:T(8,128)(2,1)S(1)} collective-permute-done((bf16[128,1024]{1,0:T(8,128)(2,1)S(1)}, bf16[128,1024]{1,0:T(8,128)(2,1)S(1)}, u32[]{:S(2)}, u32[]{:S(2)}) %collective-permute-start.6) | collective-permute-done | bytes 262176 | tf_op jit(solution)/shard_map/ppermute | solution.py:173
  34.8 1.5 collective-permute-start.7
  36.3 7.0 %collective-permute-done.7.refs_6_ = bf16[128,1024]{1,0:T(8,128)(2,1)S(1)} collective-permute-done((bf16[128,1024]{1,0:T(8,128)(2,1)S(1)}, bf16[128,1024]{1,0:T(8,128)(2,1)S(1)}, u32[]{:S(2)}, u32[]{:S(2)}) %collective-permute-start.7) | collective-permute-done | bytes 262176 | tf_op jit(solution)/shard_map/ppermute | solution.py:173
  47.7 1.5 collective-permute-start.13
  51.4 2.8 %copy-done = bf16[2,384,4096]{2,1,0:T(8,128)(2,1)S(1)} copy-done((bf16[2,384,4096]{2,1,0:T(8,128)(2,1)S(1)}, bf16[2,384,4096]{2,1,0:T(8,128)(2,1)}, u32[]{:S(2)}) %copy-start) | copy-done | bytes 6291480
  54.2 2.8 %copy-done.1 = bf16[2,384,4096]{2,1,0:T(8,128)(2,1)S(1)} copy-done((bf16[2,384,4096]{2,1,0:T(8,128)(2,1)S(1)}, bf16[2,384,4096]{2,1,0:T(8,128)(2,1)}, u32[]{:S(2)}) %copy-start.1) | copy-done | bytes 6291480
  57.0 2.8 %copy-done.2 = bf16[2,384,4096]{2,1,0:T(8,128)(2,1)S(1)} copy-done((bf16[2,384,4096]{2,1,0:T(8,128)(2,1)S(1)}, bf16[2,384,4096]{2,1,0:T(8,128)(2,1)}, u32[]{:S(2)}) %copy-start.2) | copy-done | bytes 6291480
  59.8 11.5 %shard_map.86 = (bf16[4,144,1024]{2,1,0:T(8,128)(2,1)S(1)}, bf16[4,144,1024]{2,1,0:T(8,128)(2,1)S(1)}) custom-call(s32[5]{0:T(128)S(1)} %stack.23.refs_0_, bf16[272,1024]{1,0:T(8,128)(2,1)S(1)} %pad_maximum_fusion.refs_1_, bf16[272,1024]{1,0:T(8,128)(2,1)S(1)} %collective-permute-done.2.refs_2_, bf16[272,1024]{1,0:T(8,128)(2,1)S(1)} %collective-permute-done.3.refs_3_, ...), custom_call_target="tpu_custom_call" | custom-call | flops 8053063680 | bytes 18874368 | tf_op jit(solution)/shard_map/pallas_call | solution.py:124
  75.5 1.5 collective-permute-start.23
  78.8 10.7 %shard_map.87 = (bf16[4,144,1024]{2,1,0:T(8,128)(2,1)S(1)}, bf16[4,144,1024]{2,1,0:T(8,128)(2,1)S(1)}) custom-call(s32[5]{0:T(128)S(1)} %stack.23.refs_0_, bf16[272,1024]{1,0:T(8,128)(2,1)S(1)} %collective-permute-done.refs_1_, bf16[272,1024]{1,0:T(8,128)(2,1)S(1)} %collective-permute-done.8.refs_2_, bf16[272,1024]{1,0:T(8,128)(2,1)S(1)} %collective-permute-done.9.refs_3_, ...), custom_call_target="tpu_custom_call" | custom-call | flops 8053063680 | bytes 18874368 | tf_op jit(solution)/shard_map/pallas_call | solution.py:124
  89.5 5.9 %collective-permute-done.20.refs_5_ = bf16[128,1024]{1,0:T(8,128)(2,1)S(1)} collective-permute-done((bf16[128,1024]{1,0:T(8,128)(2,1)S(1)}, bf16[128,1024]{1,0:T(8,128)(2,1)S(1)}, u32[]{:S(2)}, u32[]{:S(2)}) %collective-permute-start.20) | collective-permute-done | bytes 262176 | tf_op jit(solution)/shard_map/ppermute | solution.py:173
  96.6 1.7 collective-permute-done.28
  99.1 1.5 collective-permute-start.29
  103.5 10.7 %shard_map.88 = (bf16[4,144,1024]{2,1,0:T(8,128)(2,1)S(1)}, bf16[4,144,1024]{2,1,0:T(8,128)(2,1)S(1)}) custom-call(s32[5]{0:T(128)S(1)} %stack.23.refs_0_, bf16[272,1024]{1,0:T(8,128)(2,1)S(1)} %broadcast_select_fusion.1.refs_1_, bf16[272,1024]{1,0:T(8,128)(2,1)S(1)} %collective-permute-done.12.refs_2_, ...), custom_call_target="tpu_custom_call" | custom-call | flops 8053063680 | bytes 18874368 | tf_op jit(solution)/shard_map/pallas_call | solution.py:124
  122.1 2.6 %collective-permute-done.41 = bf16[1,1,72,1024]{3,2,1,0:T(8,128)(2,1)S(1)} collective-permute-done((bf16[1,1,72,1024]{3,2,1,0:T(8,128)(2,1)S(1)}, bf16[1,1,72,1024]{3,2,1,0:T(8,128)(2,1)S(1)}, u32[]{:S(2)}, u32[]{:S(2)}) %collective-permute-start.41) | collective-permute-done | bytes 147488 | tf_op jit(solution)/shard_map/ppermute | solution.py:173
  128.0 10.6 %shard_map.89 = (bf16[4,144,1024]{2,1,0:T(8,128)(2,1)S(1)}, bf16[4,144,1024]{2,1,0:T(8,128)(2,1)S(1)}) custom-call(s32[5]{0:T(128)S(1)} %stack.23.refs_0_, bf16[272,1024]{1,0:T(8,128)(2,1)S(1)} %broadcast_select_fusion.refs_1_, bf16[272,1024]{1,0:T(8,128)(2,1)S(1)} %collective-permute-done.22.refs_2_, bf16[272,1024]{1,0:T(8,128)(2,1)S(1)} %collective-permute-done.23.refs_3_, ...), custom_call_target="tpu_custom_call" | custom-call | flops 8053063680 | bytes 18874368 | tf_op jit(solution)/shard_map/pallas_call | solution.py:124
  141.7 4.0 %collective-permute-done.51 = bf16[1,1,72,1024]{3,2,1,0:T(8,128)(2,1)S(1)} collective-permute-done((bf16[1,1,72,1024]{3,2,1,0:T(8,128)(2,1)S(1)}, bf16[1,1,72,1024]{3,2,1,0:T(8,128)(2,1)S(1)}, u32[]{:S(2)}, u32[]{:S(2)}) %collective-permute-start.51) | collective-permute-done | bytes 147488 | tf_op jit(solution)/shard_map/ppermute | solution.py:173
  148.7 6.0 %collective-permute-done.55 = bf16[2,1,72,1024]{3,2,1,0:T(8,128)(2,1)S(1)} collective-permute-done((bf16[2,1,72,1024]{3,2,1,0:T(8,128)(2,1)S(1)}, bf16[2,1,72,1024]{3,2,1,0:T(8,128)(2,1)S(1)}, u32[]{:S(2)}, u32[]{:S(2)}) %collective-permute-start.55) | collective-permute-done | bytes 294944 | tf_op jit(solution)/shard_map/ppermute | solution.py:173
  158.1 2.8 %collective-permute-done.58 = bf16[144,1024]{1,0:T(8,128)(2,1)S(1)} collective-permute-done((bf16[144,1024]{1,0:T(8,128)(2,1)S(1)}, bf16[144,1024]{1,0:T(8,128)(2,1)S(1)}, u32[]{:S(2)}, u32[]{:S(2)}) %collective-permute-start.58) | collective-permute-done | bytes 294944 | tf_op jit(solution)/shard_map/ppermute | solution.py:173
  164.5 1.4 collective-permute-start.59
  165.9 1.6 collective-permute-done.61
  168.8 5.2 %collective-permute-done.50 = bf16[144,1024]{1,0:T(8,128)(2,1)S(1)} collective-permute-done((bf16[144,1024]{1,0:T(8,128)(2,1)S(1)}, bf16[144,1024]{1,0:T(8,128)(2,1)S(1)}, u32[]{:S(2)}, u32[]{:S(2)}) %collective-permute-start.50) | collective-permute-done | bytes 294944 | tf_op jit(solution)/shard_map/ppermute | solution.py:173
  174.0 3.0 %collective-permute-done.59 = bf16[144,1024]{1,0:T(8,128)(2,1)S(1)} collective-permute-done((bf16[144,1024]{1,0:T(8,128)(2,1)S(1)}, bf16[144,1024]{1,0:T(8,128)(2,1)S(1)}, u32[]{:S(2)}, u32[]{:S(2)}) %collective-permute-start.59) | collective-permute-done | bytes 294944 | tf_op jit(solution)/shard_map/ppermute | solution.py:173
  (163 shorter events, 48.4 us)
Async XLA Ops:
  2.4 14.4 %collective-permute-start = (bf16[272,1024]{1,0:T(8,128)(2,1)S(1)}, bf16[272,1024]{1,0:T(8,128)(2,1)S(1)}, u32[]{:S(2)}, u32[]{:S(2)}) collective-permute-start(bf16[272,1024]{1,0:T(8,128)(2,1)S(1)} %pad_maximum_fusion.refs_1_), channel_id=1, source_target_pairs={{0,8},{8,0},{16,24},{24,16},{1,9},{9,1},{17,25},{25,17},{2,10},{10... | collective-permute-start | bytes 1671176 | tf_op jit(solution)/shard_map/ppermute | solution.py:173
  2.5 17.5 %collective-permute-start.1 = (bf16[272,1024]{1,0:T(8,128)(2,1)S(1)}, bf16[272,1024]{1,0:T(8,128)(2,1)}, u32[]{:S(2)}, u32[]{:S(2)}) collective-permute-start(bf16[272,1024]{1,0:T(8,128)(2,1)S(1)} %pad_maximum_fusion.refs_1_), channel_id=1, source_target_pairs={{8,16},{16,8},{9,17},{17,9},{10,18},{18,10},{11,19},{19,11},{12,20... | collective-permute-start | bytes 1671176 | tf_op jit(solution)/shard_map/ppermute | solution.py:177
  7.6 13.9 %collective-permute-start.2 = (bf16[272,1024]{1,0:T(8,128)(2,1)S(1)}, bf16[272,1024]{1,0:T(8,128)(2,1)S(1)}, u32[]{:S(2)}, u32[]{:S(2)}) collective-permute-start(bf16[272,1024]{1,0:T(8,128)(2,1)S(1)} %pad_maximum_fusion.refs_1_), channel_id=1, source_target_pairs={{0,2},{2,0},{1,3},{3,1},{4,6},{6,4},{5,7},{7,5},{8,10},{10,8},{9,1... | collective-permute-start | bytes 1671176 | tf_op jit(solution)/shard_map/ppermute | solution.py:173
  9.1 13.5 %collective-permute-start.3 = (bf16[272,1024]{1,0:T(8,128)(2,1)S(1)}, bf16[272,1024]{1,0:T(8,128)(2,1)S(1)}, u32[]{:S(2)}, u32[]{:S(2)}) collective-permute-start(bf16[272,1024]{1,0:T(8,128)(2,1)S(1)} %pad_maximum_fusion.refs_1_), channel_id=1, source_target_pairs={{0,4},{4,0},{1,5},{5,1},{2,6},{6,2},{3,7},{7,3},{8,12},{12,8},{9,1... | collective-permute-start | bytes 1671176 | tf_op jit(solution)/shard_map/ppermute | solution.py:173
  22.7 20.6 %collective-permute-start.5 = (bf16[272,1024]{1,0:T(8,128)(2,1)S(1)}, bf16[272,1024]{1,0:T(8,128)(2,1)S(1)}, u32[]{:S(2)}, u32[]{:S(2)}) collective-permute-start(bf16[272,1024]{1,0:T(8,128)(2,1)S(1)} %collective-permute-done.refs_1_), channel_id=1, source_target_pairs={{8,16},{16,8},{9,17},{17,9},{10,18},{18,10},{11,19},{19,11},{12,20... | collective-permute-start | bytes 1671176 | tf_op jit(solution)/shard_map/ppermute | solution.py:177
  24.9 18.9 %collective-permute-start.8 = (bf16[272,1024]{1,0:T(8,128)(2,1)S(1)}, bf16[272,1024]{1,0:T(8,128)(2,1)S(1)}, u32[]{:S(2)}, u32[]{:S(2)}) collective-permute-start(bf16[272,1024]{1,0:T(8,128)(2,1)S(1)} %collective-permute-done.refs_1_), channel_id=1, source_target_pairs={{0,2},{2,0},{1,3},{3,1},{4,6},{6,4},{5,7},{7,5},{8,10},{10,8},{9,1... | collective-permute-start | bytes 1671176 | tf_op jit(solution)/shard_map/ppermute | solution.py:173
  25.5 9.3 %collective-permute-start.6 = (bf16[128,1024]{1,0:T(8,128)(2,1)S(1)}, bf16[128,1024]{1,0:T(8,128)(2,1)S(1)}, u32[]{:S(2)}, u32[]{:S(2)}) collective-permute-start(bf16[128,1024]{1,0:T(8,128)(2,1)S(1)} %slice.78), channel_id=1, source_target_pairs={{0,4},{4,0},{1,5},{5,1},{2,6},{6,2},{3,7},{7,3},{8,12},{12,8},{9,1... | collective-permute-start | bytes 786440 | tf_op jit(solution)/shard_map/ppermute | solution.py:173
  27.1 17.2 %collective-permute-start.9 = (bf16[272,1024]{1,0:T(8,128)(2,1)S(1)}, bf16[272,1024]{1,0:T(8,128)(2,1)S(1)}, u32[]{:S(2)}, u32[]{:S(2)}) collective-permute-start(bf16[272,1024]{1,0:T(8,128)(2,1)S(1)} %collective-permute-done.refs_1_), channel_id=1, source_target_pairs={{0,4},{4,0},{1,5},{5,1},{2,6},{6,2},{3,7},{7,3},{8,12},{12,8},{9,1... | collective-permute-start | bytes 1671176 | tf_op jit(solution)/shard_map/ppermute | solution.py:173
  27.6 16.7 %collective-permute-start.4 = (bf16[272,1024]{1,0:T(8,128)(2,1)}, bf16[272,1024]{1,0:T(8,128)(2,1)}, u32[]{:S(2)}, u32[]{:S(2)}) collective-permute-start(bf16[272,1024]{1,0:T(8,128)(2,1)} %collective-permute-done.1), channel_id=1, source_target_pairs={{8,0},{16,24},{9,1},{17,25},{10,2},{18,26},{11,3},{19,27},{12,4},{... | collective-permute-start | bytes 1671176 | tf_op jit(solution)/shard_map/ppermute | solution.py:177
  45.9 28.7 %collective-permute-start.24 = (bf16[272,1024]{1,0:T(8,128)(2,1)S(1)}, bf16[272,1024]{1,0:T(8,128)(2,1)S(1)}, u32[]{:S(2)}, u32[]{:S(2)}) collective-permute-start(bf16[272,1024]{1,0:T(8,128)(2,1)S(1)} %collective-permute-done.refs_1_), channel_id=1, source_target_pairs={{0,1},{1,0},{2,3},{3,2},{4,5},{5,4},{6,7},{7,6},{8,9},{9,8},{10,11... | collective-permute-start | bytes 1671176 | tf_op jit(solution)/shard_map/ppermute | solution.py:173
  46.4 24.9 %collective-permute-start.12 = (bf16[272,1024]{1,0:T(8,128)(2,1)S(1)}, bf16[272,1024]{1,0:T(8,128)(2,1)S(1)}, u32[]{:S(2)}, u32[]{:S(2)}) collective-permute-start(bf16[272,1024]{1,0:T(8,128)(2,1)S(1)} %broadcast_select_fusion.1.refs_1_), channel_id=1, source_target_pairs={{0,2},{2,0},{1,3},{3,1},{4,6},{6,4},{5,7},{7,5},{8,10},{10,8},{9,1... | collective-permute-start | bytes 1671176 | tf_op jit(solution)/shard_map/ppermute | solution.py:173
  47.7 23.7 %collective-permute-start.13 = (bf16[272,1024]{1,0:T(8,128)(2,1)S(1)}, bf16[272,1024]{1,0:T(8,128)(2,1)S(1)}, u32[]{:S(2)}, u32[]{:S(2)}) collective-permute-start(bf16[272,1024]{1,0:T(8,128)(2,1)S(1)} %broadcast_select_fusion.1.refs_1_), channel_id=1, source_target_pairs={{0,4},{4,0},{1,5},{5,1},{2,6},{6,2},{3,7},{7,3},{8,12},{12,8},{9,1... | collective-permute-start | bytes 1671176 | tf_op jit(solution)/shard_map/ppermute | solution.py:173
  49.2 23.8 %collective-permute-start.10 = (bf16[272,1024]{1,0:T(8,128)(2,1)S(1)}, bf16[272,1024]{1,0:T(8,128)(2,1)S(1)}, u32[]{:S(2)}, u32[]{:S(2)}) collective-permute-start(bf16[272,1024]{1,0:T(8,128)(2,1)S(1)} %copy-done.8), channel_id=1, source_target_pairs={{8,0},{16,24},{9,1},{17,25},{10,2},{18,26},{11,3},{19,27},{12,4},{... | collective-permute-start | bytes 1671176 | tf_op jit(solution)/shard_map/ppermute | solution.py:177
  50.6 22.4 %collective-permute-start.11 = (bf16[272,1024]{1,0:T(8,128)(2,1)S(1)}, bf16[272,1024]{1,0:T(8,128)(2,1)S(1)}, u32[]{:S(2)}, u32[]{:S(2)}) collective-permute-start(bf16[272,1024]{1,0:T(8,128)(2,1)S(1)} %collective-permute-done.9.refs_3_), channel_id=1, source_target_pairs={{0,2},{2,0},{1,3},{3,1},{4,6},{6,4},{5,7},{7,5},{8,10},{10,8},{9,1... | collective-permute-start | bytes 1671176 | tf_op jit(solution)/shard_map/ppermute | solution.py:173
  73.0 22.4 %collective-permute-start.19 = (bf16[4,144,1024]{2,1,0:T(8,128)(2,1)S(1)}, bf16[4,144,1024]{2,1,0:T(8,128)(2,1)S(1)}, u32[]{:S(2)}, u32[]{:S(2)}) collective-permute-start(bf16[4,144,1024]{2,1,0:T(8,128)(2,1)S(1)} %get-tuple-element.76), channel_id=1, source_target_pairs={{0,1},{1,0},{2,3},{3,2},{4,5},{5,4},{6,7},{7,6},{8,9},{9,8},{10,11... | collective-permute-start | bytes 3538952 | tf_op jit(solution)/shard_map/ppermute | solution.py:173
  74.7 20.7 %collective-permute-start.22 = (bf16[272,1024]{1,0:T(8,128)(2,1)S(1)}, bf16[272,1024]{1,0:T(8,128)(2,1)S(1)}, u32[]{:S(2)}, u32[]{:S(2)}) collective-permute-start(bf16[272,1024]{1,0:T(8,128)(2,1)S(1)} %broadcast_select_fusion.refs_1_), channel_id=1, source_target_pairs={{0,2},{2,0},{1,3},{3,1},{4,6},{6,4},{5,7},{7,5},{8,10},{10,8},{9,1... | collective-permute-start | bytes 1671176 | tf_op jit(solution)/shard_map/ppermute | solution.py:173
  75.5 19.9 %collective-permute-start.23 = (bf16[272,1024]{1,0:T(8,128)(2,1)S(1)}, bf16[272,1024]{1,0:T(8,128)(2,1)S(1)}, u32[]{:S(2)}, u32[]{:S(2)}) collective-permute-start(bf16[272,1024]{1,0:T(8,128)(2,1)S(1)} %broadcast_select_fusion.refs_1_), channel_id=1, source_target_pairs={{0,4},{4,0},{1,5},{5,1},{2,6},{6,2},{3,7},{7,3},{8,12},{12,8},{9,1... | collective-permute-start | bytes 1671176 | tf_op jit(solution)/shard_map/ppermute | solution.py:173
  77.1 18.3 %collective-permute-start.20 = (bf16[128,1024]{1,0:T(8,128)(2,1)S(1)}, bf16[128,1024]{1,0:T(8,128)(2,1)S(1)}, u32[]{:S(2)}, u32[]{:S(2)}) collective-permute-start(bf16[128,1024]{1,0:T(8,128)(2,1)S(1)} %slice.80), channel_id=1, source_target_pairs={{0,4},{4,0},{1,5},{5,1},{2,6},{6,2},{3,7},{7,3},{8,12},{12,8},{9,1... | collective-permute-start | bytes 786440 | tf_op jit(solution)/shard_map/ppermute | solution.py:173
  77.6 17.8 %collective-permute-start.21 = (bf16[128,1024]{1,0:T(8,128)(2,1)S(1)}, bf16[128,1024]{1,0:T(8,128)(2,1)S(1)}, u32[]{:S(2)}, u32[]{:S(2)}) collective-permute-start(bf16[128,1024]{1,0:T(8,128)(2,1)S(1)} %slice.81), channel_id=1, source_target_pairs={{0,2},{2,0},{1,3},{3,1},{4,6},{6,4},{5,7},{7,5},{8,10},{10,8},{9,1... | collective-permute-start | bytes 786440 | tf_op jit(solution)/shard_map/ppermute | solution.py:173
  99.1 15.1 %collective-permute-start.29 = (bf16[128,1024]{1,0:T(8,128)(2,1)S(1)}, bf16[128,1024]{1,0:T(8,128)(2,1)S(1)}, u32[]{:S(2)}, u32[]{:S(2)}) collective-permute-start(bf16[128,1024]{1,0:T(8,128)(2,1)S(1)} %slice.82), channel_id=1, source_target_pairs={{0,4},{4,0},{1,5},{5,1},{2,6},{6,2},{3,7},{7,3},{8,12},{12,8},{9,1... | collective-permute-start | bytes 786440 | tf_op jit(solution)/shard_map/ppermute | solution.py:173
  100.7 13.6 %collective-permute-start.30 = (bf16[128,1024]{1,0:T(8,128)(2,1)S(1)}, bf16[128,1024]{1,0:T(8,128)(2,1)S(1)}, u32[]{:S(2)}, u32[]{:S(2)}) collective-permute-start(bf16[128,1024]{1,0:T(8,128)(2,1)S(1)} %slice.83), channel_id=1, source_target_pairs={{0,2},{2,0},{1,3},{3,1},{4,6},{6,4},{5,7},{7,5},{8,10},{10,8},{9,1... | collective-permute-start | bytes 786440 | tf_op jit(solution)/shard_map/ppermute | solution.py:173
  101.9 12.3 %collective-permute-start.31 = (bf16[1,2,72,1024]{3,2,1,0:T(8,128)(2,1)S(1)}, bf16[1,2,72,1024]{3,2,1,0:T(8,128)(2,1)S(1)}, u32[]{:S(2)}, u32[]{:S(2)}) collective-permute-start(bf16[1,2,72,1024]{3,2,1,0:T(8,128)(2,1)S(1)} %get-tuple-element.89), channel_id=1, source_target_pairs={{0,4},{4,0},{1,5},{5,1},{2,6},{6,2},{3,7},{7,3},{8,12},{12,8},{9,1... | collective-permute-start | bytes 884744 | tf_op jit(solution)/shard_map/ppermute | solution.py:173
  102.7 12.5 %collective-permute-start.32 = (bf16[2,1,72,1024]{3,2,1,0:T(8,128)(2,1)S(1)}, bf16[2,1,72,1024]{3,2,1,0:T(8,128)(2,1)S(1)}, u32[]{:S(2)}, u32[]{:S(2)}) collective-permute-start(bf16[2,1,72,1024]{3,2,1,0:T(8,128)(2,1)S(1)} %get-tuple-element.90), channel_id=1, source_target_pairs={{0,2},{2,0},{1,3},{3,1},{4,6},{6,4},{5,7},{7,5},{8,10},{10,8},{9,1... | collective-permute-start | bytes 884744 | tf_op jit(solution)/shard_map/ppermute | solution.py:173
  116.2 9.5 %collective-permute-start.48 = (bf16[128,1024]{1,0:T(8,128)(2,1)S(1)}, bf16[128,1024]{1,0:T(8,128)(2,1)S(1)}, u32[]{:S(2)}, u32[]{:S(2)}) collective-permute-start(bf16[128,1024]{1,0:T(8,128)(2,1)S(1)} %collective-permute-done.29.refs_5_), channel_id=1, source_target_pairs={{0,1},{1,0},{2,3},{3,2},{4,5},{5,4},{6,7},{7,6},{8,9},{9,8},{10,11... | collective-permute-start | bytes 786440 | tf_op jit(solution)/shard_map/ppermute | solution.py:173
  120.0 18.7 %collective-permute-start.40 = (bf16[1,1,72,1024]{3,2,1,0:T(8,128)(2,1)S(1)}, bf16[1,1,72,1024]{3,2,1,0:T(8,128)(2,1)S(1)}, u32[]{:S(2)}, u32[]{:S(2)}) collective-permute-start(bf16[1,1,72,1024]{3,2,1,0:T(8,128)(2,1)S(1)} %add_convert_fusion.38), channel_id=1, source_target_pairs={{0,2},{2,0},{1,3},{3,1},{4,6},{6,4},{5,7},{7,5},{8,10},{10,8},{9,1... | collective-permute-start | bytes 442376 | tf_op jit(solution)/shard_map/ppermute | solution.py:173
  121.3 17.4 %collective-permute-start.39 = (bf16[2,1,72,1024]{3,2,1,0:T(8,128)(2,1)S(1)}, bf16[2,1,72,1024]{3,2,1,0:T(8,128)(2,1)S(1)}, u32[]{:S(2)}, u32[]{:S(2)}) collective-permute-start(bf16[2,1,72,1024]{3,2,1,0:T(8,128)(2,1)S(1)} %get-tuple-element.129), channel_id=1, source_target_pairs={{0,2},{2,0},{1,3},{3,1},{4,6},{6,4},{5,7},{7,5},{8,10},{10,8},{9,1... | collective-permute-start | bytes 884744 | tf_op jit(solution)/shard_map/ppermute | solution.py:173
  124.7 14.0 %collective-permute-start.38 = (bf16[1,2,72,1024]{3,2,1,0:T(8,128)(2,1)S(1)}, bf16[1,2,72,1024]{3,2,1,0:T(8,128)(2,1)S(1)}, u32[]{:S(2)}, u32[]{:S(2)}) collective-permute-start(bf16[1,2,72,1024]{3,2,1,0:T(8,128)(2,1)S(1)} %get-tuple-element.131), channel_id=1, source_target_pairs={{0,4},{4,0},{1,5},{5,1},{2,6},{6,2},{3,7},{7,3},{8,12},{12,8},{9,1... | collective-permute-start | bytes 884744 | tf_op jit(solution)/shard_map/ppermute | solution.py:173
  125.7 13.6 %collective-permute-start.43 = (bf16[1,2,72,1024]{3,2,1,0:T(8,128)(2,1)S(1)}, bf16[1,2,72,1024]{3,2,1,0:T(8,128)(2,1)S(1)}, u32[]{:S(2)}, u32[]{:S(2)}) collective-permute-start(bf16[1,2,72,1024]{3,2,1,0:T(8,128)(2,1)S(1)} %get-tuple-element.102), channel_id=1, source_target_pairs={{0,4},{4,0},{1,5},{5,1},{2,6},{6,2},{3,7},{7,3},{8,12},{12,8},{9,1... | collective-permute-start | bytes 884744 | tf_op jit(solution)/shard_map/ppermute | solution.py:173
  126.8 12.5 %collective-permute-start.44 = (bf16[2,1,72,1024]{3,2,1,0:T(8,128)(2,1)S(1)}, bf16[2,1,72,1024]{3,2,1,0:T(8,128)(2,1)S(1)}, u32[]{:S(2)}, u32[]{:S(2)}) collective-permute-start(bf16[2,1,72,1024]{3,2,1,0:T(8,128)(2,1)S(1)} %get-tuple-element.103), channel_id=1, source_target_pairs={{0,2},{2,0},{1,3},{3,1},{4,6},{6,4},{5,7},{7,5},{8,10},{10,8},{9,1... | collective-permute-start | bytes 884744 | tf_op jit(solution)/shard_map/ppermute | solution.py:173
  148.6 12.3 %collective-permute-start.58 = (bf16[144,1024]{1,0:T(8,128)(2,1)S(1)}, bf16[144,1024]{1,0:T(8,128)(2,1)S(1)}, u32[]{:S(2)}, u32[]{:S(2)}) collective-permute-start(bf16[144,1024]{1,0:T(8,128)(2,1)S(1)} %pad_maximum_fusion.2), channel_id=1, source_target_pairs={{0,16},{8,24},{16,0},{24,8},{1,17},{9,25},{17,1},{25,9},{2,18},{10... | collective-permute-start | bytes 884744 | tf_op jit(solution)/shard_map/ppermute | solution.py:173
  158.0 16.0 %collective-permute-start.50 = (bf16[144,1024]{1,0:T(8,128)(2,1)S(1)}, bf16[144,1024]{1,0:T(8,128)(2,1)S(1)}, u32[]{:S(2)}, u32[]{:S(2)}) collective-permute-start(bf16[144,1024]{1,0:T(8,128)(2,1)S(1)} %pad_maximum_fusion.1), channel_id=1, source_target_pairs={{0,8},{8,0},{16,24},{24,16},{1,9},{9,1},{17,25},{25,17},{2,10},{10... | collective-permute-start | bytes 884744 | tf_op jit(solution)/shard_map/ppermute | solution.py:173
  164.5 12.5 %collective-permute-start.59 = (bf16[144,1024]{1,0:T(8,128)(2,1)S(1)}, bf16[144,1024]{1,0:T(8,128)(2,1)S(1)}, u32[]{:S(2)}, u32[]{:S(2)}) collective-permute-start(bf16[144,1024]{1,0:T(8,128)(2,1)S(1)} %pad_maximum_fusion.3), channel_id=1, source_target_pairs={{0,24},{8,16},{16,8},{24,0},{1,25},{9,17},{17,9},{25,1},{2,26},{10... | collective-permute-start | bytes 884744 | tf_op jit(solution)/shard_map/ppermute | solution.py:173
  (42 other events, 267.4 us)

commit v5 on v4

--- a/solution.py
+++ b/solution.py
@@ -395,7 +395,7 @@
                 else:
                     ready.append(s.half)
             elif s.todo is None:
-                if r >= depths + 3:
+                if r >= depths + 4:
                     s.first()
                     ready += s.step()
                 else:

time: 179 us -> 177 us (0.989)
  waiting for transfers between devices: 65.8 us -> 64 us
  transfers between devices with their start and end apart: 62 -> 62, of which waited for: 26 -> 24; matrix products, arithmetic and copies ran while one was open for 3% -> 3% of each run, Pallas kernels for 24% -> 25%
where the time goes in v5:
time: 177 us
  waiting for transfers between devices  64 us (36%)
  starting transfers between devices  50.7 us (29%)
  Pallas kernels  43.6 us (25%)
  local copies, waits for them, and re-layouts  9.62 us (5%)
  other arithmetic  7.51 us (4%)
    ppermute x58, waiting for transfers between devices, exchange(): lax.ppermute(x, axis, [(i, i ^ step) for i in range(lax.axis_size(axis))])  60.9 us
    pallas_call x4, Pallas kernels, expert_call(): pl.pallas_call(functools.partial(expert_kernel, (at, out_at, len(pieces),...  43.6 us
    ppermute x58, starting transfers between devices, exchange(): lax.ppermute(x, axis, [(i, i ^ step) for i in range(lax.axis_size(axis))])  40.1 us
    ppermute x4, starting transfers between devices, passed(): return lax.ppermute(x, axis, pairs)  10.6 us
    unnamed x24, local copies, waits for them, and re-layouts  8.67 us
  transfers between devices with their start and end apart: 62, of which 24 were waited for; matrix products, arithmetic and copies ran while one was open for 3% of the time, Pallas kernels for 25%

profile of v5, /device:TPU:8, one launch (start us, length us, event | category | flops | bytes accessed | tf_op | source)
XLA Modules:
  0.0 176.7 jit_solution(17559098246087162904)
XLA Ops:
  2.5 5.0 %collective-permute-start.1 = (bf16[272,1024]{1,0:T(8,128)(2,1)S(1)}, bf16[272,1024]{1,0:T(8,128)(2,1)}, u32[]{:S(2)}, u32[]{:S(2)}) collective-permute-start(bf16[272,1024]{1,0:T(8,128)(2,1)S(1)} %pad_maximum_fusion.refs_1_), channel_id=1, source_target_pairs={{8,16},{16,8},{9,17},{17,9},{10,18},{18,10},{11,19},{19,11},{12,20... | collective-permute-start | bytes 1671176 | tf_op jit(solution)/shard_map/ppermute | solution.py:177
  7.6 1.6 collective-permute-start.2
  9.1 1.5 collective-permute-start.3
  10.6 6.2 %collective-permute-done.refs_1_ = bf16[272,1024]{1,0:T(8,128)(2,1)S(1)} collective-permute-done((bf16[272,1024]{1,0:T(8,128)(2,1)S(1)}, bf16[272,1024]{1,0:T(8,128)(2,1)S(1)}, u32[]{:S(2)}, u32[]{:S(2)}) %collective-permute-start) | collective-permute-done | bytes 557088 | tf_op jit(solution)/shard_map/ppermute | solution.py:173
  16.9 3.1 %collective-permute-done.1 = bf16[272,1024]{1,0:T(8,128)(2,1)} collective-permute-done((bf16[272,1024]{1,0:T(8,128)(2,1)S(1)}, bf16[272,1024]{1,0:T(8,128)(2,1)}, u32[]{:S(2)}, u32[]{:S(2)}) %collective-permute-start.1) | collective-permute-done | bytes 557088 | tf_op jit(solution)/shard_map/ppermute | solution.py:177
  20.0 1.4 collective-permute-done.2.refs_2_
  22.7 2.2 %collective-permute-start.5 = (bf16[272,1024]{1,0:T(8,128)(2,1)S(1)}, bf16[272,1024]{1,0:T(8,128)(2,1)S(1)}, u32[]{:S(2)}, u32[]{:S(2)}) collective-permute-start(bf16[272,1024]{1,0:T(8,128)(2,1)S(1)} %collective-permute-done.refs_1_), channel_id=1, source_target_pairs={{8,16},{16,8},{9,17},{17,9},{10,18},{18,10},{11,19},{19,11},{12,20... | collective-permute-start | bytes 1671176 | tf_op jit(solution)/shard_map/ppermute | solution.py:177
  25.5 1.6 collective-permute-start.6
  27.6 2.1 %collective-permute-start.4 = (bf16[272,1024]{1,0:T(8,128)(2,1)}, bf16[272,1024]{1,0:T(8,128)(2,1)}, u32[]{:S(2)}, u32[]{:S(2)}) collective-permute-start(bf16[272,1024]{1,0:T(8,128)(2,1)} %collective-permute-done.1), channel_id=1, source_target_pairs={{8,0},{16,24},{9,1},{17,25},{10,2},{18,26},{11,3},{19,27},{12,4},{... | collective-permute-start | bytes 1671176 | tf_op jit(solution)/shard_map/ppermute | solution.py:177
  29.7 5.1 %collective-permute-done.6.refs_5_ = bf16[128,1024]{1,0:T(8,128)(2,1)S(1)} collective-permute-done((bf16[128,1024]{1,0:T(8,128)(2,1)S(1)}, bf16[128,1024]{1,0:T(8,128)(2,1)S(1)}, u32[]{:S(2)}, u32[]{:S(2)}) %collective-permute-start.6) | collective-permute-done | bytes 262176 | tf_op jit(solution)/shard_map/ppermute | solution.py:173
  34.8 1.5 collective-permute-start.7
  36.3 7.0 %collective-permute-done.7.refs_6_ = bf16[128,1024]{1,0:T(8,128)(2,1)S(1)} collective-permute-done((bf16[128,1024]{1,0:T(8,128)(2,1)S(1)}, bf16[128,1024]{1,0:T(8,128)(2,1)S(1)}, u32[]{:S(2)}, u32[]{:S(2)}) %collective-permute-start.7) | collective-permute-done | bytes 262176 | tf_op jit(solution)/shard_map/ppermute | solution.py:173
  47.7 1.5 collective-permute-start.13
  51.4 2.8 %copy-done = bf16[2,384,4096]{2,1,0:T(8,128)(2,1)S(1)} copy-done((bf16[2,384,4096]{2,1,0:T(8,128)(2,1)S(1)}, bf16[2,384,4096]{2,1,0:T(8,128)(2,1)}, u32[]{:S(2)}) %copy-start) | copy-done | bytes 6291480
  54.2 2.8 %copy-done.1 = bf16[2,384,4096]{2,1,0:T(8,128)(2,1)S(1)} copy-done((bf16[2,384,4096]{2,1,0:T(8,128)(2,1)S(1)}, bf16[2,384,4096]{2,1,0:T(8,128)(2,1)}, u32[]{:S(2)}) %copy-start.1) | copy-done | bytes 6291480
  57.0 2.8 %copy-done.2 = bf16[2,384,4096]{2,1,0:T(8,128)(2,1)S(1)} copy-done((bf16[2,384,4096]{2,1,0:T(8,128)(2,1)S(1)}, bf16[2,384,4096]{2,1,0:T(8,128)(2,1)}, u32[]{:S(2)}) %copy-start.2) | copy-done | bytes 6291480
  59.8 11.5 %shard_map.86 = (bf16[4,144,1024]{2,1,0:T(8,128)(2,1)S(1)}, bf16[4,144,1024]{2,1,0:T(8,128)(2,1)S(1)}) custom-call(s32[5]{0:T(128)S(1)} %stack.23.refs_0_, bf16[272,1024]{1,0:T(8,128)(2,1)S(1)} %pad_maximum_fusion.refs_1_, bf16[272,1024]{1,0:T(8,128)(2,1)S(1)} %collective-permute-done.2.refs_2_, bf16[272,1024]{1,0:T(8,128)(2,1)S(1)} %collective-permute-done.3.refs_3_, ...), custom_call_target="tpu_custom_call" | custom-call | flops 8053063680 | bytes 18874368 | tf_op jit(solution)/shard_map/pallas_call | solution.py:124
  75.5 1.5 collective-permute-start.23
  78.8 10.7 %shard_map.87 = (bf16[4,144,1024]{2,1,0:T(8,128)(2,1)S(1)}, bf16[4,144,1024]{2,1,0:T(8,128)(2,1)S(1)}) custom-call(s32[5]{0:T(128)S(1)} %stack.23.refs_0_, bf16[272,1024]{1,0:T(8,128)(2,1)S(1)} %collective-permute-done.refs_1_, bf16[272,1024]{1,0:T(8,128)(2,1)S(1)} %collective-permute-done.8.refs_2_, bf16[272,1024]{1,0:T(8,128)(2,1)S(1)} %collective-permute-done.9.refs_3_, ...), custom_call_target="tpu_custom_call" | custom-call | flops 8053063680 | bytes 18874368 | tf_op jit(solution)/shard_map/pallas_call | solution.py:124
  89.5 5.9 %collective-permute-done.20.refs_5_ = bf16[128,1024]{1,0:T(8,128)(2,1)S(1)} collective-permute-done((bf16[128,1024]{1,0:T(8,128)(2,1)S(1)}, bf16[128,1024]{1,0:T(8,128)(2,1)S(1)}, u32[]{:S(2)}, u32[]{:S(2)}) %collective-permute-start.20) | collective-permute-done | bytes 262176 | tf_op jit(solution)/shard_map/ppermute | solution.py:173
  96.6 1.7 collective-permute-done.28
  99.1 1.5 collective-permute-start.29
  103.5 10.7 %shard_map.88 = (bf16[4,144,1024]{2,1,0:T(8,128)(2,1)S(1)}, bf16[4,144,1024]{2,1,0:T(8,128)(2,1)S(1)}) custom-call(s32[5]{0:T(128)S(1)} %stack.23.refs_0_, bf16[272,1024]{1,0:T(8,128)(2,1)S(1)} %broadcast_select_fusion.1.refs_1_, bf16[272,1024]{1,0:T(8,128)(2,1)S(1)} %collective-permute-done.12.refs_2_, ...), custom_call_target="tpu_custom_call" | custom-call | flops 8053063680 | bytes 18874368 | tf_op jit(solution)/shard_map/pallas_call | solution.py:124
  116.3 1.7 collective-permute-done.40
  122.9 10.7 %shard_map.89 = (bf16[4,144,1024]{2,1,0:T(8,128)(2,1)S(1)}, bf16[4,144,1024]{2,1,0:T(8,128)(2,1)S(1)}) custom-call(s32[5]{0:T(128)S(1)} %stack.23.refs_0_, bf16[272,1024]{1,0:T(8,128)(2,1)S(1)} %broadcast_select_fusion.refs_1_, bf16[272,1024]{1,0:T(8,128)(2,1)S(1)} %collective-permute-done.22.refs_2_, bf16[272,1024]{1,0:T(8,128)(2,1)S(1)} %collective-permute-done.23.refs_3_, ...), custom_call_target="tpu_custom_call" | custom-call | flops 8053063680 | bytes 18874368 | tf_op jit(solution)/shard_map/pallas_call | solution.py:124
  138.6 1.9 %collective-permute-done.51 = bf16[1,1,72,1024]{3,2,1,0:T(8,128)(2,1)S(1)} collective-permute-done((bf16[1,1,72,1024]{3,2,1,0:T(8,128)(2,1)S(1)}, bf16[1,1,72,1024]{3,2,1,0:T(8,128)(2,1)S(1)}, u32[]{:S(2)}, u32[]{:S(2)}) %collective-permute-start.51) | collective-permute-done | bytes 147488 | tf_op jit(solution)/shard_map/ppermute | solution.py:173
  143.5 3.3 %collective-permute-done.50 = bf16[2,1,72,1024]{3,2,1,0:T(8,128)(2,1)S(1)} collective-permute-done((bf16[2,1,72,1024]{3,2,1,0:T(8,128)(2,1)S(1)}, bf16[2,1,72,1024]{3,2,1,0:T(8,128)(2,1)S(1)}, u32[]{:S(2)}, u32[]{:S(2)}) %collective-permute-start.50) | collective-permute-done | bytes 294944 | tf_op jit(solution)/shard_map/ppermute | solution.py:173
  148.2 4.5 %collective-permute-done.55 = bf16[2,1,72,1024]{3,2,1,0:T(8,128)(2,1)S(1)} collective-permute-done((bf16[2,1,72,1024]{3,2,1,0:T(8,128)(2,1)S(1)}, bf16[2,1,72,1024]{3,2,1,0:T(8,128)(2,1)S(1)}, u32[]{:S(2)}, u32[]{:S(2)}) %collective-permute-start.55) | collective-permute-done | bytes 294944 | tf_op jit(solution)/shard_map/ppermute | solution.py:173
  156.0 3.1 %collective-permute-done.57 = bf16[1,1,72,1024]{3,2,1,0:T(8,128)(2,1)S(1)} collective-permute-done((bf16[1,1,72,1024]{3,2,1,0:T(8,128)(2,1)S(1)}, bf16[1,1,72,1024]{3,2,1,0:T(8,128)(2,1)S(1)}, u32[]{:S(2)}, u32[]{:S(2)}) %collective-permute-start.57) | collective-permute-done | bytes 147488 | tf_op jit(solution)/shard_map/ppermute | solution.py:173
  162.3 1.4 collective-permute-start.59
  163.8 1.6 collective-permute-done.61
  166.7 8.4 %collective-permute-done.59 = bf16[144,1024]{1,0:T(8,128)(2,1)S(1)} collective-permute-done((bf16[144,1024]{1,0:T(8,128)(2,1)S(1)}, bf16[144,1024]{1,0:T(8,128)(2,1)S(1)}, u32[]{:S(2)}, u32[]{:S(2)}) %collective-permute-start.59) | collective-permute-done | bytes 294944 | tf_op jit(solution)/shard_map/ppermute | solution.py:173
  (163 shorter events, 47.1 us)
Async XLA Ops:
  2.4 14.4 %collective-permute-start = (bf16[272,1024]{1,0:T(8,128)(2,1)S(1)}, bf16[272,1024]{1,0:T(8,128)(2,1)S(1)}, u32[]{:S(2)}, u32[]{:S(2)}) collective-permute-start(bf16[272,1024]{1,0:T(8,128)(2,1)S(1)} %pad_maximum_fusion.refs_1_), channel_id=1, source_target_pairs={{0,8},{8,0},{16,24},{24,16},{1,9},{9,1},{17,25},{25,17},{2,10},{10... | collective-permute-start | bytes 1671176 | tf_op jit(solution)/shard_map/ppermute | solution.py:173
  2.5 17.5 %collective-permute-start.1 = (bf16[272,1024]{1,0:T(8,128)(2,1)S(1)}, bf16[272,1024]{1,0:T(8,128)(2,1)}, u32[]{:S(2)}, u32[]{:S(2)}) collective-permute-start(bf16[272,1024]{1,0:T(8,128)(2,1)S(1)} %pad_maximum_fusion.refs_1_), channel_id=1, source_target_pairs={{8,16},{16,8},{9,17},{17,9},{10,18},{18,10},{11,19},{19,11},{12,20... | collective-permute-start | bytes 1671176 | tf_op jit(solution)/shard_map/ppermute | solution.py:177
  7.6 13.9 %collective-permute-start.2 = (bf16[272,1024]{1,0:T(8,128)(2,1)S(1)}, bf16[272,1024]{1,0:T(8,128)(2,1)S(1)}, u32[]{:S(2)}, u32[]{:S(2)}) collective-permute-start(bf16[272,1024]{1,0:T(8,128)(2,1)S(1)} %pad_maximum_fusion.refs_1_), channel_id=1, source_target_pairs={{0,2},{2,0},{1,3},{3,1},{4,6},{6,4},{5,7},{7,5},{8,10},{10,8},{9,1... | collective-permute-start | bytes 1671176 | tf_op jit(solution)/shard_map/ppermute | solution.py:173
  9.1 13.5 %collective-permute-start.3 = (bf16[272,1024]{1,0:T(8,128)(2,1)S(1)}, bf16[272,1024]{1,0:T(8,128)(2,1)S(1)}, u32[]{:S(2)}, u32[]{:S(2)}) collective-permute-start(bf16[272,1024]{1,0:T(8,128)(2,1)S(1)} %pad_maximum_fusion.refs_1_), channel_id=1, source_target_pairs={{0,4},{4,0},{1,5},{5,1},{2,6},{6,2},{3,7},{7,3},{8,12},{12,8},{9,1... | collective-permute-start | bytes 1671176 | tf_op jit(solution)/shard_map/ppermute | solution.py:173
  22.7 20.6 %collective-permute-start.5 = (bf16[272,1024]{1,0:T(8,128)(2,1)S(1)}, bf16[272,1024]{1,0:T(8,128)(2,1)S(1)}, u32[]{:S(2)}, u32[]{:S(2)}) collective-permute-start(bf16[272,1024]{1,0:T(8,128)(2,1)S(1)} %collective-permute-done.refs_1_), channel_id=1, source_target_pairs={{8,16},{16,8},{9,17},{17,9},{10,18},{18,10},{11,19},{19,11},{12,20... | collective-permute-start | bytes 1671176 | tf_op jit(solution)/shard_map/ppermute | solution.py:177
  24.9 18.9 %collective-permute-start.8 = (bf16[272,1024]{1,0:T(8,128)(2,1)S(1)}, bf16[272,1024]{1,0:T(8,128)(2,1)S(1)}, u32[]{:S(2)}, u32[]{:S(2)}) collective-permute-start(bf16[272,1024]{1,0:T(8,128)(2,1)S(1)} %collective-permute-done.refs_1_), channel_id=1, source_target_pairs={{0,2},{2,0},{1,3},{3,1},{4,6},{6,4},{5,7},{7,5},{8,10},{10,8},{9,1... | collective-permute-start | bytes 1671176 | tf_op jit(solution)/shard_map/ppermute | solution.py:173
  27.1 17.2 %collective-permute-start.9 = (bf16[272,1024]{1,0:T(8,128)(2,1)S(1)}, bf16[272,1024]{1,0:T(8,128)(2,1)S(1)}, u32[]{:S(2)}, u32[]{:S(2)}) collective-permute-start(bf16[272,1024]{1,0:T(8,128)(2,1)S(1)} %collective-permute-done.refs_1_), channel_id=1, source_target_pairs={{0,4},{4,0},{1,5},{5,1},{2,6},{6,2},{3,7},{7,3},{8,12},{12,8},{9,1... | collective-permute-start | bytes 1671176 | tf_op jit(solution)/shard_map/ppermute | solution.py:173
  27.6 16.7 %collective-permute-start.4 = (bf16[272,1024]{1,0:T(8,128)(2,1)}, bf16[272,1024]{1,0:T(8,128)(2,1)}, u32[]{:S(2)}, u32[]{:S(2)}) collective-permute-start(bf16[272,1024]{1,0:T(8,128)(2,1)} %collective-permute-done.1), channel_id=1, source_target_pairs={{8,0},{16,24},{9,1},{17,25},{10,2},{18,26},{11,3},{19,27},{12,4},{... | collective-permute-start | bytes 1671176 | tf_op jit(solution)/shard_map/ppermute | solution.py:177
  45.9 28.7 %collective-permute-start.24 = (bf16[272,1024]{1,0:T(8,128)(2,1)S(1)}, bf16[272,1024]{1,0:T(8,128)(2,1)S(1)}, u32[]{:S(2)}, u32[]{:S(2)}) collective-permute-start(bf16[272,1024]{1,0:T(8,128)(2,1)S(1)} %collective-permute-done.refs_1_), channel_id=1, source_target_pairs={{0,1},{1,0},{2,3},{3,2},{4,5},{5,4},{6,7},{7,6},{8,9},{9,8},{10,11... | collective-permute-start | bytes 1671176 | tf_op jit(solution)/shard_map/ppermute | solution.py:173
  46.4 24.9 %collective-permute-start.12 = (bf16[272,1024]{1,0:T(8,128)(2,1)S(1)}, bf16[272,1024]{1,0:T(8,128)(2,1)S(1)}, u32[]{:S(2)}, u32[]{:S(2)}) collective-permute-start(bf16[272,1024]{1,0:T(8,128)(2,1)S(1)} %broadcast_select_fusion.1.refs_1_), channel_id=1, source_target_pairs={{0,2},{2,0},{1,3},{3,1},{4,6},{6,4},{5,7},{7,5},{8,10},{10,8},{9,1... | collective-permute-start | bytes 1671176 | tf_op jit(solution)/shard_map/ppermute | solution.py:173
  47.7 23.7 %collective-permute-start.13 = (bf16[272,1024]{1,0:T(8,128)(2,1)S(1)}, bf16[272,1024]{1,0:T(8,128)(2,1)S(1)}, u32[]{:S(2)}, u32[]{:S(2)}) collective-permute-start(bf16[272,1024]{1,0:T(8,128)(2,1)S(1)} %broadcast_select_fusion.1.refs_1_), channel_id=1, source_target_pairs={{0,4},{4,0},{1,5},{5,1},{2,6},{6,2},{3,7},{7,3},{8,12},{12,8},{9,1... | collective-permute-start | bytes 1671176 | tf_op jit(solution)/shard_map/ppermute | solution.py:173
  49.2 23.8 %collective-permute-start.10 = (bf16[272,1024]{1,0:T(8,128)(2,1)S(1)}, bf16[272,1024]{1,0:T(8,128)(2,1)S(1)}, u32[]{:S(2)}, u32[]{:S(2)}) collective-permute-start(bf16[272,1024]{1,0:T(8,128)(2,1)S(1)} %copy-done.8), channel_id=1, source_target_pairs={{8,0},{16,24},{9,1},{17,25},{10,2},{18,26},{11,3},{19,27},{12,4},{... | collective-permute-start | bytes 1671176 | tf_op jit(solution)/shard_map/ppermute | solution.py:177
  50.6 22.4 %collective-permute-start.11 = (bf16[272,1024]{1,0:T(8,128)(2,1)S(1)}, bf16[272,1024]{1,0:T(8,128)(2,1)S(1)}, u32[]{:S(2)}, u32[]{:S(2)}) collective-permute-start(bf16[272,1024]{1,0:T(8,128)(2,1)S(1)} %collective-permute-done.9.refs_3_), channel_id=1, source_target_pairs={{0,2},{2,0},{1,3},{3,1},{4,6},{6,4},{5,7},{7,5},{8,10},{10,8},{9,1... | collective-permute-start | bytes 1671176 | tf_op jit(solution)/shard_map/ppermute | solution.py:173
  73.0 22.4 %collective-permute-start.19 = (bf16[4,144,1024]{2,1,0:T(8,128)(2,1)S(1)}, bf16[4,144,1024]{2,1,0:T(8,128)(2,1)S(1)}, u32[]{:S(2)}, u32[]{:S(2)}) collective-permute-start(bf16[4,144,1024]{2,1,0:T(8,128)(2,1)S(1)} %get-tuple-element.75), channel_id=1, source_target_pairs={{0,1},{1,0},{2,3},{3,2},{4,5},{5,4},{6,7},{7,6},{8,9},{9,8},{10,11... | collective-permute-start | bytes 3538952 | tf_op jit(solution)/shard_map/ppermute | solution.py:173
  74.7 20.7 %collective-permute-start.22 = (bf16[272,1024]{1,0:T(8,128)(2,1)S(1)}, bf16[272,1024]{1,0:T(8,128)(2,1)S(1)}, u32[]{:S(2)}, u32[]{:S(2)}) collective-permute-start(bf16[272,1024]{1,0:T(8,128)(2,1)S(1)} %broadcast_select_fusion.refs_1_), channel_id=1, source_target_pairs={{0,2},{2,0},{1,3},{3,1},{4,6},{6,4},{5,7},{7,5},{8,10},{10,8},{9,1... | collective-permute-start | bytes 1671176 | tf_op jit(solution)/shard_map/ppermute | solution.py:173
  75.5 19.9 %collective-permute-start.23 = (bf16[272,1024]{1,0:T(8,128)(2,1)S(1)}, bf16[272,1024]{1,0:T(8,128)(2,1)S(1)}, u32[]{:S(2)}, u32[]{:S(2)}) collective-permute-start(bf16[272,1024]{1,0:T(8,128)(2,1)S(1)} %broadcast_select_fusion.refs_1_), channel_id=1, source_target_pairs={{0,4},{4,0},{1,5},{5,1},{2,6},{6,2},{3,7},{7,3},{8,12},{12,8},{9,1... | collective-permute-start | bytes 1671176 | tf_op jit(solution)/shard_map/ppermute | solution.py:173
  77.1 18.3 %collective-permute-start.20 = (bf16[128,1024]{1,0:T(8,128)(2,1)S(1)}, bf16[128,1024]{1,0:T(8,128)(2,1)S(1)}, u32[]{:S(2)}, u32[]{:S(2)}) collective-permute-start(bf16[128,1024]{1,0:T(8,128)(2,1)S(1)} %slice.80), channel_id=1, source_target_pairs={{0,4},{4,0},{1,5},{5,1},{2,6},{6,2},{3,7},{7,3},{8,12},{12,8},{9,1... | collective-permute-start | bytes 786440 | tf_op jit(solution)/shard_map/ppermute | solution.py:173
  77.6 17.8 %collective-permute-start.21 = (bf16[128,1024]{1,0:T(8,128)(2,1)S(1)}, bf16[128,1024]{1,0:T(8,128)(2,1)S(1)}, u32[]{:S(2)}, u32[]{:S(2)}) collective-permute-start(bf16[128,1024]{1,0:T(8,128)(2,1)S(1)} %slice.81), channel_id=1, source_target_pairs={{0,2},{2,0},{1,3},{3,1},{4,6},{6,4},{5,7},{7,5},{8,10},{10,8},{9,1... | collective-permute-start | bytes 786440 | tf_op jit(solution)/shard_map/ppermute | solution.py:173
  99.1 15.1 %collective-permute-start.29 = (bf16[128,1024]{1,0:T(8,128)(2,1)S(1)}, bf16[128,1024]{1,0:T(8,128)(2,1)S(1)}, u32[]{:S(2)}, u32[]{:S(2)}) collective-permute-start(bf16[128,1024]{1,0:T(8,128)(2,1)S(1)} %slice.82), channel_id=1, source_target_pairs={{0,4},{4,0},{1,5},{5,1},{2,6},{6,2},{3,7},{7,3},{8,12},{12,8},{9,1... | collective-permute-start | bytes 786440 | tf_op jit(solution)/shard_map/ppermute | solution.py:173
  100.7 13.6 %collective-permute-start.30 = (bf16[128,1024]{1,0:T(8,128)(2,1)S(1)}, bf16[128,1024]{1,0:T(8,128)(2,1)S(1)}, u32[]{:S(2)}, u32[]{:S(2)}) collective-permute-start(bf16[128,1024]{1,0:T(8,128)(2,1)S(1)} %slice.83), channel_id=1, source_target_pairs={{0,2},{2,0},{1,3},{3,1},{4,6},{6,4},{5,7},{7,5},{8,10},{10,8},{9,1... | collective-permute-start | bytes 786440 | tf_op jit(solution)/shard_map/ppermute | solution.py:173
  101.9 12.3 %collective-permute-start.31 = (bf16[1,2,72,1024]{3,2,1,0:T(8,128)(2,1)S(1)}, bf16[1,2,72,1024]{3,2,1,0:T(8,128)(2,1)S(1)}, u32[]{:S(2)}, u32[]{:S(2)}) collective-permute-start(bf16[1,2,72,1024]{3,2,1,0:T(8,128)(2,1)S(1)} %get-tuple-element.88), channel_id=1, source_target_pairs={{0,4},{4,0},{1,5},{5,1},{2,6},{6,2},{3,7},{7,3},{8,12},{12,8},{9,1... | collective-permute-start | bytes 884744 | tf_op jit(solution)/shard_map/ppermute | solution.py:173
  102.7 12.5 %collective-permute-start.32 = (bf16[2,1,72,1024]{3,2,1,0:T(8,128)(2,1)S(1)}, bf16[2,1,72,1024]{3,2,1,0:T(8,128)(2,1)S(1)}, u32[]{:S(2)}, u32[]{:S(2)}) collective-permute-start(bf16[2,1,72,1024]{3,2,1,0:T(8,128)(2,1)S(1)} %get-tuple-element.89), channel_id=1, source_target_pairs={{0,2},{2,0},{1,3},{3,1},{4,6},{6,4},{5,7},{7,5},{8,10},{10,8},{9,1... | collective-permute-start | bytes 884744 | tf_op jit(solution)/shard_map/ppermute | solution.py:173
  118.8 14.8 %collective-permute-start.39 = (bf16[1,1,72,1024]{3,2,1,0:T(8,128)(2,1)S(1)}, bf16[1,1,72,1024]{3,2,1,0:T(8,128)(2,1)S(1)}, u32[]{:S(2)}, u32[]{:S(2)}) collective-permute-start(bf16[1,1,72,1024]{3,2,1,0:T(8,128)(2,1)S(1)} %add_convert_fusion.37), channel_id=1, source_target_pairs={{0,4},{4,0},{1,5},{5,1},{2,6},{6,2},{3,7},{7,3},{8,12},{12,8},{9,1... | collective-permute-start | bytes 442376 | tf_op jit(solution)/shard_map/ppermute | solution.py:173
  119.8 13.8 %collective-permute-start.38 = (bf16[1,1,72,1024]{3,2,1,0:T(8,128)(2,1)S(1)}, bf16[1,1,72,1024]{3,2,1,0:T(8,128)(2,1)S(1)}, u32[]{:S(2)}, u32[]{:S(2)}) collective-permute-start(bf16[1,1,72,1024]{3,2,1,0:T(8,128)(2,1)S(1)} %add_convert_fusion.38), channel_id=1, source_target_pairs={{0,2},{2,0},{1,3},{3,1},{4,6},{6,4},{5,7},{7,5},{8,10},{10,8},{9,1... | collective-permute-start | bytes 442376 | tf_op jit(solution)/shard_map/ppermute | solution.py:173
  121.0 12.6 %collective-permute-start.41 = (bf16[1,2,72,1024]{3,2,1,0:T(8,128)(2,1)S(1)}, bf16[1,2,72,1024]{3,2,1,0:T(8,128)(2,1)S(1)}, u32[]{:S(2)}, u32[]{:S(2)}) collective-permute-start(bf16[1,2,72,1024]{3,2,1,0:T(8,128)(2,1)S(1)} %get-tuple-element.100), channel_id=1, source_target_pairs={{0,4},{4,0},{1,5},{5,1},{2,6},{6,2},{3,7},{7,3},{8,12},{12,8},{9,1... | collective-permute-start | bytes 884744 | tf_op jit(solution)/shard_map/ppermute | solution.py:173
  122.1 11.5 %collective-permute-start.42 = (bf16[2,1,72,1024]{3,2,1,0:T(8,128)(2,1)S(1)}, bf16[2,1,72,1024]{3,2,1,0:T(8,128)(2,1)S(1)}, u32[]{:S(2)}, u32[]{:S(2)}) collective-permute-start(bf16[2,1,72,1024]{3,2,1,0:T(8,128)(2,1)S(1)} %get-tuple-element.101), channel_id=1, source_target_pairs={{0,2},{2,0},{1,3},{3,1},{4,6},{6,4},{5,7},{7,5},{8,10},{10,8},{9,1... | collective-permute-start | bytes 884744 | tf_op jit(solution)/shard_map/ppermute | solution.py:173
  137.4 10.8 %collective-permute-start.49 = (bf16[1,2,72,1024]{3,2,1,0:T(8,128)(2,1)S(1)}, bf16[1,2,72,1024]{3,2,1,0:T(8,128)(2,1)S(1)}, u32[]{:S(2)}, u32[]{:S(2)}) collective-permute-start(bf16[1,2,72,1024]{3,2,1,0:T(8,128)(2,1)S(1)} %get-tuple-element.129), channel_id=1, source_target_pairs={{0,4},{4,0},{1,5},{5,1},{2,6},{6,2},{3,7},{7,3},{8,12},{12,8},{9,1... | collective-permute-start | bytes 884744 | tf_op jit(solution)/shard_map/ppermute | solution.py:173
  140.8 11.9 %collective-permute-start.55 = (bf16[2,1,72,1024]{3,2,1,0:T(8,128)(2,1)S(1)}, bf16[2,1,72,1024]{3,2,1,0:T(8,128)(2,1)S(1)}, u32[]{:S(2)}, u32[]{:S(2)}) collective-permute-start(bf16[2,1,72,1024]{3,2,1,0:T(8,128)(2,1)S(1)} %get-tuple-element.131), channel_id=1, source_target_pairs={{0,2},{2,0},{1,3},{3,1},{4,6},{6,4},{5,7},{7,5},{8,10},{10,8},{9,1... | collective-permute-start | bytes 884744 | tf_op jit(solution)/shard_map/ppermute | solution.py:173
  142.3 11.5 %collective-permute-start.54 = (bf16[1,2,72,1024]{3,2,1,0:T(8,128)(2,1)S(1)}, bf16[1,2,72,1024]{3,2,1,0:T(8,128)(2,1)S(1)}, u32[]{:S(2)}, u32[]{:S(2)}) collective-permute-start(bf16[1,2,72,1024]{3,2,1,0:T(8,128)(2,1)S(1)} %get-tuple-element.133), channel_id=1, source_target_pairs={{0,4},{4,0},{1,5},{5,1},{2,6},{6,2},{3,7},{7,3},{8,12},{12,8},{9,1... | collective-permute-start | bytes 884744 | tf_op jit(solution)/shard_map/ppermute | solution.py:173
  143.4 12.6 %collective-permute-start.58 = (bf16[144,1024]{1,0:T(8,128)(2,1)S(1)}, bf16[144,1024]{1,0:T(8,128)(2,1)S(1)}, u32[]{:S(2)}, u32[]{:S(2)}) collective-permute-start(bf16[144,1024]{1,0:T(8,128)(2,1)S(1)} %pad_maximum_fusion.2), channel_id=1, source_target_pairs={{0,16},{8,24},{16,0},{24,8},{1,17},{9,25},{17,1},{25,9},{2,18},{10... | collective-permute-start | bytes 884744 | tf_op jit(solution)/shard_map/ppermute | solution.py:173
  155.9 10.8 %collective-permute-start.48 = (bf16[144,1024]{1,0:T(8,128)(2,1)S(1)}, bf16[144,1024]{1,0:T(8,128)(2,1)S(1)}, u32[]{:S(2)}, u32[]{:S(2)}) collective-permute-start(bf16[144,1024]{1,0:T(8,128)(2,1)S(1)} %pad_maximum_fusion.1), channel_id=1, source_target_pairs={{0,8},{8,0},{16,24},{24,16},{1,9},{9,1},{17,25},{25,17},{2,10},{10... | collective-permute-start | bytes 884744 | tf_op jit(solution)/shard_map/ppermute | solution.py:173
  162.3 12.8 %collective-permute-start.59 = (bf16[144,1024]{1,0:T(8,128)(2,1)S(1)}, bf16[144,1024]{1,0:T(8,128)(2,1)S(1)}, u32[]{:S(2)}, u32[]{:S(2)}) collective-permute-start(bf16[144,1024]{1,0:T(8,128)(2,1)S(1)} %pad_maximum_fusion.3), channel_id=1, source_target_pairs={{0,24},{8,16},{16,8},{24,0},{1,25},{9,17},{17,9},{25,1},{2,26},{10... | collective-permute-start | bytes 884744 | tf_op jit(solution)/shard_map/ppermute | solution.py:173
  (42 other events, 256.9 us)

commit v6 on v5

--- a/solution.py
+++ b/solution.py
@@ -16,10 +16,14 @@
 
 
 def expert_kernel(plan, *refs):
-    at, out_at, n_in, ndy, ndx, local, experts, rows, tile, wide = plan
+    at, out_at, n_in, ndy, ndx, local, experts, rows, tile, wide, bring = plan
     where = refs[0]
     pieces = refs[1 : 1 + n_in]
-    wg, wu, wd, keep, send, d_gate, d_up, score = refs[1 + n_in :]
+    given, (keep, send) = refs[1 + n_in : 4 + n_in], refs[4 + n_in : 6 + n_in]
+    if bring:
+        wg, wu, wd, d_gate, d_up, score, arrived = refs[6 + n_in :]
+    else:
+        (wg, wu, wd), (d_gate, d_up, score) = given, refs[6 + n_in :]
     width = pieces[0].shape[1]
     units = wg.shape[0]
     hidden = units // local
@@ -40,6 +44,14 @@
             term = lax.dot_general(x, w, NT, preferred_element_type=jnp.float32)
             total = term if total is None else total + term
         return total
+
+    def weight_copy(k, n):
+        part = pl.ds(pl.multiple_of(n * tile, tile), tile)
+        return pltpu.make_async_copy(given[k].at[part], (wg, wu, wd)[k].at[part], arrived.at[k, n])
+
+    if bring:
+        for k in range(3):
+            weight_copy(k, 0).start()
 
     slots = padded(experts)
     expert = lax.broadcasted_iota(jnp.int32, (slots, 128), 0)
@@ -63,7 +75,21 @@
     @pl.loop(0, units // tile)
     def _(n):
         first = pl.multiple_of(n * tile, tile)
-        gate, up, hid = product(0, wg, first), product(0, wu, first), product(1, wd, first)
+        if bring:
+            weight_copy(0, n).wait()
+
+            @pl.when(n + 1 < units // tile)
+            def _():
+                for k in range(3):
+                    weight_copy(k, n + 1).start()
+
+        gate = product(0, wg, first)
+        if bring:
+            weight_copy(1, n).wait()
+        up = product(0, wu, first)
+        if bring:
+            weight_copy(2, n).wait()
+        hid = product(1, wd, first)
         unit = first + lax.broadcasted_iota(jnp.int32, gate.shape, 1)
         share = jnp.zeros(gate.shape, jnp.float32)
         sig = jax.nn.sigmoid(gate)
@@ -112,24 +138,28 @@
                 (keep, send)[dc][out_at[dy, dx], :rows, pl.ds(start, wide)] = total[dy * rows : (dy + 1) * rows]
 
 
-def expert_call(where, pieces, weights, local, experts, rows, at, out_at, ndy, ndx):
+def expert_call(where, pieces, weights, local, experts, rows, at, out_at, ndy, ndx, bring):
     units, full = weights[0].shape
     width = pieces[0].shape[1]
     tile = next(t for t in (256, 128, 64, 32, 16) if units % t == 0)
     wide = next(t for t in (1024, 512, 256, 128) if width % t == 0)
     vmem = pl.BlockSpec(memory_space=pltpu.VMEM)
+    if bring:
+        weights = [pltpu.with_memory_space_constraint(w, pltpu.HBM) for w in weights]
     extra = padded(-(-experts // (width // rows)))
     out = jax.ShapeDtypeStruct((ndy * ndx, rows + extra, width), jnp.bfloat16)
     m = ndy * rows
     return pl.pallas_call(
         functools.partial(
-            expert_kernel, (at, out_at, len(pieces), ndy, ndx, local, experts, rows, tile, wide)
+            expert_kernel, (at, out_at, len(pieces), ndy, ndx, local, experts, rows, tile, wide, bring)
         ),
-        in_specs=[pl.BlockSpec(memory_space=pltpu.SMEM)] + [vmem] * (len(pieces) + 3),
-        out_specs=[vmem] * 2,
+        in_specs=[pl.BlockSpec(memory_space=pltpu.SMEM)] + [vmem] * len(pieces)
+        + [pl.BlockSpec(memory_space=pltpu.HBM) if bring else vmem] * 3,
+        out_specs=[vmem] * (5 if bring else 2),
         scratch_shapes=[pltpu.VMEM((m, units), jnp.bfloat16)] * 2
-        + [pltpu.VMEM((padded(local), m), jnp.float32)],
-        out_shape=[out] * 2,
+        + [pltpu.VMEM((padded(local), m), jnp.float32)]
+        + [pltpu.SemaphoreType.DMA((3, units // tile))] * bring,
+        out_shape=[out] * 2 + [jax.ShapeDtypeStruct(w.shape, w.dtype) for w in weights] * bring,
         compiler_params=pltpu.CompilerParams(vmem_limit_bytes=16 << 20),
         cost_estimate=pl.CostEstimate(
             flops=10 * m * units * full, bytes_accessed=6 * units * full, transcendentals=0
@@ -308,6 +338,8 @@
             if depth[dy, dx] == level
         ]
 
+    brought = []
+
     def compute(q):
         pieces, at = [], {}
         for l, cells in have[q].items():
@@ -317,7 +349,12 @@
             at[(1,) + l] = (first, rows) if len(cells) == 1 else (first + 1, 0)
             at[(2,) + l] = (first, 2 * rows)
         out_at = {(dy, dx): dy * cols + dx for dy, dx in labels}
-        return expert_call(where, pieces, weights, local, experts, rows, at, out_at, near, cols)
+        bring = not brought
+        results = expert_call(
+            where, pieces, brought or weights, local, experts, rows, at, out_at, near, cols, bring
+        )
+        brought.extend(results[2:])
+        return results[:2]
 
     class Sum:
         def __init__(self, q, keep, send):

time: 177 us -> 177 us (level)
  local copies, waits for them, and re-layouts: 9.62 us -> 1.28 us
  Pallas kernels: 43.6 us -> 49.6 us
  waiting for transfers between devices: 64 us -> 66.5 us
    unnamed x24 -> x14, local copies, waits for them, and re-layouts: 8.67 us -> 0.33 us
    pallas_call x4, Pallas kernels: 43.6 us -> 49.6 us  [expert_call(): pl.pallas_call(functools.partial(expert_kernel, (at, out_at, len(pieces),...]
    ppermute x58, waiting for transfers between devices: 60.9 us -> 63.4 us  [exchange(): lax.ppermute(x, axis, [(i, i ^ step) for i in range(lax.axis_size(axis))])]
  transfers between devices with their start and end apart: 62 -> 62, of which waited for: 24 -> 24; matrix products, arithmetic and copies ran while one was open for 3% -> 3% of each run, Pallas kernels for 25% -> 28%
where the time goes in v6:
time: 177 us
  waiting for transfers between devices  66.5 us (38%)
  starting transfers between devices  50.7 us (29%)
  Pallas kernels  49.6 us (28%)
  other arithmetic  7.51 us (4%)
    ppermute x58, waiting for transfers between devices, exchange(): lax.ppermute(x, axis, [(i, i ^ step) for i in range(lax.axis_size(axis))])  63.4 us
    pallas_call x4, Pallas kernels, expert_call(): pl.pallas_call(functools.partial(expert_kernel, (at, out_at, len(pieces),...  49.6 us
    ppermute x58, starting transfers between devices, exchange(): lax.ppermute(x, axis, [(i, i ^ step) for i in range(lax.axis_size(axis))])  40 us
    ppermute x4, starting transfers between devices, passed(): return lax.ppermute(x, axis, pairs)  10.6 us
  transfers between devices with their start and end apart: 62, of which 24 were waited for; matrix products, arithmetic and copies ran while one was open for 3% of the time, Pallas kernels for 28%

profile of v6, /device:TPU:8, one launch (start us, length us, event | category | flops | bytes accessed | tf_op | source)
XLA Modules:
  0.0 176.8 jit_solution(16047800991703136788)
XLA Ops:
  2.5 5.0 %collective-permute-start.1 = (bf16[272,1024]{1,0:T(8,128)(2,1)S(1)}, bf16[272,1024]{1,0:T(8,128)(2,1)}, u32[]{:S(2)}, u32[]{:S(2)}) collective-permute-start(bf16[272,1024]{1,0:T(8,128)(2,1)S(1)} %pad_maximum_fusion.refs_1_), channel_id=1, source_target_pairs={{8,16},{16,8},{9,17},{17,9},{10,18},{18,10},{11,19},{19,11},{12,20... | collective-permute-start | bytes 1671176 | tf_op jit(solution)/shard_map/ppermute | solution.py:207
  7.6 1.6 collective-permute-start.2
  9.1 1.5 collective-permute-start.3
  10.6 6.2 %collective-permute-done.refs_1_ = bf16[272,1024]{1,0:T(8,128)(2,1)S(1)} collective-permute-done((bf16[272,1024]{1,0:T(8,128)(2,1)S(1)}, bf16[272,1024]{1,0:T(8,128)(2,1)S(1)}, u32[]{:S(2)}, u32[]{:S(2)}) %collective-permute-start) | collective-permute-done | bytes 557088 | tf_op jit(solution)/shard_map/ppermute | solution.py:203
  16.9 3.1 %collective-permute-done.1 = bf16[272,1024]{1,0:T(8,128)(2,1)} collective-permute-done((bf16[272,1024]{1,0:T(8,128)(2,1)S(1)}, bf16[272,1024]{1,0:T(8,128)(2,1)}, u32[]{:S(2)}, u32[]{:S(2)}) %collective-permute-start.1) | collective-permute-done | bytes 557088 | tf_op jit(solution)/shard_map/ppermute | solution.py:207
  20.0 1.4 collective-permute-done.2.refs_2_
  22.7 2.2 %collective-permute-start.5 = (bf16[272,1024]{1,0:T(8,128)(2,1)S(1)}, bf16[272,1024]{1,0:T(8,128)(2,1)S(1)}, u32[]{:S(2)}, u32[]{:S(2)}) collective-permute-start(bf16[272,1024]{1,0:T(8,128)(2,1)S(1)} %collective-permute-done.refs_1_), channel_id=1, source_target_pairs={{8,16},{16,8},{9,17},{17,9},{10,18},{18,10},{11,19},{19,11},{12,20... | collective-permute-start | bytes 1671176 | tf_op jit(solution)/shard_map/ppermute | solution.py:207
  25.5 1.6 collective-permute-start.6
  27.6 2.1 %collective-permute-start.4 = (bf16[272,1024]{1,0:T(8,128)(2,1)}, bf16[272,1024]{1,0:T(8,128)(2,1)}, u32[]{:S(2)}, u32[]{:S(2)}) collective-permute-start(bf16[272,1024]{1,0:T(8,128)(2,1)} %collective-permute-done.1), channel_id=1, source_target_pairs={{8,0},{16,24},{9,1},{17,25},{10,2},{18,26},{11,3},{19,27},{12,4},{... | collective-permute-start | bytes 1671176 | tf_op jit(solution)/shard_map/ppermute | solution.py:207
  29.7 5.1 %collective-permute-done.6.refs_5_ = bf16[128,1024]{1,0:T(8,128)(2,1)S(1)} collective-permute-done((bf16[128,1024]{1,0:T(8,128)(2,1)S(1)}, bf16[128,1024]{1,0:T(8,128)(2,1)S(1)}, u32[]{:S(2)}, u32[]{:S(2)}) %collective-permute-start.6) | collective-permute-done | bytes 262176 | tf_op jit(solution)/shard_map/ppermute | solution.py:203
  34.8 1.5 collective-permute-start.7
  36.3 7.0 %collective-permute-done.7.refs_6_ = bf16[128,1024]{1,0:T(8,128)(2,1)S(1)} collective-permute-done((bf16[128,1024]{1,0:T(8,128)(2,1)S(1)}, bf16[128,1024]{1,0:T(8,128)(2,1)S(1)}, u32[]{:S(2)}, u32[]{:S(2)}) %collective-permute-start.7) | collective-permute-done | bytes 262176 | tf_op jit(solution)/shard_map/ppermute | solution.py:203
  47.7 1.5 collective-permute-start.13
  51.4 17.3 %shard_map.86 = (bf16[4,144,1024]{2,1,0:T(8,128)(2,1)S(1)}, bf16[4,144,1024]{2,1,0:T(8,128)(2,1)S(1)}, bf16[768,4096]{1,0:T(8,128)(2,1)S(1)}, bf16[768,4096]{1,0:T(8,128)(2,1)S(1)}, bf16[768,4096]{1,0:T(8,128)(2,1)S(1)}) custom-call(s32[5]{0:T(128)S(1)} %stack.23.refs_0_, bf16[272,1024]{1,0:T(8,128)(2,1)S(1)} %pad_maximum_fusion.refs_1_, ...), custom_call_target="tpu_custom_call" | custom-call | flops 8053063680 | bytes 18874368 | tf_op jit(solution)/shard_map/pallas_call | solution.py:152
  69.3 3.7 %collective-permute-done.11.refs_5_ = bf16[272,1024]{1,0:T(8,128)(2,1)S(1)} collective-permute-done((bf16[272,1024]{1,0:T(8,128)(2,1)S(1)}, bf16[272,1024]{1,0:T(8,128)(2,1)S(1)}, u32[]{:S(2)}, u32[]{:S(2)}) %collective-permute-start.11) | collective-permute-done | bytes 557088 | tf_op jit(solution)/shard_map/ppermute | solution.py:203
  75.5 1.5 collective-permute-start.23
  78.8 10.7 %shard_map.87 = (bf16[4,144,1024]{2,1,0:T(8,128)(2,1)S(1)}, bf16[4,144,1024]{2,1,0:T(8,128)(2,1)S(1)}) custom-call(s32[5]{0:T(128)S(1)} %stack.23.refs_0_, bf16[272,1024]{1,0:T(8,128)(2,1)S(1)} %collective-permute-done.refs_1_, bf16[272,1024]{1,0:T(8,128)(2,1)S(1)} %collective-permute-done.8.refs_2_, bf16[272,1024]{1,0:T(8,128)(2,1)S(1)} %collective-permute-done.9.refs_3_, ...), custom_call_target="tpu_custom_call" | custom-call | flops 8053063680 | bytes 18874368 | tf_op jit(solution)/shard_map/pallas_call | solution.py:152
  89.5 5.9 %collective-permute-done.20.refs_5_ = bf16[128,1024]{1,0:T(8,128)(2,1)S(1)} collective-permute-done((bf16[128,1024]{1,0:T(8,128)(2,1)S(1)}, bf16[128,1024]{1,0:T(8,128)(2,1)S(1)}, u32[]{:S(2)}, u32[]{:S(2)}) %collective-permute-start.20) | collective-permute-done | bytes 262176 | tf_op jit(solution)/shard_map/ppermute | solution.py:203
  96.6 1.7 collective-permute-done.28
  99.1 1.5 collective-permute-start.29
  103.5 10.8 %shard_map.88 = (bf16[4,144,1024]{2,1,0:T(8,128)(2,1)S(1)}, bf16[4,144,1024]{2,1,0:T(8,128)(2,1)S(1)}) custom-call(s32[5]{0:T(128)S(1)} %stack.23.refs_0_, bf16[272,1024]{1,0:T(8,128)(2,1)S(1)} %broadcast_select_fusion.1.refs_1_, bf16[272,1024]{1,0:T(8,128)(2,1)S(1)} %collective-permute-done.12.refs_2_, ...), custom_call_target="tpu_custom_call" | custom-call | flops 8053063680 | bytes 18874368 | tf_op jit(solution)/shard_map/pallas_call | solution.py:152
  116.3 1.7 collective-permute-done.40
  122.9 10.8 %shard_map.89 = (bf16[4,144,1024]{2,1,0:T(8,128)(2,1)S(1)}, bf16[4,144,1024]{2,1,0:T(8,128)(2,1)S(1)}) custom-call(s32[5]{0:T(128)S(1)} %stack.23.refs_0_, bf16[272,1024]{1,0:T(8,128)(2,1)S(1)} %broadcast_select_fusion.refs_1_, bf16[272,1024]{1,0:T(8,128)(2,1)S(1)} %collective-permute-done.22.refs_2_, bf16[272,1024]{1,0:T(8,128)(2,1)S(1)} %collective-permute-done.23.refs_3_, ...), custom_call_target="tpu_custom_call" | custom-call | flops 8053063680 | bytes 18874368 | tf_op jit(solution)/shard_map/pallas_call | solution.py:152
  133.8 1.4 collective-permute-start.51
  138.6 1.9 %collective-permute-done.51 = bf16[1,1,72,1024]{3,2,1,0:T(8,128)(2,1)S(1)} collective-permute-done((bf16[1,1,72,1024]{3,2,1,0:T(8,128)(2,1)S(1)}, bf16[1,1,72,1024]{3,2,1,0:T(8,128)(2,1)S(1)}, u32[]{:S(2)}, u32[]{:S(2)}) %collective-permute-start.51) | collective-permute-done | bytes 147488 | tf_op jit(solution)/shard_map/ppermute | solution.py:203
  143.6 3.2 %collective-permute-done.50 = bf16[2,1,72,1024]{3,2,1,0:T(8,128)(2,1)S(1)} collective-permute-done((bf16[2,1,72,1024]{3,2,1,0:T(8,128)(2,1)S(1)}, bf16[2,1,72,1024]{3,2,1,0:T(8,128)(2,1)S(1)}, u32[]{:S(2)}, u32[]{:S(2)}) %collective-permute-start.50) | collective-permute-done | bytes 294944 | tf_op jit(solution)/shard_map/ppermute | solution.py:203
  146.8 1.4 collective-permute-done.49
  148.3 4.5 %collective-permute-done.55 = bf16[2,1,72,1024]{3,2,1,0:T(8,128)(2,1)S(1)} collective-permute-done((bf16[2,1,72,1024]{3,2,1,0:T(8,128)(2,1)S(1)}, bf16[2,1,72,1024]{3,2,1,0:T(8,128)(2,1)S(1)}, u32[]{:S(2)}, u32[]{:S(2)}) %collective-permute-start.55) | collective-permute-done | bytes 294944 | tf_op jit(solution)/shard_map/ppermute | solution.py:203
  156.1 3.1 %collective-permute-done.57 = bf16[1,1,72,1024]{3,2,1,0:T(8,128)(2,1)S(1)} collective-permute-done((bf16[1,1,72,1024]{3,2,1,0:T(8,128)(2,1)S(1)}, bf16[1,1,72,1024]{3,2,1,0:T(8,128)(2,1)S(1)}, u32[]{:S(2)}, u32[]{:S(2)}) %collective-permute-start.57) | collective-permute-done | bytes 147488 | tf_op jit(solution)/shard_map/ppermute | solution.py:203
  162.4 1.4 collective-permute-start.59
  163.8 1.6 collective-permute-done.61
  166.8 8.4 %collective-permute-done.59 = bf16[144,1024]{1,0:T(8,128)(2,1)S(1)} collective-permute-done((bf16[144,1024]{1,0:T(8,128)(2,1)S(1)}, bf16[144,1024]{1,0:T(8,128)(2,1)S(1)}, u32[]{:S(2)}, u32[]{:S(2)}) %collective-permute-start.59) | collective-permute-done | bytes 294944 | tf_op jit(solution)/shard_map/ppermute | solution.py:203
  (152 shorter events, 43.2 us)
Async XLA Ops:
  2.4 14.4 %collective-permute-start = (bf16[272,1024]{1,0:T(8,128)(2,1)S(1)}, bf16[272,1024]{1,0:T(8,128)(2,1)S(1)}, u32[]{:S(2)}, u32[]{:S(2)}) collective-permute-start(bf16[272,1024]{1,0:T(8,128)(2,1)S(1)} %pad_maximum_fusion.refs_1_), channel_id=1, source_target_pairs={{0,8},{8,0},{16,24},{24,16},{1,9},{9,1},{17,25},{25,17},{2,10},{10... | collective-permute-start | bytes 1671176 | tf_op jit(solution)/shard_map/ppermute | solution.py:203
  2.5 17.5 %collective-permute-start.1 = (bf16[272,1024]{1,0:T(8,128)(2,1)S(1)}, bf16[272,1024]{1,0:T(8,128)(2,1)}, u32[]{:S(2)}, u32[]{:S(2)}) collective-permute-start(bf16[272,1024]{1,0:T(8,128)(2,1)S(1)} %pad_maximum_fusion.refs_1_), channel_id=1, source_target_pairs={{8,16},{16,8},{9,17},{17,9},{10,18},{18,10},{11,19},{19,11},{12,20... | collective-permute-start | bytes 1671176 | tf_op jit(solution)/shard_map/ppermute | solution.py:207
  7.6 13.9 %collective-permute-start.2 = (bf16[272,1024]{1,0:T(8,128)(2,1)S(1)}, bf16[272,1024]{1,0:T(8,128)(2,1)S(1)}, u32[]{:S(2)}, u32[]{:S(2)}) collective-permute-start(bf16[272,1024]{1,0:T(8,128)(2,1)S(1)} %pad_maximum_fusion.refs_1_), channel_id=1, source_target_pairs={{0,2},{2,0},{1,3},{3,1},{4,6},{6,4},{5,7},{7,5},{8,10},{10,8},{9,1... | collective-permute-start | bytes 1671176 | tf_op jit(solution)/shard_map/ppermute | solution.py:203
  9.1 13.5 %collective-permute-start.3 = (bf16[272,1024]{1,0:T(8,128)(2,1)S(1)}, bf16[272,1024]{1,0:T(8,128)(2,1)S(1)}, u32[]{:S(2)}, u32[]{:S(2)}) collective-permute-start(bf16[272,1024]{1,0:T(8,128)(2,1)S(1)} %pad_maximum_fusion.refs_1_), channel_id=1, source_target_pairs={{0,4},{4,0},{1,5},{5,1},{2,6},{6,2},{3,7},{7,3},{8,12},{12,8},{9,1... | collective-permute-start | bytes 1671176 | tf_op jit(solution)/shard_map/ppermute | solution.py:203
  22.7 20.6 %collective-permute-start.5 = (bf16[272,1024]{1,0:T(8,128)(2,1)S(1)}, bf16[272,1024]{1,0:T(8,128)(2,1)S(1)}, u32[]{:S(2)}, u32[]{:S(2)}) collective-permute-start(bf16[272,1024]{1,0:T(8,128)(2,1)S(1)} %collective-permute-done.refs_1_), channel_id=1, source_target_pairs={{8,16},{16,8},{9,17},{17,9},{10,18},{18,10},{11,19},{19,11},{12,20... | collective-permute-start | bytes 1671176 | tf_op jit(solution)/shard_map/ppermute | solution.py:207
  24.9 18.9 %collective-permute-start.8 = (bf16[272,1024]{1,0:T(8,128)(2,1)S(1)}, bf16[272,1024]{1,0:T(8,128)(2,1)S(1)}, u32[]{:S(2)}, u32[]{:S(2)}) collective-permute-start(bf16[272,1024]{1,0:T(8,128)(2,1)S(1)} %collective-permute-done.refs_1_), channel_id=1, source_target_pairs={{0,2},{2,0},{1,3},{3,1},{4,6},{6,4},{5,7},{7,5},{8,10},{10,8},{9,1... | collective-permute-start | bytes 1671176 | tf_op jit(solution)/shard_map/ppermute | solution.py:203
  27.1 17.2 %collective-permute-start.9 = (bf16[272,1024]{1,0:T(8,128)(2,1)S(1)}, bf16[272,1024]{1,0:T(8,128)(2,1)S(1)}, u32[]{:S(2)}, u32[]{:S(2)}) collective-permute-start(bf16[272,1024]{1,0:T(8,128)(2,1)S(1)} %collective-permute-done.refs_1_), channel_id=1, source_target_pairs={{0,4},{4,0},{1,5},{5,1},{2,6},{6,2},{3,7},{7,3},{8,12},{12,8},{9,1... | collective-permute-start | bytes 1671176 | tf_op jit(solution)/shard_map/ppermute | solution.py:203
  27.6 16.7 %collective-permute-start.4 = (bf16[272,1024]{1,0:T(8,128)(2,1)}, bf16[272,1024]{1,0:T(8,128)(2,1)}, u32[]{:S(2)}, u32[]{:S(2)}) collective-permute-start(bf16[272,1024]{1,0:T(8,128)(2,1)} %collective-permute-done.1), channel_id=1, source_target_pairs={{8,0},{16,24},{9,1},{17,25},{10,2},{18,26},{11,3},{19,27},{12,4},{... | collective-permute-start | bytes 1671176 | tf_op jit(solution)/shard_map/ppermute | solution.py:207
  46.0 28.7 %collective-permute-start.24 = (bf16[272,1024]{1,0:T(8,128)(2,1)S(1)}, bf16[272,1024]{1,0:T(8,128)(2,1)S(1)}, u32[]{:S(2)}, u32[]{:S(2)}) collective-permute-start(bf16[272,1024]{1,0:T(8,128)(2,1)S(1)} %collective-permute-done.refs_1_), channel_id=1, source_target_pairs={{0,1},{1,0},{2,3},{3,2},{4,5},{5,4},{6,7},{7,6},{8,9},{9,8},{10,11... | collective-permute-start | bytes 1671176 | tf_op jit(solution)/shard_map/ppermute | solution.py:203
  46.4 22.3 %collective-permute-start.12 = (bf16[272,1024]{1,0:T(8,128)(2,1)S(1)}, bf16[272,1024]{1,0:T(8,128)(2,1)S(1)}, u32[]{:S(2)}, u32[]{:S(2)}) collective-permute-start(bf16[272,1024]{1,0:T(8,128)(2,1)S(1)} %broadcast_select_fusion.1.refs_1_), channel_id=1, source_target_pairs={{0,2},{2,0},{1,3},{3,1},{4,6},{6,4},{5,7},{7,5},{8,10},{10,8},{9,1... | collective-permute-start | bytes 1671176 | tf_op jit(solution)/shard_map/ppermute | solution.py:203
  47.7 21.1 %collective-permute-start.13 = (bf16[272,1024]{1,0:T(8,128)(2,1)S(1)}, bf16[272,1024]{1,0:T(8,128)(2,1)S(1)}, u32[]{:S(2)}, u32[]{:S(2)}) collective-permute-start(bf16[272,1024]{1,0:T(8,128)(2,1)S(1)} %broadcast_select_fusion.1.refs_1_), channel_id=1, source_target_pairs={{0,4},{4,0},{1,5},{5,1},{2,6},{6,2},{3,7},{7,3},{8,12},{12,8},{9,1... | collective-permute-start | bytes 1671176 | tf_op jit(solution)/shard_map/ppermute | solution.py:203
  49.2 23.8 %collective-permute-start.10 = (bf16[272,1024]{1,0:T(8,128)(2,1)S(1)}, bf16[272,1024]{1,0:T(8,128)(2,1)S(1)}, u32[]{:S(2)}, u32[]{:S(2)}) collective-permute-start(bf16[272,1024]{1,0:T(8,128)(2,1)S(1)} %copy-done.5), channel_id=1, source_target_pairs={{8,0},{16,24},{9,1},{17,25},{10,2},{18,26},{11,3},{19,27},{12,4},{... | collective-permute-start | bytes 1671176 | tf_op jit(solution)/shard_map/ppermute | solution.py:207
  50.6 22.4 %collective-permute-start.11 = (bf16[272,1024]{1,0:T(8,128)(2,1)S(1)}, bf16[272,1024]{1,0:T(8,128)(2,1)S(1)}, u32[]{:S(2)}, u32[]{:S(2)}) collective-permute-start(bf16[272,1024]{1,0:T(8,128)(2,1)S(1)} %collective-permute-done.9.refs_3_), channel_id=1, source_target_pairs={{0,2},{2,0},{1,3},{3,1},{4,6},{6,4},{5,7},{7,5},{8,10},{10,8},{9,1... | collective-permute-start | bytes 1671176 | tf_op jit(solution)/shard_map/ppermute | solution.py:203
  73.0 22.4 %collective-permute-start.19 = (bf16[4,144,1024]{2,1,0:T(8,128)(2,1)S(1)}, bf16[4,144,1024]{2,1,0:T(8,128)(2,1)S(1)}, u32[]{:S(2)}, u32[]{:S(2)}) collective-permute-start(bf16[4,144,1024]{2,1,0:T(8,128)(2,1)S(1)} %get-tuple-element.78), channel_id=1, source_target_pairs={{0,1},{1,0},{2,3},{3,2},{4,5},{5,4},{6,7},{7,6},{8,9},{9,8},{10,11... | collective-permute-start | bytes 3538952 | tf_op jit(solution)/shard_map/ppermute | solution.py:203
  74.7 20.7 %collective-permute-start.22 = (bf16[272,1024]{1,0:T(8,128)(2,1)S(1)}, bf16[272,1024]{1,0:T(8,128)(2,1)S(1)}, u32[]{:S(2)}, u32[]{:S(2)}) collective-permute-start(bf16[272,1024]{1,0:T(8,128)(2,1)S(1)} %broadcast_select_fusion.refs_1_), channel_id=1, source_target_pairs={{0,2},{2,0},{1,3},{3,1},{4,6},{6,4},{5,7},{7,5},{8,10},{10,8},{9,1... | collective-permute-start | bytes 1671176 | tf_op jit(solution)/shard_map/ppermute | solution.py:203
  75.5 19.9 %collective-permute-start.23 = (bf16[272,1024]{1,0:T(8,128)(2,1)S(1)}, bf16[272,1024]{1,0:T(8,128)(2,1)S(1)}, u32[]{:S(2)}, u32[]{:S(2)}) collective-permute-start(bf16[272,1024]{1,0:T(8,128)(2,1)S(1)} %broadcast_select_fusion.refs_1_), channel_id=1, source_target_pairs={{0,4},{4,0},{1,5},{5,1},{2,6},{6,2},{3,7},{7,3},{8,12},{12,8},{9,1... | collective-permute-start | bytes 1671176 | tf_op jit(solution)/shard_map/ppermute | solution.py:203
  77.1 18.3 %collective-permute-start.20 = (bf16[128,1024]{1,0:T(8,128)(2,1)S(1)}, bf16[128,1024]{1,0:T(8,128)(2,1)S(1)}, u32[]{:S(2)}, u32[]{:S(2)}) collective-permute-start(bf16[128,1024]{1,0:T(8,128)(2,1)S(1)} %slice.80), channel_id=1, source_target_pairs={{0,4},{4,0},{1,5},{5,1},{2,6},{6,2},{3,7},{7,3},{8,12},{12,8},{9,1... | collective-permute-start | bytes 786440 | tf_op jit(solution)/shard_map/ppermute | solution.py:203
  77.6 17.8 %collective-permute-start.21 = (bf16[128,1024]{1,0:T(8,128)(2,1)S(1)}, bf16[128,1024]{1,0:T(8,128)(2,1)S(1)}, u32[]{:S(2)}, u32[]{:S(2)}) collective-permute-start(bf16[128,1024]{1,0:T(8,128)(2,1)S(1)} %slice.81), channel_id=1, source_target_pairs={{0,2},{2,0},{1,3},{3,1},{4,6},{6,4},{5,7},{7,5},{8,10},{10,8},{9,1... | collective-permute-start | bytes 786440 | tf_op jit(solution)/shard_map/ppermute | solution.py:203
  99.1 15.2 %collective-permute-start.29 = (bf16[128,1024]{1,0:T(8,128)(2,1)S(1)}, bf16[128,1024]{1,0:T(8,128)(2,1)S(1)}, u32[]{:S(2)}, u32[]{:S(2)}) collective-permute-start(bf16[128,1024]{1,0:T(8,128)(2,1)S(1)} %slice.82), channel_id=1, source_target_pairs={{0,4},{4,0},{1,5},{5,1},{2,6},{6,2},{3,7},{7,3},{8,12},{12,8},{9,1... | collective-permute-start | bytes 786440 | tf_op jit(solution)/shard_map/ppermute | solution.py:203
  100.7 13.7 %collective-permute-start.30 = (bf16[128,1024]{1,0:T(8,128)(2,1)S(1)}, bf16[128,1024]{1,0:T(8,128)(2,1)S(1)}, u32[]{:S(2)}, u32[]{:S(2)}) collective-permute-start(bf16[128,1024]{1,0:T(8,128)(2,1)S(1)} %slice.83), channel_id=1, source_target_pairs={{0,2},{2,0},{1,3},{3,1},{4,6},{6,4},{5,7},{7,5},{8,10},{10,8},{9,1... | collective-permute-start | bytes 786440 | tf_op jit(solution)/shard_map/ppermute | solution.py:203
  101.9 12.5 %collective-permute-start.31 = (bf16[1,2,72,1024]{3,2,1,0:T(8,128)(2,1)S(1)}, bf16[1,2,72,1024]{3,2,1,0:T(8,128)(2,1)S(1)}, u32[]{:S(2)}, u32[]{:S(2)}) collective-permute-start(bf16[1,2,72,1024]{3,2,1,0:T(8,128)(2,1)S(1)} %get-tuple-element.94), channel_id=1, source_target_pairs={{0,4},{4,0},{1,5},{5,1},{2,6},{6,2},{3,7},{7,3},{8,12},{12,8},{9,1... | collective-permute-start | bytes 884744 | tf_op jit(solution)/shard_map/ppermute | solution.py:203
  102.7 12.4 %collective-permute-start.32 = (bf16[2,1,72,1024]{3,2,1,0:T(8,128)(2,1)S(1)}, bf16[2,1,72,1024]{3,2,1,0:T(8,128)(2,1)S(1)}, u32[]{:S(2)}, u32[]{:S(2)}) collective-permute-start(bf16[2,1,72,1024]{3,2,1,0:T(8,128)(2,1)S(1)} %get-tuple-element.95), channel_id=1, source_target_pairs={{0,2},{2,0},{1,3},{3,1},{4,6},{6,4},{5,7},{7,5},{8,10},{10,8},{9,1... | collective-permute-start | bytes 884744 | tf_op jit(solution)/shard_map/ppermute | solution.py:203
  118.8 14.8 %collective-permute-start.39 = (bf16[1,1,72,1024]{3,2,1,0:T(8,128)(2,1)S(1)}, bf16[1,1,72,1024]{3,2,1,0:T(8,128)(2,1)S(1)}, u32[]{:S(2)}, u32[]{:S(2)}) collective-permute-start(bf16[1,1,72,1024]{3,2,1,0:T(8,128)(2,1)S(1)} %add_convert_fusion.37), channel_id=1, source_target_pairs={{0,4},{4,0},{1,5},{5,1},{2,6},{6,2},{3,7},{7,3},{8,12},{12,8},{9,1... | collective-permute-start | bytes 442376 | tf_op jit(solution)/shard_map/ppermute | solution.py:203
  119.8 13.9 %collective-permute-start.38 = (bf16[1,1,72,1024]{3,2,1,0:T(8,128)(2,1)S(1)}, bf16[1,1,72,1024]{3,2,1,0:T(8,128)(2,1)S(1)}, u32[]{:S(2)}, u32[]{:S(2)}) collective-permute-start(bf16[1,1,72,1024]{3,2,1,0:T(8,128)(2,1)S(1)} %add_convert_fusion.38), channel_id=1, source_target_pairs={{0,2},{2,0},{1,3},{3,1},{4,6},{6,4},{5,7},{7,5},{8,10},{10,8},{9,1... | collective-permute-start | bytes 442376 | tf_op jit(solution)/shard_map/ppermute | solution.py:203
  121.1 12.6 %collective-permute-start.41 = (bf16[1,2,72,1024]{3,2,1,0:T(8,128)(2,1)S(1)}, bf16[1,2,72,1024]{3,2,1,0:T(8,128)(2,1)S(1)}, u32[]{:S(2)}, u32[]{:S(2)}) collective-permute-start(bf16[1,2,72,1024]{3,2,1,0:T(8,128)(2,1)S(1)} %get-tuple-element.106), channel_id=1, source_target_pairs={{0,4},{4,0},{1,5},{5,1},{2,6},{6,2},{3,7},{7,3},{8,12},{12,8},{9,1... | collective-permute-start | bytes 884744 | tf_op jit(solution)/shard_map/ppermute | solution.py:203
  122.1 11.5 %collective-permute-start.42 = (bf16[2,1,72,1024]{3,2,1,0:T(8,128)(2,1)S(1)}, bf16[2,1,72,1024]{3,2,1,0:T(8,128)(2,1)S(1)}, u32[]{:S(2)}, u32[]{:S(2)}) collective-permute-start(bf16[2,1,72,1024]{3,2,1,0:T(8,128)(2,1)S(1)} %get-tuple-element.107), channel_id=1, source_target_pairs={{0,2},{2,0},{1,3},{3,1},{4,6},{6,4},{5,7},{7,5},{8,10},{10,8},{9,1... | collective-permute-start | bytes 884744 | tf_op jit(solution)/shard_map/ppermute | solution.py:203
  137.5 10.8 %collective-permute-start.49 = (bf16[1,2,72,1024]{3,2,1,0:T(8,128)(2,1)S(1)}, bf16[1,2,72,1024]{3,2,1,0:T(8,128)(2,1)S(1)}, u32[]{:S(2)}, u32[]{:S(2)}) collective-permute-start(bf16[1,2,72,1024]{3,2,1,0:T(8,128)(2,1)S(1)} %get-tuple-element.135), channel_id=1, source_target_pairs={{0,4},{4,0},{1,5},{5,1},{2,6},{6,2},{3,7},{7,3},{8,12},{12,8},{9,1... | collective-permute-start | bytes 884744 | tf_op jit(solution)/shard_map/ppermute | solution.py:203
  140.8 11.9 %collective-permute-start.55 = (bf16[2,1,72,1024]{3,2,1,0:T(8,128)(2,1)S(1)}, bf16[2,1,72,1024]{3,2,1,0:T(8,128)(2,1)S(1)}, u32[]{:S(2)}, u32[]{:S(2)}) collective-permute-start(bf16[2,1,72,1024]{3,2,1,0:T(8,128)(2,1)S(1)} %get-tuple-element.137), channel_id=1, source_target_pairs={{0,2},{2,0},{1,3},{3,1},{4,6},{6,4},{5,7},{7,5},{8,10},{10,8},{9,1... | collective-permute-start | bytes 884744 | tf_op jit(solution)/shard_map/ppermute | solution.py:203
  142.4 11.5 %collective-permute-start.54 = (bf16[1,2,72,1024]{3,2,1,0:T(8,128)(2,1)S(1)}, bf16[1,2,72,1024]{3,2,1,0:T(8,128)(2,1)S(1)}, u32[]{:S(2)}, u32[]{:S(2)}) collective-permute-start(bf16[1,2,72,1024]{3,2,1,0:T(8,128)(2,1)S(1)} %get-tuple-element.139), channel_id=1, source_target_pairs={{0,4},{4,0},{1,5},{5,1},{2,6},{6,2},{3,7},{7,3},{8,12},{12,8},{9,1... | collective-permute-start | bytes 884744 | tf_op jit(solution)/shard_map/ppermute | solution.py:203
  143.5 12.5 %collective-permute-start.58 = (bf16[144,1024]{1,0:T(8,128)(2,1)S(1)}, bf16[144,1024]{1,0:T(8,128)(2,1)S(1)}, u32[]{:S(2)}, u32[]{:S(2)}) collective-permute-start(bf16[144,1024]{1,0:T(8,128)(2,1)S(1)} %pad_maximum_fusion.2), channel_id=1, source_target_pairs={{0,16},{8,24},{16,0},{24,8},{1,17},{9,25},{17,1},{25,9},{2,18},{10... | collective-permute-start | bytes 884744 | tf_op jit(solution)/shard_map/ppermute | solution.py:203
  156.0 10.8 %collective-permute-start.48 = (bf16[144,1024]{1,0:T(8,128)(2,1)S(1)}, bf16[144,1024]{1,0:T(8,128)(2,1)S(1)}, u32[]{:S(2)}, u32[]{:S(2)}) collective-permute-start(bf16[144,1024]{1,0:T(8,128)(2,1)S(1)} %pad_maximum_fusion.1), channel_id=1, source_target_pairs={{0,8},{8,0},{16,24},{24,16},{1,9},{9,1},{17,25},{25,17},{2,10},{10... | collective-permute-start | bytes 884744 | tf_op jit(solution)/shard_map/ppermute | solution.py:203
  162.4 12.8 %collective-permute-start.59 = (bf16[144,1024]{1,0:T(8,128)(2,1)S(1)}, bf16[144,1024]{1,0:T(8,128)(2,1)S(1)}, u32[]{:S(2)}, u32[]{:S(2)}) collective-permute-start(bf16[144,1024]{1,0:T(8,128)(2,1)S(1)} %pad_maximum_fusion.3), channel_id=1, source_target_pairs={{0,24},{8,16},{16,8},{24,0},{1,25},{9,17},{17,9},{25,1},{2,26},{10... | collective-permute-start | bytes 884744 | tf_op jit(solution)/shard_map/ppermute | solution.py:203
  (37 other events, 205.6 us)
